TPU v7x, 32 devices: a whole 2x2x4 slice. The times are simulated.
32 devices in a mesh: dp: 4 (over y, x), ctx: 2 (over core), wt: 4 (over z).
Axes of the slice: x: 2, y: 2, z: 4, core: 2. Of those that a mesh axis runs over, the one named last changes fastest.
Arguments:
- tokens: bfloat16 [16, 2048, 1600], P(('dp', 'wt'), 'ctx'), may hold values from -6 to 6
- cotangent: bfloat16 [16, 2048, 1600], P(('dp', 'wt'), 'ctx'), may hold values from -6 to 6
- doc_lengths: int32 [16, 4], P(('dp', 'wt')), may hold values from 1 to 2045, as said below
- adapter_ids: int32 [16, 1], P(('dp', 'wt')), may hold values from 0 to 7
- first_gain: bfloat16 [1600], P('wt'), may hold values from 0.5 to 1.5
- first_shift: bfloat16 [1600], P('wt'), may hold values from -1 to 1
- qkv_weight: bfloat16 [1600, 4800], P('wt'), may hold values from -0.21875 to 0.21875
- qkv_bias: bfloat16 [4800], P('wt'), may hold values from -1 to 1
- out_weight: bfloat16 [1600, 1600], P('wt'), may hold values from -0.875 to 0.875
- out_bias: bfloat16 [1600], P('wt'), may hold values from -1 to 1
- second_gain: bfloat16 [1600], P('wt'), may hold values from 0.5 to 1.5
- second_shift: bfloat16 [1600], P('wt'), may hold values from -1 to 1
- up_weight: bfloat16 [1600, 6400], P('wt'), may hold values from -0.15625 to 0.15625
- up_bias: bfloat16 [6400], P('wt'), may hold values from -1 to 1
- down_weight: bfloat16 [6400, 1600], P('wt'), may hold values from -0.078125 to 0.078125
- down_bias: bfloat16 [1600], P('wt'), may hold values from -1 to 1
- qkv_adapt_in: bfloat16 [8, 16, 1600], replicated, may hold values from -0.15625 to 0.15625
- qkv_adapt_out: bfloat16 [8, 16, 4800], replicated, may hold values from -0.75 to 0.75
- out_adapt_in: bfloat16 [8, 16, 1600], replicated, may hold values from -0.875 to 0.875
- out_adapt_out: bfloat16 [8, 16, 1600], replicated, may hold values from -0.75 to 0.75
- up_adapt_in: bfloat16 [8, 16, 1600], replicated, may hold values from -0.15625 to 0.15625
- up_adapt_out: bfloat16 [8, 16, 6400], replicated, may hold values from -0.75 to 0.75
- down_adapt_in: bfloat16 [8, 16, 6400], replicated, may hold values from -0.078125 to 0.078125
- down_adapt_out: bfloat16 [8, 16, 1600], replicated, may hold values from -0.75 to 0.75
Outputs:
- output: bfloat16 [16, 2048, 1600], P(('dp', 'wt'), 'ctx')
- grad_tokens: float32 [16, 2048, 1600], P(('dp', 'wt'), 'ctx')
- grad_qkv_in: float32 [8, 16, 1600], replicated
- grad_qkv_out: float32 [8, 16, 4800], replicated
- grad_out_in: float32 [8, 16, 1600], replicated
- grad_out_out: float32 [8, 16, 1600], replicated
- grad_up_in: float32 [8, 16, 1600], replicated
- grad_up_out: float32 [8, 16, 6400], replicated
- grad_down_in: float32 [8, 16, 6400], replicated
- grad_down_out: float32 [8, 16, 1600], replicated
Inputs may be any that keep to these rules, and one draw needn't show every extreme that they name: `doc_lengths`: each row sums to 2048. `adapter_ids`: every adapter is the adapter of some sequence.
All inputs are finite; a program needn't handle non-finite values.
Results may differ from a plain program's by a relative error of at most 0.015.
The roundings to bfloat16 on the way count: a program that leaves them out, or rounds other values in their place, can miss the bound.
Values may be sent and summed in bfloat16 or wider, within the bound.
No kernel may reach another device: no remote copies, remote signals or barrier semaphores. Data moves between devices by JAX's collectives and lax.ppermute only.
A program may use at most 320 MiB of HBM per device.

v0:
```python
from functools import partial

import jax
import jax.numpy as jnp
from jax import lax
from jax.sharding import PartitionSpec as P

HEADS = 25
HEAD_DIM = 64
ADAPTERS = 8
WINDOW = 1024


EPSILON = 1e-05
MASKED = -1e30


def shifted(array, axis, by):
    devices = lax.axis_size(axis)
    pairs = [(i, i + by) for i in range(devices) if 0 <= i + by < devices]
    return lax.ppermute(array, axis, pairs)


def product(left_side, right_side):
    return jnp.dot(left_side, right_side, preferred_element_type=jnp.float32)


def product_transposed(left_side, right_side):
    return lax.dot_general(
        left_side, right_side, (((1,), (1,)), ((), ())), preferred_element_type=jnp.float32
    )


def product_outer(left_side, right_side):
    return lax.dot_general(
        left_side, right_side, (((0,), (0,)), ((), ())), preferred_element_type=jnp.float32
    )


def norm_forward(values, norm_gain, norm_shift):
    center = values - jnp.mean(values, axis=-1, keepdims=True)
    inverse = lax.rsqrt(jnp.mean(center * center, axis=-1, keepdims=True) + EPSILON)
    normed = center * inverse
    return (normed * norm_gain + norm_shift, normed, inverse)


def norm_backward(upstream, normed, inverse, norm_gain):
    scaled = upstream * norm_gain
    return inverse * (
        scaled
        - jnp.mean(scaled, axis=-1, keepdims=True)
        - normed * jnp.mean(scaled * normed, axis=-1, keepdims=True)
    )


def document_index(positions, lengths):
    bounds = jnp.cumsum(lengths)[:-1]
    return jnp.sum((positions[:, None] >= bounds[None, :]).astype(jnp.int32), axis=1)


def block_mask(query_pos, key_pos, lengths):
    query_doc = document_index(query_pos, lengths)
    key_doc = document_index(key_pos, lengths)
    distance = query_pos[:, None] - key_pos[None, :]
    same_doc = query_doc[:, None] == key_doc[None, :]
    return (key_pos[None, :] >= 0) & same_doc & (distance >= 0) & (distance < WINDOW)


def head_grouping():
    per_group = max((divisor for divisor in range(1, 9) if HEADS % divisor == 0))
    return (per_group, HEADS // per_group)


def attend_forward(queries, key_buffer, value_buffer, first_query, lengths):
    row_count, feature_count = queries.shape
    block_rows = min(512, row_count)
    key_rows = WINDOW + block_rows
    offset_rows = key_buffer.shape[0] - row_count
    per_group, groups = head_grouping()
    span = per_group * HEAD_DIM
    factor = HEAD_DIM ** (-0.5)

    def one_block(block_index, carry):
        row_start = block_index * block_rows
        query_pos = first_query + row_start + jnp.arange(block_rows, dtype=jnp.int32)
        key_pos = first_query + row_start - WINDOW + jnp.arange(key_rows, dtype=jnp.int32)
        allowed = block_mask(query_pos, key_pos, lengths)[None]
        key_start = offset_rows + row_start - WINDOW

        def one_group(group_index, inner):
            attended, logsums = inner
            column = group_index * span
            query_part = lax.dynamic_slice(
                queries, (row_start, column), (block_rows, span)
            ).reshape(block_rows, per_group, HEAD_DIM)
            key_part = lax.dynamic_slice(key_buffer, (key_start, column), (key_rows, span)).reshape(
                key_rows, per_group, HEAD_DIM
            )
            value_part = lax.dynamic_slice(
                value_buffer, (key_start, column), (key_rows, span)
            ).reshape(key_rows, per_group, HEAD_DIM)
            products = jnp.einsum(
                "qhd,khd->hqk", query_part, key_part, preferred_element_type=jnp.float32
            )
            scores = jnp.where(allowed, products * factor, MASKED)
            highest = jnp.max(scores, axis=-1, keepdims=True)
            exponent = jnp.exp(scores - highest)
            summed = jnp.sum(exponent, axis=-1, keepdims=True)
            chances = (exponent / summed).astype(jnp.bfloat16)
            combined = jnp.einsum(
                "hqk,khd->qhd", chances, value_part, preferred_element_type=jnp.float32
            )
            attended = lax.dynamic_update_slice(
                attended, combined.reshape(block_rows, span), (row_start, column)
            )
            logsums = lax.dynamic_update_slice(
                logsums, (highest + jnp.log(summed))[:, :, 0], (group_index * per_group, row_start)
            )
            return (attended, logsums)

        return lax.fori_loop(0, groups, one_group, carry)

    start_state = (
        jnp.zeros((row_count, feature_count), jnp.float32),
        jnp.zeros((HEADS, row_count), jnp.float32),
    )
    return lax.fori_loop(0, row_count // block_rows, one_block, start_state)


def attend_backward(queries, key_buffer, value_buffer, grad_mixed, logsums, first_query, lengths):
    row_count, feature_count = queries.shape
    block_rows = min(512, row_count)
    key_rows = WINDOW + block_rows
    offset_rows = key_buffer.shape[0] - row_count
    per_group, groups = head_grouping()
    span = per_group * HEAD_DIM
    factor = HEAD_DIM ** (-0.5)

    def one_block(block_index, carry):
        row_start = block_index * block_rows
        query_pos = first_query + row_start + jnp.arange(block_rows, dtype=jnp.int32)
        key_pos = first_query + row_start - WINDOW + jnp.arange(key_rows, dtype=jnp.int32)
        allowed = block_mask(query_pos, key_pos, lengths)[None]
        key_start = offset_rows + row_start - WINDOW

        def one_group(group_index, inner):
            grad_queries, grad_keys, grad_values = inner
            column = group_index * span
            query_part = lax.dynamic_slice(
                queries, (row_start, column), (block_rows, span)
            ).reshape(block_rows, per_group, HEAD_DIM)
            key_part = lax.dynamic_slice(key_buffer, (key_start, column), (key_rows, span)).reshape(
                key_rows, per_group, HEAD_DIM
            )
            value_part = lax.dynamic_slice(
                value_buffer, (key_start, column), (key_rows, span)
            ).reshape(key_rows, per_group, HEAD_DIM)
            grad_part = lax.dynamic_slice(
                grad_mixed, (row_start, column), (block_rows, span)
            ).reshape(block_rows, per_group, HEAD_DIM)
            kept_sums = lax.dynamic_slice(
                logsums, (group_index * per_group, row_start), (per_group, block_rows)
            )
            products = jnp.einsum(
                "qhd,khd->hqk", query_part, key_part, preferred_element_type=jnp.float32
            )
            scores = jnp.where(allowed, products * factor, MASKED)
            chances = jnp.exp(scores - kept_sums[:, :, None])
            grad_chances = jnp.einsum(
                "qhd,khd->hqk", grad_part, value_part, preferred_element_type=jnp.float32
            )
            centered = jnp.sum(chances * grad_chances, axis=-1, keepdims=True)
            grad_scores = (chances * (grad_chances - centered) * factor).astype(jnp.bfloat16)
            query_grad = jnp.einsum(
                "hqk,khd->qhd", grad_scores, key_part, preferred_element_type=jnp.float32
            )
            key_grad = jnp.einsum(
                "hqk,qhd->khd", grad_scores, query_part, preferred_element_type=jnp.float32
            )
            value_grad = jnp.einsum(
                "hqk,qhd->khd",
                chances.astype(jnp.bfloat16),
                grad_part,
                preferred_element_type=jnp.float32,
            )
            grad_queries = lax.dynamic_update_slice(
                grad_queries, query_grad.reshape(block_rows, span), (row_start, column)
            )
            old_keys = lax.dynamic_slice(grad_keys, (key_start, column), (key_rows, span))
            grad_keys = lax.dynamic_update_slice(
                grad_keys, old_keys + key_grad.reshape(key_rows, span), (key_start, column)
            )
            old_values = lax.dynamic_slice(grad_values, (key_start, column), (key_rows, span))
            grad_values = lax.dynamic_update_slice(
                grad_values, old_values + value_grad.reshape(key_rows, span), (key_start, column)
            )
            return (grad_queries, grad_keys, grad_values)

        return lax.fori_loop(0, groups, one_group, carry)

    buffer_shape = (key_buffer.shape[0], feature_count)
    start_state = (
        jnp.zeros((row_count, feature_count), jnp.float32),
        jnp.zeros(buffer_shape, jnp.float32),
        jnp.zeros(buffer_shape, jnp.float32),
    )
    return lax.fori_loop(0, row_count // block_rows, one_block, start_state)


def shards(
    tokens,
    cotangent,
    doc_lengths,
    adapter_ids,
    first_gain,
    first_shift,
    qkv_weight,
    qkv_bias,
    out_weight,
    out_bias,
    second_gain,
    second_shift,
    up_weight,
    up_bias,
    down_weight,
    down_bias,
    qkv_adapt_in,
    qkv_adapt_out,
    out_adapt_in,
    out_adapt_out,
    up_adapt_in,
    up_adapt_out,
    down_adapt_in,
    down_adapt_out,
):
    gathered = (
        lax.all_gather(first_gain, "wt", axis=0, tiled=True),
        lax.all_gather(first_shift, "wt", axis=0, tiled=True),
        lax.all_gather(qkv_weight, "wt", axis=0, tiled=True),
        lax.all_gather(qkv_bias, "wt", axis=0, tiled=True),
        lax.all_gather(out_weight, "wt", axis=0, tiled=True),
        lax.all_gather(out_bias, "wt", axis=0, tiled=True),
        lax.all_gather(second_gain, "wt", axis=0, tiled=True),
        lax.all_gather(second_shift, "wt", axis=0, tiled=True),
        lax.all_gather(up_weight, "wt", axis=0, tiled=True),
        lax.all_gather(up_bias, "wt", axis=0, tiled=True),
        lax.all_gather(down_weight, "wt", axis=0, tiled=True),
        lax.all_gather(down_bias, "wt", axis=0, tiled=True),
    )
    (
        gain_one,
        shift_one,
        weight_qkv,
        bias_qkv,
        weight_out,
        bias_out,
        gain_two,
        shift_two,
        weight_up,
        bias_up,
        weight_down,
        bias_down,
    ) = gathered
    lengths = doc_lengths[0]
    chosen = adapter_ids[0, 0]

    def select(stacked):
        return lax.dynamic_index_in_dim(stacked, chosen, 0, keepdims=False)

    adapter_qkv_in = select(qkv_adapt_in)
    adapter_qkv_out = select(qkv_adapt_out)
    adapter_out_in = select(out_adapt_in)
    adapter_out_out = select(out_adapt_out)
    adapter_up_in = select(up_adapt_in)
    adapter_up_out = select(up_adapt_out)
    adapter_down_in = select(down_adapt_in)
    adapter_down_out = select(down_adapt_out)
    values = tokens[0].astype(jnp.float32)
    row_count, feature_count = values.shape
    first_query = lax.axis_index("ctx") * row_count
    reach = -(-WINDOW // row_count)
    normed_in, normed_one, inverse_one = norm_forward(
        values, gain_one.astype(jnp.float32), shift_one.astype(jnp.float32)
    )
    first_in = normed_in.astype(jnp.bfloat16)
    qkv_low = product_transposed(first_in, adapter_qkv_in).astype(jnp.bfloat16)
    qkv_all = (
        product(first_in, weight_qkv)
        + bias_qkv.astype(jnp.float32)
        + product(qkv_low, adapter_qkv_out)
    ).astype(jnp.bfloat16)
    queries = qkv_all[:, :feature_count]
    key_value = jnp.stack(
        [qkv_all[:, feature_count : 2 * feature_count], qkv_all[:, 2 * feature_count :]]
    )
    pieces = []
    for offset in range(reach, 0, -1):
        pieces.append(shifted(key_value, "ctx", offset))
    pieces.append(key_value)
    buffer = jnp.concatenate(pieces, axis=1)
    key_buffer = buffer[0]
    value_buffer = buffer[1]
    attended, logsums = attend_forward(queries, key_buffer, value_buffer, first_query, lengths)
    mixed_low = attended.astype(jnp.bfloat16)
    out_low = product_transposed(mixed_low, adapter_out_in).astype(jnp.bfloat16)
    branch = (
        product(mixed_low, weight_out)
        + bias_out.astype(jnp.float32)
        + product(out_low, adapter_out_out)
    )
    hidden = values + branch
    normed_mid, normed_two, inverse_two = norm_forward(
        hidden, gain_two.astype(jnp.float32), shift_two.astype(jnp.float32)
    )
    second_in = normed_mid.astype(jnp.bfloat16)
    up_low = product_transposed(second_in, adapter_up_in).astype(jnp.bfloat16)
    upper_sum = (
        product(second_in, weight_up)
        + bias_up.astype(jnp.float32)
        + product(up_low, adapter_up_out)
    )
    active = jax.nn.gelu(upper_sum, approximate=True).astype(jnp.bfloat16)
    down_low = product_transposed(active, adapter_down_in).astype(jnp.bfloat16)
    output = (
        hidden
        + (
            product(active, weight_down)
            + bias_down.astype(jnp.float32)
            + product(down_low, adapter_down_out)
        )
    ).astype(jnp.bfloat16)
    gain_one, weight_qkv, weight_out, gain_two, weight_up, weight_down = (
        lax.all_gather(first_gain, "wt", axis=0, tiled=True),
        lax.all_gather(qkv_weight, "wt", axis=0, tiled=True),
        lax.all_gather(out_weight, "wt", axis=0, tiled=True),
        lax.all_gather(second_gain, "wt", axis=0, tiled=True),
        lax.all_gather(up_weight, "wt", axis=0, tiled=True),
        lax.all_gather(down_weight, "wt", axis=0, tiled=True),
    )
    upstream = cotangent[0]
    grad_down_out = product_outer(down_low, upstream)
    grad_down_low = product_transposed(upstream, adapter_down_out).astype(jnp.bfloat16)
    grad_down_in = product_outer(grad_down_low, active)
    grad_active = (
        product_transposed(upstream, weight_down) + product(grad_down_low, adapter_down_in)
    ).astype(jnp.bfloat16)
    gelu_pull = jax.vjp(partial(jax.nn.gelu, approximate=True), upper_sum)[1]
    grad_upper = gelu_pull(grad_active.astype(jnp.float32))[0].astype(jnp.bfloat16)
    grad_up_out = product_outer(up_low, grad_upper)
    grad_up_low = product_transposed(grad_upper, adapter_up_out).astype(jnp.bfloat16)
    grad_up_in = product_outer(grad_up_low, second_in)
    grad_second = product_transposed(grad_upper, weight_up) + product(grad_up_low, adapter_up_in)
    grad_hidden = upstream.astype(jnp.float32) + norm_backward(
        grad_second, normed_two, inverse_two, gain_two.astype(jnp.float32)
    )
    grad_branch = grad_hidden.astype(jnp.bfloat16)
    grad_out_out = product_outer(out_low, grad_branch)
    grad_out_low = product_transposed(grad_branch, adapter_out_out).astype(jnp.bfloat16)
    grad_out_in = product_outer(grad_out_low, mixed_low)
    grad_mixed = (
        product_transposed(grad_branch, weight_out) + product(grad_out_low, adapter_out_in)
    ).astype(jnp.bfloat16)
    grad_queries, grad_keys, grad_values = attend_backward(
        queries, key_buffer, value_buffer, grad_mixed, logsums, first_query, lengths
    )
    grad_pair = jnp.stack([grad_keys, grad_values])
    owned_grads = grad_pair[:, reach * row_count :]
    for offset in range(reach, 0, -1):
        first_row = (reach - offset) * row_count
        owned_grads = owned_grads + shifted(
            grad_pair[:, first_row : first_row + row_count].astype(jnp.bfloat16), "ctx", -offset
        ).astype(jnp.float32)
    grad_qkv = jnp.concatenate([grad_queries, owned_grads[0], owned_grads[1]], axis=1).astype(
        jnp.bfloat16
    )
    grad_qkv_out = product_outer(qkv_low, grad_qkv)
    grad_qkv_low = product_transposed(grad_qkv, adapter_qkv_out).astype(jnp.bfloat16)
    grad_qkv_in = product_outer(grad_qkv_low, first_in)
    grad_first = product_transposed(grad_qkv, weight_qkv) + product(grad_qkv_low, adapter_qkv_in)
    grad_input = grad_hidden + norm_backward(
        grad_first, normed_one, inverse_one, gain_one.astype(jnp.float32)
    )
    selector = (jnp.arange(ADAPTERS, dtype=jnp.int32) == chosen).astype(jnp.float32)

    def spread_out(single):
        return selector[:, None, None] * single[None]

    stacked_qkv_in = spread_out(grad_qkv_in)
    stacked_qkv_out = spread_out(grad_qkv_out)
    stacked_out_in = spread_out(grad_out_in)
    stacked_out_out = spread_out(grad_out_out)
    stacked_up_in = spread_out(grad_up_in)
    stacked_up_out = spread_out(grad_up_out)
    stacked_down_in = spread_out(grad_down_in)
    stacked_down_out = spread_out(grad_down_out)
    totals = lax.psum(
        (
            stacked_qkv_in,
            stacked_qkv_out,
            stacked_out_in,
            stacked_out_out,
            stacked_up_in,
            stacked_up_out,
            stacked_down_in,
            stacked_down_out,
        ),
        ("dp", "ctx", "wt"),
    )
    return (
        output[None],
        grad_input[None],
        totals[0],
        totals[1],
        totals[2],
        totals[3],
        totals[4],
        totals[5],
        totals[6],
        totals[7],
    )


def solution(mesh):
    return jax.shard_map(
        shards,
        mesh=mesh,
        in_specs=(
            P(("dp", "wt"), "ctx", None),
            P(("dp", "wt"), "ctx", None),
            P(("dp", "wt"), None),
            P(("dp", "wt"), None),
            P("wt"),
            P("wt"),
            P("wt", None),
            P("wt"),
            P("wt", None),
            P("wt"),
            P("wt"),
            P("wt"),
            P("wt", None),
            P("wt"),
            P("wt", None),
            P("wt"),
            P(),
            P(),
            P(),
            P(),
            P(),
            P(),
            P(),
            P(),
        ),
        out_specs=(
            P(("dp", "wt"), "ctx", None),
            P(("dp", "wt"), "ctx", None),
            P(),
            P(),
            P(),
            P(),
            P(),
            P(),
            P(),
            P(),
        ),
        check_vma=False,
    )
```

profile of v0, /device:TPU:0, one launch (start us, length us, event | category | flops | bytes accessed | tf_op | source)
XLA Modules:
  0.0 2609.7 jit_solution(8763115180189730011)
XLA Ops:
  14.9 35.8 %all-reduce.9 = (bf16[1600]{0:T(1024)(128)(2,1)S(1)}, bf16[1600]{0:T(1024)(128)(2,1)S(1)}, bf16[4800]{0:T(1024)(128)(2,1)S(1)}, bf16[1600]{0:T(1024)(128)(2,1)S(...) all-reduce(bf16[1600]{0:T(1024)(128)(2,1)S(1)} %dynamic-update-slic, ...), channel_id=1, replica_groups=mesh['dp'=4,'ctx'=2,'wt'=4] {'wt'}, use_global_device_ids=true, to_apply=%add.1 | all-reduce | flops 20800 | bytes 83200
  68.2 211.8 %all-gather.5.cloned.1.call-done = bf16[1600,4800]{1,0:T(8,128)(2,1)} async-done(((bf16[400,4800]{1,0:T(8,128)(2,1)}), bf16[1600,4800]{1,0:T(8,128)(2,1)}) %all-gather.5.cloned.1.call-update) | async-done | bytes 15360016 | tf_op jit(solution)/shard_map/all_gather | solution.py:239
  280.0 29.0 %add_convert_fusion.1 = bf16[1024,4800]{0,1:T(8,128)(2,1)} fusion(f32[1024,4800]{0,1:T(8,128)} %fusion.116, bf16[1600,4800]{1,0:T(8,128)(2,1)} %all-gather.5.cloned.1.call-done, f32[4800]{0:T(1024)S(1)} %convert_element_type.193, bf16[1,1024,1600]{1,2,0:T(8,128)(2,1)} %param.32, f32[1600]{0:T(1024)S(1)} %convert_element_type.191, ...), kind=kOutput, calls=%fused_computation.80 | convolution fusion | flops 15753216000 | bytes 48168192 | tf_op jit(solution)/shard_map/dot_general | solution.py:25
  355.0 240.4 %while.119 = (s32[]{:T(128)}, bf16[1024,1600]{0,1:T(8,128)(2,1)}, f32[25,1024]{1,0:T(8,128)}, s32[]{:T(128)}, s32[4,1]{0,1:T(1,128)}, /*index=5*/bf16[2048,1600]...) while((s32[]{:T(128)}, bf16[1024,1600]{0,1:T(8,128)(2,1)}, ...), condition=%wide.region_10.11_spmd, body=%wide.region_3.10_spmd.sunk | while | flops 1059342848 | bytes 58343196 | solution.py:127
  355.9 122.2 %while.122 = (s32[]{:T(128)}, bf16[1024,1600]{0,1:T(8,128)(2,1)}, f32[25,1024]{1,0:T(8,128)}, bf16[2048,1600]{0,1:T(8,128)(2,1)}, s32[]{:T(128)}, /*index=5*/bf1...) while((s32[]{:T(128)}, bf16[1024,1600]{0,1:T(8,128)(2,1)}, ...), condition=%wide.region_9.9_spmd.clone, body=%wide.region_6.8_spmd.clone.sunk | while | flops 1059321344 | bytes 58316580 | solution.py:121
  478.9 116.1 %while.122 = (s32[]{:T(128)}, bf16[1024,1600]{0,1:T(8,128)(2,1)}, f32[25,1024]{1,0:T(8,128)}, bf16[2048,1600]{0,1:T(8,128)(2,1)}, s32[]{:T(128)}, /*index=5*/bf1...) while((s32[]{:T(128)}, bf16[1024,1600]{0,1:T(8,128)(2,1)}, ...), condition=%wide.region_9.9_spmd.clone, body=%wide.region_6.8_spmd.clone.sunk | while | flops 1059321344 | bytes 58316580 | solution.py:121
  627.9 100.2 %all-gather.9.cloned.1.call-done = bf16[1600,6400]{1,0:T(8,128)(2,1)} async-done(((bf16[400,6400]{1,0:T(8,128)(2,1)}), bf16[1600,6400]{1,0:T(8,128)(2,1)}) %all-gather.9.cloned.1.call-update) | async-done | bytes 20480016 | tf_op jit(solution)/shard_map/all_gather | solution.py:245
  728.1 47.3 %multiply_convert_fusion.1 = (bf16[1024,6400]{1,0:T(8,128)(2,1)}, f32[1024,6400]{1,0:T(8,128)}) fusion(f32[1024,6400]{1,0:T(8,128)} %fusion.109, f32[6400]{0:T(1024)S(1)} %copy-done.40, bf16[1024,1600]{0,1:T(8,128)(2,1)} %copy-done.13, bf16[1600,6400]{1,0:T(8,128)(2,1)} %all-gather.9.cloned.1.call-done), kind=kOutput, calls=%fused_computation.78 | convolution fusion | flops 21043609600 | bytes 89318400 | tf_op jit(solution)/shard_map/dot_general | solution.py:25
  775.4 315.0 %all-gather.11.cloned.1.call-done = bf16[6400,1600]{1,0:T(8,128)(2,1)} async-done(((bf16[1600,1600]{1,0:T(8,128)(2,1)}), bf16[6400,1600]{1,0:T(8,128)(2,1)}) %all-gather.11.cloned.1.call-update) | async-done | bytes 20480016 | tf_op jit(solution)/shard_map/all_gather | solution.py:247
  1090.4 49.1 %fusion.59 = bf16[1024,6400]{1,0:T(8,128)(2,1)} fusion(f32[1024,6400]{1,0:T(8,128)} %get-tuple-element.1439, f32[1024,6400]{1,0:T(8,128)} %fusion.105, bf16[6400,1600]{1,0:T(8,128)(2,1)} %all-gather.11.cloned.1.call-done, bf16[1,1024,1600]{1,2,0:T(8,128)(2,1)} %param.33), kind=kOutput, calls=%fused_computation.67 | convolution fusion | flops 21122252800 | bytes 89292800 | tf_op jit(solution)/shard_map/dot_general | solution.py:29
  1149.7 31.0 %fusion.174 = (f32[1024]{0:T(1024)S(1)}, f32[1024]{0:T(1024)S(1)}, f32[1024,1600]{0,1:T(8,128)}) fusion(f32[1024]{0:T(1024)S(1)} %add_rsqrt_fusion, f32[1024,1600]{0,1:T(8,128)} %copy-done.2, f32[1024]{0:T(1024)S(1)} %broadcast_multiply_fusion.12, f32[1600]{0:T(1024)S(1)} %copy-done.38, f32[1024,1600]{0,1:T(8,128)S(1)} %fusion.123, ...), kind=kOutput, calls=%fused_computation.226 | convolution fusion | flops 20982988800 | bytes 53270784 | tf_op jit(solution)/shard_map/dot_general | solution.py:29
  1220.5 1054.7 %while.121 = (s32[]{:T(128)}, bf16[1024,1600]{0,1:T(8,128)(2,1)}, f32[2048,1600]{0,1:T(8,128)}, f32[2048,1600]{0,1:T(8,128)}, s32[]{:T(128)}, /*index=5*/s32[4,1...) while((s32[]{:T(128)}, bf16[1024,1600]{0,1:T(8,128)(2,1)}, ...), condition=%wide.region_21.22_spmd, body=%wide.region_15.21_spmd.sunk | while | flops 2625336320 | bytes 147421040 | solution.py:207
  1221.6 530.6 %while.123 = (s32[]{:T(128)}, bf16[1024,1600]{0,1:T(8,128)(2,1)}, f32[2048,1600]{0,1:T(8,128)}, f32[2048,1600]{0,1:T(8,128)}, bf16[2048,1600]{0,1:T(8,128)(2,1)}...) while((s32[]{:T(128)}, bf16[1024,1600]{0,1:T(8,128)(2,1)}, ...), condition=%wide.region_20.20_spmd.clone, body=%wide.region_18.19_spmd.clone.sunk | while | flops 2625314816 | bytes 147394368 | solution.py:199
  1280.1 25.1 fusion.268
  1386.2 25.1 fusion.268
  1704.7 25.1 fusion.268
  1753.0 522.0 %while.123 = (s32[]{:T(128)}, bf16[1024,1600]{0,1:T(8,128)(2,1)}, f32[2048,1600]{0,1:T(8,128)}, f32[2048,1600]{0,1:T(8,128)}, bf16[2048,1600]{0,1:T(8,128)(2,1)}...) while((s32[]{:T(128)}, bf16[1024,1600]{0,1:T(8,128)(2,1)}, ...), condition=%wide.region_20.20_spmd.clone, body=%wide.region_18.19_spmd.clone.sunk | while | flops 2625314816 | bytes 147394368 | solution.py:199
  1810.9 25.1 fusion.268
  1915.3 25.1 fusion.268
  2019.8 25.1 fusion.268
  2228.7 25.1 fusion.268
  2343.1 31.7 %fusion.98 = bf16[1,1024,1600]{1,2,0:T(8,128)(2,1)} fusion(f32[1024,1600]{0,1:T(8,128)} %copy-done.2, f32[1024,1600]{0,1:T(8,128)} %fusion.121, f32[1600]{0:T(1024)S(1)} %convert_element_type.207, bf16[1024,6400]{1,0:T(8,128)(2,1)} %get-tuple-element.1438, bf16[6400,1600]{1,0:T(8,128)(2,1)} %all-gather.11.cloned.1.call-done), kind=kOutput, calls=%fused_computation.133 | convolution fusion | flops 20978073600 | bytes 49977600 | tf_op jit(solution)/shard_map/dot_general | solution.py:25
  2379.6 27.4 %fusion.173 = (f32[1024]{0:T(1024)S(1)}, f32[1024]{0:T(1024)S(1)}, f32[1024,1600]{0,1:T(8,128)}) fusion(f32[1024]{0:T(1024)S(1)} %copy-done.42, f32[1024]{0:T(1024)S(1)} %copy-done.36, bf16[1,1024,1600]{1,2,0:T(8,128)(2,1)S(1)} %copy-done.7, f32[1600]{0:T(1024)S(1)} %copy-done.44, f32[1024,1600]{0,1:T(8,128)} %fusion.130, ...), kind=kOutput, calls=%fused_computation.225 | convolution fusion | flops 15771236352 | bytes 41597184 | tf_op jit(solution)/shard_map/dot_general | solution.py:29
  2415.8 174.5 %all-reduce.12.cloned.1.call-done = (f32[8,16,1600]{2,1,0:T(8,128)}, f32[8,16,4800]{2,1,0:T(8,128)}, f32[8,16,1600]{2,1,0:T(8,128)}, f32[8,16,1600]{2,1,0:T(8,12...) async-done(((f32[8,16,1600]{2,1,0:T(8,128)}, f32[8,16,4800]{2,1,0:T(8,128)}, f32[8,16,1600]{2,1,0:T(8,128)}, ...) | async-done | bytes 13107216 | tf_op jit(solution)/shard_map/psum | solution.py:396
  (520 shorter events, 1362.3 us)
Async XLA Ops:
  7.2 610.0 %copy-start = (bf16[8,16,6400]{2,1,0:T(8,128)(2,1)S(1)}, bf16[8,16,6400]{2,1,0:T(8,128)(2,1)}, u32[]{:S(2)}) copy-start(bf16[8,16,6400]{2,1,0:T(8,128)(2,1)} %param.53) | copy-start | bytes 4915204
  7.3 272.7 %all-gather.5.cloned.1.call-start = ((), (), s32[]{:S(2)}) async-start(), calls=%async_computation | async-start | bytes 19456000 | tf_op jit(solution)/shard_map/all_gather | solution.py:239
  8.0 590.0 %all-gather.7.cloned.1.call-start = ((), (), s32[]{:S(2)}) async-start(), calls=%async_computation.1 | async-start | bytes 6656000 | tf_op jit(solution)/shard_map/all_gather | solution.py:241
  8.8 719.3 %all-gather.9.cloned.1.call-start = ((), (), s32[]{:S(2)}) async-start(), calls=%async_computation.2 | async-start | bytes 25600000 | tf_op jit(solution)/shard_map/all_gather | solution.py:245
  9.5 1080.9 %all-gather.11.cloned.1.call-start = ((), (), s32[]{:S(2)}) async-start(), calls=%async_computation.3 | async-start | bytes 26624000 | tf_op jit(solution)/shard_map/all_gather | solution.py:247
  50.7 229.3 %copy-start.45 = (f32[1600]{0:T(1024)}, f32[1600]{0:T(1024)S(1)}, u32[]{:S(2)}) copy-start(f32[1600]{0:T(1024)S(1)} %convert_element_type.191) | copy-start | bytes 19204
  50.7 229.3 %copy-start.43 = (f32[1600]{0:T(1024)}, f32[1600]{0:T(1024)S(1)}, u32[]{:S(2)}) copy-start(f32[1600]{0:T(1024)S(1)} %convert_element_type.190) | copy-start | bytes 19204
  53.5 226.5 %copy-start.35 = (f32[1024]{0:T(1024)}, f32[1024]{0:T(1024)S(1)}, u32[]{:S(2)}) copy-start(f32[1024]{0:T(1024)S(1)} %broadcast_multiply_fusion.13) | copy-start | bytes 12292
  56.4 223.6 %copy-start.41 = (f32[1024]{0:T(1024)}, f32[1024]{0:T(1024)S(1)}, u32[]{:S(2)}) copy-start(f32[1024]{0:T(1024)S(1)} %add_rsqrt_fusion.1) | copy-start | bytes 12292
  319.6 22.1 collective-permute-start
  324.2 2266.1 %all-reduce.12.cloned.1.call-start = ((), (), s32[]{:S(2)}) async-start(), calls=%async_computation.4 | async-start | bytes 26607616 | tf_op jit(solution)/shard_map/psum | solution.py:396
  329.9 11.8 copy-start.11
  617.2 110.9 %copy-start.40 = (f32[6400]{0:T(1024)S(1)}, f32[6400]{0:T(1024)}, u32[]{:S(2)}) copy-start(f32[6400]{0:T(1024)} %convert_element_type.204) | copy-start | bytes 76804
  1147.7 33.1 %copy-start.23 = (bf16[1024,16]{0,1:T(8,128)(2,1)}, bf16[1024,16]{0,1:T(8,128)(2,1)S(1)}, u32[]{:S(2)}) copy-start(bf16[1024,16]{0,1:T(8,128)(2,1)S(1)} %convolution_convert_fusion.4) | copy-start | bytes 98308
  1147.7 33.1 %slice-start.8 = ((s8[6553600]{0:T(1024)(128)(4,1)}), s8[4194304]{0:T(1024)(128)(4,1)S(1)}, s32[]{:S(2)}) async-start(s8[6553600]{0:T(1024)(128)(4,1)} %bitcast.261), calls=%async_computation.13 | async-start | bytes 8388608
  1149.7 31.0 %slice-start.9 = ((s8[6553600]{0:T(1024)(128)(4,1)}), s8[2359296]{0:T(1024)(128)(4,1)S(1)}, s32[]{:S(2)}) async-start(s8[6553600]{0:T(1024)(128)(4,1)} %bitcast.261), calls=%async_computation.14 | async-start | bytes 4718592
  2275.3 12.7 copy-start.24
  2283.8 39.9 %collective-permute-start.1 = (bf16[2,1024,1600]{1,2,0:T(8,128)(2,1)}, bf16[2,1024,1600]{1,2,0:T(8,128)(2,1)}, u32[]{:S(2)}, u32[]{:S(2)}) collective-permute-start(bf16[2,1024,1600]{1,2,0:T(8,128)(2,1)} %fusion.70), channel_id=1, source_target_pairs={{4,0},{5,1},{6,2},{7,3},{12,8},{13,9},{14,10},{15,11},{20,16},{21,... | collective-permute-start | bytes 19660808 | tf_op jit(solution)/shard_map/ppermute | solution.py:21
  2306.2 17.5 slice-start
  2306.2 17.5 slice-start.1
  2306.2 17.5 slice-start.4
  2306.3 17.5 slice-start.5
  2374.8 32.2 %slice-start.12 = ((s8[6553600]{0:T(1024)(128)(4,1)}), s8[4194304]{0:T(1024)(128)(4,1)S(1)}, s32[]{:S(2)}) async-start(s8[6553600]{0:T(1024)(128)(4,1)} %bitcast.265), calls=%async_computation.17 | async-start | bytes 8388608
  2379.6 27.4 %slice-start.13 = ((s8[6553600]{0:T(1024)(128)(4,1)}), s8[2359296]{0:T(1024)(128)(4,1)S(1)}, s32[]{:S(2)}) async-start(s8[6553600]{0:T(1024)(128)(4,1)} %bitcast.265), calls=%async_computation.18 | async-start | bytes 4718592
  (55 other events, 329.3 us)
Sparse Core Ops, SparseCore 0:
  9.7 270.2 all-gather.4
  281.6 97.6 all-gather.6
  380.9 347.1 all-gather.8
  729.5 360.8 all-gather.10
  2343.2 247.1 all-reduce.11
where the time goes:
time: 2620 us; the launch traced here: 2610 us
  matrix products  1150 us (44%)
  waiting for transfers between devices  804 us (31%)
  local copies, waits for them, and re-layouts  431 us (16%)
  other arithmetic  167 us (6%)
  blocking collectives  35.8 us (1%)
    all_gather x1, waiting for transfers between devices, shards(): lax.all_gather(down_weight, 'wt', axis=0, tiled=True)  315 us
    dot_general x10, matrix products, one_group(): jnp.einsum('hqk,qhd->khd', grad_scores, query_part, preferred_element_typ...  251 us
    dot_general x10, matrix products, one_group(): jnp.einsum('hqk,khd->qhd', grad_scores, key_part, preferred_element_type=...  230 us
    all_gather x1, waiting for transfers between devices, shards(): lax.all_gather(qkv_weight, 'wt', axis=0, tiled=True)  212 us
    psum x1, waiting for transfers between devices, shards(): lax.psum((stacked_qkv_in, stacked_qkv_out, stacked_out_in, stacked_out_ou...  175 us
    dot_general x12, matrix products, product(): return jnp.dot(left_side, right_side, preferred_element_type=jnp.float32)  168 us
    dot_general x12, matrix products, product_transposed(): lax.dot_general(left_side, right_side, (((1,), (1,)), ((), ())), preferre...  147 us
    dot_general x20, matrix products, one_group(): jnp.einsum('qhd,khd->hqk', query_part, key_part, preferred_element_type=j...  107 us
  transfers between devices with their start and end apart: 7, of which 4 were waited for; matrix products, arithmetic and copies ran while one was open for 20% of the time, Pallas kernels for 0%

commit v1 on v0

--- a/solution.py
+++ b/solution.py
@@ -3,6 +3,8 @@
 import jax
 import jax.numpy as jnp
 from jax import lax
+from jax.experimental import pallas as pl
+from jax.experimental.pallas import tpu as pltpu
 from jax.sharding import PartitionSpec as P
 
 HEADS = 25
@@ -53,158 +55,181 @@
     )
 
 
-def document_index(positions, lengths):
-    bounds = jnp.cumsum(lengths)[:-1]
-    return jnp.sum((positions[:, None] >= bounds[None, :]).astype(jnp.int32), axis=1)
-
-
-def block_mask(query_pos, key_pos, lengths):
-    query_doc = document_index(query_pos, lengths)
-    key_doc = document_index(key_pos, lengths)
-    distance = query_pos[:, None] - key_pos[None, :]
-    same_doc = query_doc[:, None] == key_doc[None, :]
-    return (key_pos[None, :] >= 0) & same_doc & (distance >= 0) & (distance < WINDOW)
-
-
-def head_grouping():
-    per_group = max((divisor for divisor in range(1, 9) if HEADS % divisor == 0))
-    return (per_group, HEADS // per_group)
-
-
-def attend_forward(queries, key_buffer, value_buffer, first_query, lengths):
-    row_count, feature_count = queries.shape
-    block_rows = min(512, row_count)
-    key_rows = WINDOW + block_rows
-    offset_rows = key_buffer.shape[0] - row_count
-    per_group, groups = head_grouping()
-    span = per_group * HEAD_DIM
-    factor = HEAD_DIM ** (-0.5)
-
-    def one_block(block_index, carry):
-        row_start = block_index * block_rows
-        query_pos = first_query + row_start + jnp.arange(block_rows, dtype=jnp.int32)
-        key_pos = first_query + row_start - WINDOW + jnp.arange(key_rows, dtype=jnp.int32)
-        allowed = block_mask(query_pos, key_pos, lengths)[None]
-        key_start = offset_rows + row_start - WINDOW
-
-        def one_group(group_index, inner):
-            attended, logsums = inner
-            column = group_index * span
-            query_part = lax.dynamic_slice(
-                queries, (row_start, column), (block_rows, span)
-            ).reshape(block_rows, per_group, HEAD_DIM)
-            key_part = lax.dynamic_slice(key_buffer, (key_start, column), (key_rows, span)).reshape(
-                key_rows, per_group, HEAD_DIM
+TILE = 256
+REACH_TILES = WINDOW // TILE
+SPAN_TILES = REACH_TILES + 1
+PAIRS = (HEADS + 1) // 2
+PADDED = PAIRS * 128
+FACTOR = HEAD_DIM ** (-0.5)
+
+
+def split_pair(pair):
+    lane = lax.broadcasted_iota(jnp.int32, pair.shape, 1)
+    zero = jnp.zeros_like(pair)
+    return jnp.concatenate(
+        [jnp.where(lane < HEAD_DIM, pair, zero), jnp.where(lane >= HEAD_DIM, pair, zero)], axis=0
+    )
+
+
+def join_pair(stacked):
+    lane = lax.broadcasted_iota(jnp.int32, (TILE, 128), 1)
+    return jnp.where(lane < HEAD_DIM, stacked[:TILE], stacked[TILE:])
+
+
+def tile_bias(bounds, query_start, key_start):
+    rows = query_start + lax.broadcasted_iota(jnp.int32, (TILE, 1), 0)
+    columns = key_start + lax.broadcasted_iota(jnp.int32, (1, TILE), 1)
+    row_doc = sum((rows >= bound).astype(jnp.int32) for bound in bounds)
+    column_doc = sum((columns >= bound).astype(jnp.int32) for bound in bounds)
+    shape = (TILE, TILE)
+    distance = jnp.broadcast_to(rows, shape) - jnp.broadcast_to(columns, shape)
+    same = jnp.broadcast_to(row_doc, shape) == jnp.broadcast_to(column_doc, shape)
+    seen = jnp.broadcast_to(columns, shape) >= 0
+    return jnp.where(same & seen & (distance >= 0) & (distance < WINDOW), 0.0, MASKED)
+
+
+def fill_biases(meta, bias_scr, tiles):
+    bounds = [meta[place] for place in range(3)]
+    first = meta[3]
+
+    def one(step, carry):
+        tile = step // SPAN_TILES
+        key_tile = tile + lax.rem(step, SPAN_TILES) - REACH_TILES
+        bias_scr[step] = tile_bias(bounds, first + tile * TILE, first + key_tile * TILE)
+        return carry
+
+    lax.fori_loop(0, tiles * SPAN_TILES, one, 0)
+
+
+def attend_forward_kernel(tiles, meta, q_ref, k_ref, v_ref, o_ref, lse_ref, bias_scr, acc_scr, va_scr):
+    @pl.when(pl.program_id(0) == 0)
+    def _():
+        fill_biases(meta, bias_scr, tiles)
+        va_scr[:, 128:] = jnp.ones((va_scr.shape[0], 128), jnp.bfloat16)
+
+    va_scr[:, :128] = v_ref[...]
+    chunk = TILE // 2
+    for tile in range(tiles):
+        stacked = split_pair(q_ref[pl.ds(tile * TILE, TILE), :] * FACTOR)
+        window = pl.ds(tile * TILE, SPAN_TILES * TILE)
+        keys = k_ref[window, :]
+        values = va_scr[window, :]
+        for part in range(2 * TILE // chunk):
+            start = part * chunk
+            bias_rows = pl.ds(start % TILE, chunk)
+            bias = jnp.concatenate(
+                [bias_scr[tile * SPAN_TILES + t, bias_rows, :] for t in range(SPAN_TILES)], axis=1
             )
-            value_part = lax.dynamic_slice(
-                value_buffer, (key_start, column), (key_rows, span)
-            ).reshape(key_rows, per_group, HEAD_DIM)
-            products = jnp.einsum(
-                "qhd,khd->hqk", query_part, key_part, preferred_element_type=jnp.float32
-            )
-            scores = jnp.where(allowed, products * factor, MASKED)
-            highest = jnp.max(scores, axis=-1, keepdims=True)
-            exponent = jnp.exp(scores - highest)
-            summed = jnp.sum(exponent, axis=-1, keepdims=True)
-            chances = (exponent / summed).astype(jnp.bfloat16)
-            combined = jnp.einsum(
-                "hqk,khd->qhd", chances, value_part, preferred_element_type=jnp.float32
-            )
-            attended = lax.dynamic_update_slice(
-                attended, combined.reshape(block_rows, span), (row_start, column)
-            )
-            logsums = lax.dynamic_update_slice(
-                logsums, (highest + jnp.log(summed))[:, :, 0], (group_index * per_group, row_start)
-            )
-            return (attended, logsums)
-
-        return lax.fori_loop(0, groups, one_group, carry)
-
-    start_state = (
-        jnp.zeros((row_count, feature_count), jnp.float32),
-        jnp.zeros((HEADS, row_count), jnp.float32),
-    )
-    return lax.fori_loop(0, row_count // block_rows, one_block, start_state)
-
-
-def attend_backward(queries, key_buffer, value_buffer, grad_mixed, logsums, first_query, lengths):
-    row_count, feature_count = queries.shape
-    block_rows = min(512, row_count)
-    key_rows = WINDOW + block_rows
-    offset_rows = key_buffer.shape[0] - row_count
-    per_group, groups = head_grouping()
-    span = per_group * HEAD_DIM
-    factor = HEAD_DIM ** (-0.5)
-
-    def one_block(block_index, carry):
-        row_start = block_index * block_rows
-        query_pos = first_query + row_start + jnp.arange(block_rows, dtype=jnp.int32)
-        key_pos = first_query + row_start - WINDOW + jnp.arange(key_rows, dtype=jnp.int32)
-        allowed = block_mask(query_pos, key_pos, lengths)[None]
-        key_start = offset_rows + row_start - WINDOW
-
-        def one_group(group_index, inner):
-            grad_queries, grad_keys, grad_values = inner
-            column = group_index * span
-            query_part = lax.dynamic_slice(
-                queries, (row_start, column), (block_rows, span)
-            ).reshape(block_rows, per_group, HEAD_DIM)
-            key_part = lax.dynamic_slice(key_buffer, (key_start, column), (key_rows, span)).reshape(
-                key_rows, per_group, HEAD_DIM
-            )
-            value_part = lax.dynamic_slice(
-                value_buffer, (key_start, column), (key_rows, span)
-            ).reshape(key_rows, per_group, HEAD_DIM)
-            grad_part = lax.dynamic_slice(
-                grad_mixed, (row_start, column), (block_rows, span)
-            ).reshape(block_rows, per_group, HEAD_DIM)
-            kept_sums = lax.dynamic_slice(
-                logsums, (group_index * per_group, row_start), (per_group, block_rows)
-            )
-            products = jnp.einsum(
-                "qhd,khd->hqk", query_part, key_part, preferred_element_type=jnp.float32
-            )
-            scores = jnp.where(allowed, products * factor, MASKED)
-            chances = jnp.exp(scores - kept_sums[:, :, None])
-            grad_chances = jnp.einsum(
-                "qhd,khd->hqk", grad_part, value_part, preferred_element_type=jnp.float32
-            )
-            centered = jnp.sum(chances * grad_chances, axis=-1, keepdims=True)
-            grad_scores = (chances * (grad_chances - centered) * factor).astype(jnp.bfloat16)
-            query_grad = jnp.einsum(
-                "hqk,khd->qhd", grad_scores, key_part, preferred_element_type=jnp.float32
-            )
-            key_grad = jnp.einsum(
-                "hqk,qhd->khd", grad_scores, query_part, preferred_element_type=jnp.float32
-            )
-            value_grad = jnp.einsum(
-                "hqk,qhd->khd",
-                chances.astype(jnp.bfloat16),
-                grad_part,
-                preferred_element_type=jnp.float32,
-            )
-            grad_queries = lax.dynamic_update_slice(
-                grad_queries, query_grad.reshape(block_rows, span), (row_start, column)
-            )
-            old_keys = lax.dynamic_slice(grad_keys, (key_start, column), (key_rows, span))
-            grad_keys = lax.dynamic_update_slice(
-                grad_keys, old_keys + key_grad.reshape(key_rows, span), (key_start, column)
-            )
-            old_values = lax.dynamic_slice(grad_values, (key_start, column), (key_rows, span))
-            grad_values = lax.dynamic_update_slice(
-                grad_values, old_values + value_grad.reshape(key_rows, span), (key_start, column)
-            )
-            return (grad_queries, grad_keys, grad_values)
-
-        return lax.fori_loop(0, groups, one_group, carry)
-
-    buffer_shape = (key_buffer.shape[0], feature_count)
-    start_state = (
-        jnp.zeros((row_count, feature_count), jnp.float32),
-        jnp.zeros(buffer_shape, jnp.float32),
-        jnp.zeros(buffer_shape, jnp.float32),
-    )
-    return lax.fori_loop(0, row_count // block_rows, one_block, start_state)
+            scores = product_transposed(stacked[start : start + chunk], keys) + bias
+            highest = jnp.max(scores, axis=1, keepdims=True)
+            mixed = product(jnp.exp(scores - highest).astype(jnp.bfloat16), values)
+            summed = mixed[:, 128:]
+            acc_scr[pl.ds(start, chunk), :] = mixed[:, :128] / summed
+            lse_ref[pl.ds(tile * 2 * TILE + start, chunk), :] = highest + jnp.log(summed)
+        o_ref[pl.ds(tile * TILE, TILE), :] = join_pair(acc_scr[...]).astype(jnp.bfloat16)
+
+
+def attend_forward(meta, queries, keys, values):
+    rows, key_rows = queries.shape[0], keys.shape[0]
+    tiles = rows // TILE
+    column = lambda count: pl.BlockSpec((count, 128), lambda j, m: (0, j))
+    return pl.pallas_call(
+        partial(attend_forward_kernel, tiles),
+        grid_spec=pltpu.PrefetchScalarGridSpec(
+            num_scalar_prefetch=1,
+            grid=(PAIRS,),
+            in_specs=[column(rows), column(key_rows), column(key_rows)],
+            out_specs=[column(rows), pl.BlockSpec((None, 2 * rows, 128), lambda j, m: (j, 0, 0))],
+            scratch_shapes=[
+                pltpu.VMEM((tiles * SPAN_TILES, TILE, TILE), jnp.float32),
+                pltpu.VMEM((2 * TILE, 128), jnp.float32),
+                pltpu.VMEM((key_rows, 256), jnp.bfloat16),
+            ],
+        ),
+        out_shape=[
+            jax.ShapeDtypeStruct((rows, PADDED), jnp.bfloat16),
+            jax.ShapeDtypeStruct((PAIRS, 2 * rows, 128), jnp.float32),
+        ],
+        compiler_params=pltpu.CompilerParams(vmem_limit_bytes=56 << 20),
+        name="attend_forward",
+    )(meta, queries, keys, values)
+
+
+def attend_backward_kernel(
+    tiles, meta, q_ref, k_ref, v_ref, g_ref, o_ref, lse_ref,
+    dq_ref, dk_far_ref, dk_ref, dv_far_ref, dv_ref, bias_scr, dq_scr, dkt, dvt,
+):
+    @pl.when(pl.program_id(0) == 0)
+    def _():
+        fill_biases(meta, bias_scr, tiles)
+
+    dkt[...] = jnp.zeros_like(dkt)
+    dvt[...] = jnp.zeros_like(dvt)
+    for tile in range(tiles):
+        rows = pl.ds(tile * TILE, TILE)
+        queries = split_pair(q_ref[rows, :] * FACTOR)
+        grads = split_pair(g_ref[rows, :])
+        mixed = o_ref[rows, :].astype(jnp.float32)
+        centered = jnp.sum(
+            grads.astype(jnp.float32) * jnp.concatenate([mixed, mixed], axis=0), axis=1, keepdims=True
+        )
+        lse = lse_ref[pl.ds(tile * 2 * TILE, 2 * TILE), :]
+        lse = jnp.concatenate([lse, lse], axis=1)
+        queries_t = queries.T
+        grads_t = grads.T
+        dq_scr[...] = jnp.zeros_like(dq_scr)
+        for t in range(SPAN_TILES):
+            at = pl.ds((tile + t) * TILE, TILE)
+            keys = k_ref[at, :]
+            bias = bias_scr[tile * SPAN_TILES + t]
+            scores = product_transposed(queries, keys)
+            chances = jnp.exp(scores + jnp.concatenate([bias, bias], axis=0) - lse)
+            grad_chances = product_transposed(grads, v_ref[at, :])
+            grad_scores = (chances * (grad_chances - centered)).astype(jnp.bfloat16)
+            dvt[tile + t] += product(grads_t, chances.astype(jnp.bfloat16))
+            dkt[tile + t] += product(queries_t, grad_scores)
+            dq_scr[...] += product(grad_scores, keys)
+        dq_ref[rows, :] = (join_pair(dq_scr[...]) * FACTOR).astype(jnp.bfloat16)
+    for t in range(tiles + REACH_TILES):
+        if t < REACH_TILES:
+            at = pl.ds(t * TILE, TILE)
+            dk_far_ref[at, :] = dkt[t].T.astype(jnp.bfloat16)
+            dv_far_ref[at, :] = dvt[t].T.astype(jnp.bfloat16)
+        else:
+            at = pl.ds((t - REACH_TILES) * TILE, TILE)
+            dk_ref[at, :] = dkt[t].T
+            dv_ref[at, :] = dvt[t].T
+
+
+def attend_backward(meta, queries, keys, values, grad_mixed, mixed, lse):
+    rows, key_rows = queries.shape[0], keys.shape[0]
+    tiles = rows // TILE
+    column = lambda count: pl.BlockSpec((count, 128), lambda j, m: (0, j))
+    out = lambda count, kind: jax.ShapeDtypeStruct((count, PADDED), kind)
+    return pl.pallas_call(
+        partial(attend_backward_kernel, tiles),
+        grid_spec=pltpu.PrefetchScalarGridSpec(
+            num_scalar_prefetch=1,
+            grid=(PAIRS,),
+            in_specs=[
+                column(rows), column(key_rows), column(key_rows), column(rows), column(rows),
+                pl.BlockSpec((None, 2 * rows, 128), lambda j, m: (j, 0, 0)),
+            ],
+            out_specs=[column(rows), column(WINDOW), column(rows), column(WINDOW), column(rows)],
+            scratch_shapes=[
+                pltpu.VMEM((tiles * SPAN_TILES, TILE, TILE), jnp.float32),
+                pltpu.VMEM((2 * TILE, 128), jnp.float32),
+                pltpu.VMEM((key_rows // TILE, 128, TILE), jnp.float32),
+                pltpu.VMEM((key_rows // TILE, 128, TILE), jnp.float32),
+            ],
+        ),
+        out_shape=[
+            out(rows, jnp.bfloat16), out(WINDOW, jnp.bfloat16), out(rows, jnp.float32),
+            out(WINDOW, jnp.bfloat16), out(rows, jnp.float32),
+        ],
+        compiler_params=pltpu.CompilerParams(vmem_limit_bytes=56 << 20),
+        name="attend_backward",
+    )(meta, queries, keys, values, grad_mixed, mixed, lse)
 
 
 def shards(
@@ -289,9 +314,13 @@
         + bias_qkv.astype(jnp.float32)
         + product(qkv_low, adapter_qkv_out)
     ).astype(jnp.bfloat16)
-    queries = qkv_all[:, :feature_count]
+    padding = ((0, 0), (0, PADDED - feature_count))
+    queries = jnp.pad(qkv_all[:, :feature_count], padding)
     key_value = jnp.stack(
-        [qkv_all[:, feature_count : 2 * feature_count], qkv_all[:, 2 * feature_count :]]
+        [
+            jnp.pad(qkv_all[:, feature_count : 2 * feature_count], padding),
+            jnp.pad(qkv_all[:, 2 * feature_count :], padding),
+        ]
     )
     pieces = []
     for offset in range(reach, 0, -1):
@@ -300,8 +329,9 @@
     buffer = jnp.concatenate(pieces, axis=1)
     key_buffer = buffer[0]
     value_buffer = buffer[1]
-    attended, logsums = attend_forward(queries, key_buffer, value_buffer, first_query, lengths)
-    mixed_low = attended.astype(jnp.bfloat16)
+    meta = jnp.concatenate([jnp.cumsum(lengths)[:3], first_query[None]]).astype(jnp.int32)
+    mixed_padded, logsums = attend_forward(meta, queries, key_buffer, value_buffer)
+    mixed_low = mixed_padded[:, :feature_count]
     out_low = product_transposed(mixed_low, adapter_out_in).astype(jnp.bfloat16)
     branch = (
         product(mixed_low, weight_out)
@@ -360,18 +390,23 @@
     grad_mixed = (
         product_transposed(grad_branch, weight_out) + product(grad_out_low, adapter_out_in)
     ).astype(jnp.bfloat16)
-    grad_queries, grad_keys, grad_values = attend_backward(
-        queries, key_buffer, value_buffer, grad_mixed, logsums, first_query, lengths
-    )
-    grad_pair = jnp.stack([grad_keys, grad_values])
-    owned_grads = grad_pair[:, reach * row_count :]
+    grad_queries, far_keys, near_keys, far_values, near_values = attend_backward(
+        meta, queries, key_buffer, value_buffer, jnp.pad(grad_mixed, padding), mixed_padded, logsums
+    )
+    far_pair = jnp.stack([far_keys, far_values])
+    owned_keys, owned_values = near_keys, near_values
     for offset in range(reach, 0, -1):
         first_row = (reach - offset) * row_count
-        owned_grads = owned_grads + shifted(
-            grad_pair[:, first_row : first_row + row_count].astype(jnp.bfloat16), "ctx", -offset
-        ).astype(jnp.float32)
-    grad_qkv = jnp.concatenate([grad_queries, owned_grads[0], owned_grads[1]], axis=1).astype(
-        jnp.bfloat16
+        moved = shifted(far_pair[:, first_row : first_row + row_count], "ctx", -offset)
+        owned_keys = owned_keys + moved[0].astype(jnp.float32)
+        owned_values = owned_values + moved[1].astype(jnp.float32)
+    grad_qkv = jnp.concatenate(
+        [
+            grad_queries[:, :feature_count],
+            owned_keys[:, :feature_count].astype(jnp.bfloat16),
+            owned_values[:, :feature_count].astype(jnp.bfloat16),
+        ],
+        axis=1,
     )
     grad_qkv_out = product_outer(qkv_low, grad_qkv)
     grad_qkv_low = product_transposed(grad_qkv, adapter_qkv_out).astype(jnp.bfloat16)

time: 2620 us -> 1670 us (0.64)
  matrix products: 1150 us -> 324 us
  local copies, waits for them, and re-layouts: 431 us -> 65.2 us
  waiting for transfers between devices: 804 us -> 991 us
  Pallas kernels: 0 us -> 164 us
  other arithmetic: 167 us -> 60 us
    dot_general x70 -> x0, matrix products: 806 us -> none  [the longest x10 251 us: one_group(): jnp.einsum('hqk,qhd->khd', grad_scores, query_part, preferred_element_typ...]
    dynamic_update_slice x50 -> x0, local copies, waits for them, and re-layouts: 287 us -> none  [the longest x10 89.8 us: one_group(): lax.dynamic_update_slice(grad_keys, old_keys + key_grad.reshape(key_rows,...]
    all_gather x1, waiting for transfers between devices: 100 us -> 283 us  [shards(): lax.all_gather(up_weight, 'wt', axis=0, tiled=True)]
    pallas_call x0 -> x2, Pallas kernels: none -> 164 us  [the longest x1 107 us: attend_backward(): pl.pallas_call(partial(attend_backward_kernel, tiles), grid_spec=pltpu.Pr...]
    dynamic_slice x80 -> x0, local copies, waits for them, and re-layouts: 89.2 us -> none  [the longest x20 25.4 us: one_group(): lax.dynamic_slice(value_buffer, (key_start, column), (key_rows, span))]
    reduce_sum x18 -> x0, other arithmetic: 42.2 us -> none  [the longest x10 41.5 us: one_group(): summed = jnp.sum(exponent, axis=-1, keepdims=True)]
    add x28 -> x0, other arithmetic: 41 us -> none  [the longest x10 40.9 us: one_group(): old_values + value_grad.reshape(key_rows, span)]
  transfers between devices with their start and end apart: 7 -> 7, of which waited for: 4 -> 4; matrix products, arithmetic and copies ran while one was open for 20% -> 16% of each run, Pallas kernels for 0% -> 3%
where the time goes in v1:
time: 1670 us; the launch traced here: 1660 us
  waiting for transfers between devices  991 us (59%)
  matrix products  324 us (19%)
  Pallas kernels  164 us (10%)
  local copies, waits for them, and re-layouts  65.2 us (4%)
  other arithmetic  60 us (4%)
  blocking collectives  35.9 us (2%)
  between operations  17.3 us (1%)
    all_gather x1, waiting for transfers between devices, shards(): lax.all_gather(down_weight, 'wt', axis=0, tiled=True)  315 us
    all_gather x1, waiting for transfers between devices, shards(): lax.all_gather(up_weight, 'wt', axis=0, tiled=True)  283 us
    all_gather x1, waiting for transfers between devices, shards(): lax.all_gather(qkv_weight, 'wt', axis=0, tiled=True)  211 us
    psum x1, waiting for transfers between devices, shards(): lax.psum((stacked_qkv_in, stacked_qkv_out, stacked_out_in, stacked_out_ou...  180 us
    dot_general x12, matrix products, product(): return jnp.dot(left_side, right_side, preferred_element_type=jnp.float32)  164 us
    dot_general x12, matrix products, product_transposed(): lax.dot_general(left_side, right_side, (((1,), (1,)), ((), ())), preferre...  149 us
    pallas_call x1, Pallas kernels, attend_backward(): pl.pallas_call(partial(attend_backward_kernel, tiles), grid_spec=pltpu.Pr...  107 us
    pallas_call x1, Pallas kernels, attend_forward(): pl.pallas_call(partial(attend_forward_kernel, tiles), grid_spec=pltpu.Pre...  56.3 us
  transfers between devices with their start and end apart: 7, of which 4 were waited for; matrix products, arithmetic and copies ran while one was open for 16% of the time, Pallas kernels for 3%

profile of v1, /device:TPU:0, one launch (start us, length us, event | category | flops | bytes accessed | tf_op | source)
XLA Modules:
  0.0 1663.0 jit_solution(6490105634514465227)
XLA Ops:
  18.0 35.9 %all-reduce.12 = (bf16[1600]{0:T(1024)(128)(2,1)S(1)}, bf16[1600]{0:T(1024)(128)(2,1)S(1)}, bf16[4800]{0:T(1024)(128)(2,1)S(1)}, bf16[1600]{0:T(1024)(128)(2,1)S...) all-reduce(bf16[1600]{0:T(1024)(128)(2,1)S(1)} %dynamic-update-slic, ...), channel_id=1, replica_groups=mesh['dp'=4,'ctx'=2,'wt'=4] {'wt'}, use_global_device_ids=true, to_apply=%add.4 | all-reduce | flops 20800 | bytes 83200
  60.7 9.1 fusion.66
  69.8 210.6 %all-gather.5.cloned.1.call-done = bf16[1600,4800]{1,0:T(8,128)(2,1)} async-done(((bf16[400,4800]{1,0:T(8,128)(2,1)}), bf16[1600,4800]{1,0:T(8,128)(2,1)}) %all-gather.5.cloned.1.call-update) | async-done | bytes 15360016 | tf_op jit(solution)/shard_map/all_gather | solution.py:264
  280.4 28.4 %add_convert_fusion.1 = bf16[1024,4800]{1,0:T(8,128)(2,1)} fusion(f32[1024,4800]{1,0:T(8,128)} %fusion.66, bf16[1600,4800]{1,0:T(8,128)(2,1)} %all-gather.5.cloned.1.call-done, f32[4800]{0:T(1024)S(1)} %convert_element_type.127, bf16[1,1024,1600]{1,2,0:T(8,128)(2,1)} %param.24, f32[1600]{0:T(1024)S(1)} %convert_element_type.125, ...), kind=kOutput, calls=%fused_computation.17 | convolution fusion | flops 15753216000 | bytes 48168192 | tf_op jit(solution)/shard_map/dot_general | solution.py:27
  327.9 11.7 fusion.55
  344.8 7.5 maximum_maximum_fusion
  357.6 56.3 %attend_forward.1 = (bf16[1024,1664]{1,0:T(8,128)(2,1)}, f32[13,2048,128]{2,1,0:T(8,128)}) custom-call(s32[4]{0:T(128)} %pad_add_fusion.meta, bf16[1024,1664]{1,0:T(8,128)(2,1)} %slice_select_fusion.q_ref, bf16[2048,1664]{1,0:T(8,128)(2,1)} %get-tuple-element.45.k_ref, bf16[2048,1664]{1,0:T(8,128)(2,1)} %get-tuple-element.44.v_ref), custom_call_target="tpu_custom_call" | custom-call | tf_op jit(solution)/shard_map/attend_forward/pallas_call | solution.py:136
  416.9 9.9 fusion.44
  435.6 10.7 fusion.59
  446.3 282.5 %all-gather.9.cloned.1.call-done = bf16[1600,6400]{1,0:T(8,128)(2,1)} async-done(((bf16[400,6400]{1,0:T(8,128)(2,1)}), bf16[1600,6400]{1,0:T(8,128)(2,1)}) %all-gather.9.cloned.1.call-update) | async-done | bytes 20480016 | tf_op jit(solution)/shard_map/all_gather | solution.py:270
  728.9 47.2 %multiply_convert_fusion = (bf16[1024,6400]{1,0:T(8,128)(2,1)}, f32[1024,6400]{1,0:T(8,128)}) fusion(f32[1024,6400]{1,0:T(8,128)} %fusion.59, f32[6400]{0:T(1024)S(1)} %convert_element_type.137, bf16[1024,1600]{0,1:T(8,128)(2,1)} %copy-done.13, bf16[1600,6400]{1,0:T(8,128)(2,1)} %all-gather.9.cloned.1.call-done), kind=kOutput, calls=%fused_computation.15 | convolution fusion | flops 21043609600 | bytes 89318400 | tf_op jit(solution)/shard_map/dot_general | solution.py:27
  776.0 315.1 %all-gather.11.cloned.1.call-done = bf16[6400,1600]{1,0:T(8,128)(2,1)} async-done(((bf16[1600,1600]{1,0:T(8,128)(2,1)}), bf16[6400,1600]{1,0:T(8,128)(2,1)}) %all-gather.11.cloned.1.call-update) | async-done | bytes 20480016 | tf_op jit(solution)/shard_map/all_gather | solution.py:272
  1091.2 48.8 %fusion.2 = bf16[1024,6400]{1,0:T(8,128)(2,1)} fusion(f32[1024,6400]{1,0:T(8,128)} %get-tuple-element.60, f32[1024,6400]{1,0:T(8,128)} %fusion.55, bf16[6400,1600]{1,0:T(8,128)(2,1)} %all-gather.11.cloned.1.call-done, bf16[1,1024,1600]{1,2,0:T(8,128)(2,1)} %param.25), kind=kOutput, calls=%fused_computation.6 | convolution fusion | flops 21122252800 | bytes 89292800 | tf_op jit(solution)/shard_map/dot_general | solution.py:31
  1139.9 8.2 convolution_convert_fusion.3
  1150.2 30.8 %fusion.118 = (f32[1024]{0:T(1024)S(1)}, f32[1024]{0:T(1024)S(1)}, f32[1024,1600]{0,1:T(8,128)}) fusion(f32[1024]{0:T(1024)S(1)} %add_rsqrt_fusion, f32[1024,1600]{0,1:T(8,128)} %copy-done.3, f32[1024]{0:T(1024)S(1)} %broadcast_multiply_fusion.12, f32[1600]{0:T(1024)S(1)} %convert_element_type.134, f32[1024,1600]{0,1:T(8,128)S(1)} %fusion.73, ...), kind=kOutput, calls=%fused_computation.165 | convolution fusion | flops 20982988800 | bytes 53270784 | tf_op jit(solution)/shard_map/dot_general | solution.py:31
  1181.0 8.5 multiply_add_fusion
  1194.3 8.1 fusion.111
  1215.3 107.4 %attend_backward.1 = (bf16[1024,1664]{1,0:T(8,128)(2,1)}, bf16[1024,1664]{1,0:T(8,128)(2,1)}, f32[1024,1664]{1,0:T(8,128)}, bf16[1024,1664]{1,0:T(8,128)(2,1)}, f32[1024,1664]{1,0:T(8,128)}) custom-call(s32[4]{0:T(128)} %pad_add_fusion.meta, bf16[1024,1664]{1,0:T(8,128)(2,1)} %slice_select_fusion.q_ref, bf16[2048,1664]{1,0:T(8,128)(2,1)} %get-tuple-element.45.k_ref, ...), custom_call_target="tpu_custom_call" | custom-call | tf_op jit(solution)/shard_map/attend_backward/pallas_call | solution.py:209
  1331.8 8.6 convolution_convert_fusion.4
  1365.5 17.0 %concatenate.11 = bf16[1024,4800]{1,0:T(8,128)(2,1)} concatenate(bf16[1024,1600]{1,0:T(8,128)(2,1)} %bitcast.174, bf16[1024,1600]{1,0:T(8,128)(2,1)} %fusion.18, bf16[1024,1600]{1,0:T(8,128)(2,1)} %fusion.17), dimensions={1} | concatenate | bytes 19660800 | tf_op jit(solution)/shard_map/concatenate | solution.py:403
  1396.4 31.8 %fusion.39 = bf16[1,1024,1600]{1,2,0:T(8,128)(2,1)} fusion(f32[1024,1600]{0,1:T(8,128)} %copy-done.3, f32[1024,1600]{0,1:T(8,128)} %fusion.71, f32[1600]{0:T(1024)S(1)} %convert_element_type.140, bf16[1024,6400]{1,0:T(8,128)(2,1)} %get-tuple-element.59, bf16[6400,1600]{1,0:T(8,128)(2,1)} %all-gather.11.cloned.1.call-done), kind=kOutput, calls=%fused_computation.70 | convolution fusion | flops 20978073600 | bytes 49977600 | tf_op jit(solution)/shard_map/dot_general | solution.py:27
  1430.2 24.5 %fusion.117 = (f32[1024]{0:T(1024)S(1)}, f32[1024]{0:T(1024)S(1)}, f32[1024,1600]{0,1:T(8,128)}) fusion(f32[1024]{0:T(1024)S(1)} %copy-done.33, f32[1024]{0:T(1024)S(1)} %copy-done.31, bf16[1,1024,1600]{1,2,0:T(8,128)(2,1)S(1)} %copy-done.7, f32[1600]{0:T(1024)S(1)} %copy-done.35, f32[1024,1600]{0,1:T(8,128)S(1)} %fusion.80, ...), kind=kOutput, calls=%fused_computation.164 | convolution fusion | flops 15741745152 | bytes 41597184 | tf_op jit(solution)/shard_map/dot_general | solution.py:31
  1454.8 8.8 fusion.25
  1463.6 180.0 %all-reduce.15.cloned.1.call-done = (f32[8,16,1600]{2,1,0:T(8,128)}, f32[8,16,4800]{2,1,0:T(8,128)}, f32[8,16,1600]{2,1,0:T(8,128)}, f32[8,16,1600]{2,1,0:T(8,12...) async-done(((f32[8,16,1600]{2,1,0:T(8,128)}, f32[8,16,4800]{2,1,0:T(8,128)}, f32[8,16,1600]{2,1,0:T(8,128)}, ...) | async-done | bytes 13107216 | tf_op jit(solution)/shard_map/psum | solution.py:431
  (240 shorter events, 138.4 us)
Async XLA Ops:
  7.2 428.4 %copy-start = (bf16[8,16,6400]{2,1,0:T(8,128)(2,1)S(1)}, bf16[8,16,6400]{2,1,0:T(8,128)(2,1)}, u32[]{:S(2)}) copy-start(bf16[8,16,6400]{2,1,0:T(8,128)(2,1)} %param.45) | copy-start | bytes 4915204
  7.2 273.2 %all-gather.5.cloned.1.call-start = ((), (), s32[]{:S(2)}) async-start(), calls=%async_computation | async-start | bytes 19456000 | tf_op jit(solution)/shard_map/all_gather | solution.py:264
  7.9 409.0 %all-gather.7.cloned.1.call-start = ((), (), s32[]{:S(2)}) async-start(), calls=%async_computation.1 | async-start | bytes 6656000 | tf_op jit(solution)/shard_map/all_gather | solution.py:266
  8.8 720.1 %all-gather.9.cloned.1.call-start = ((), (), s32[]{:S(2)}) async-start(), calls=%async_computation.2 | async-start | bytes 25600000 | tf_op jit(solution)/shard_map/all_gather | solution.py:270
  9.5 1081.6 %all-gather.11.cloned.1.call-start = ((), (), s32[]{:S(2)}) async-start(), calls=%async_computation.3 | async-start | bytes 26624000 | tf_op jit(solution)/shard_map/all_gather | solution.py:272
  10.1 1633.4 %all-reduce.15.cloned.1.call-start = ((), (), s32[]{:S(2)}) async-start(), calls=%async_computation.4 | async-start | bytes 26607616 | tf_op jit(solution)/shard_map/psum | solution.py:431
  53.9 226.5 %copy-start.36 = (f32[1600]{0:T(1024)}, f32[1600]{0:T(1024)S(1)}, u32[]{:S(2)}) copy-start(f32[1600]{0:T(1024)S(1)} %convert_element_type.125) | copy-start | bytes 19204
  53.9 226.5 %copy-start.34 = (f32[1600]{0:T(1024)}, f32[1600]{0:T(1024)S(1)}, u32[]{:S(2)}) copy-start(f32[1600]{0:T(1024)S(1)} %convert_element_type.124) | copy-start | bytes 19204
  53.9 226.4 %copy-start.30 = (f32[1024]{0:T(1024)}, f32[1024]{0:T(1024)S(1)}, u32[]{:S(2)}) copy-start(f32[1024]{0:T(1024)S(1)} %broadcast_multiply_fusion.13) | copy-start | bytes 12292
  56.8 223.5 %copy-start.32 = (f32[1024]{0:T(1024)}, f32[1024]{0:T(1024)S(1)}, u32[]{:S(2)}) copy-start(f32[1024]{0:T(1024)S(1)} %add_rsqrt_fusion.1) | copy-start | bytes 12292
  314.7 9.8 copy-start.48
  319.6 24.2 %collective-permute-start = (bf16[2,1024,1664]{2,1,0:T(8,128)(2,1)}, bf16[2,1024,1664]{2,1,0:T(8,128)(2,1)}, u32[]{:S(2)}, u32[]{:S(2)}) collective-permute-start(bf16[2,1024,1664]{2,1,0:T(8,128)(2,1)} %pad_maximum_fusion), channel_id=1, source_target_pairs={{0,4},{1,5},{2,6},{3,7},{8,12},{9,13},{10,14},{11,15},{16,20},{17,... | collective-permute-start | bytes 20447240 | tf_op jit(solution)/shard_map/ppermute | solution.py:23
  327.9 11.7 copy-start.22
  327.9 11.7 copy-start.41
  416.9 9.9 copy-start.28
  416.9 9.9 copy-start.5
  1148.1 32.8 %slice-start = ((s8[6553600]{0:T(1024)(128)(4,1)}), s8[4194304]{0:T(1024)(128)(4,1)S(1)}, s32[]{:S(2)}) async-start(s8[6553600]{0:T(1024)(128)(4,1)} %bitcast.160), calls=%async_computation.5 | async-start | bytes 8388608
  1150.2 30.8 %slice-start.1 = ((s8[6553600]{0:T(1024)(128)(4,1)}), s8[2359296]{0:T(1024)(128)(4,1)S(1)}, s32[]{:S(2)}) async-start(s8[6553600]{0:T(1024)(128)(4,1)} %bitcast.160), calls=%async_computation.6 | async-start | bytes 4718592
  1329.3 27.3 %collective-permute-start.1 = (bf16[2,1024,1664]{2,1,0:T(8,128)(2,1)}, bf16[2,1024,1664]{2,1,0:T(8,128)(2,1)}, u32[]{:S(2)}, u32[]{:S(2)}) collective-permute-start(bf16[2,1024,1664]{2,1,0:T(8,128)(2,1)} %pad_maximum_fusion.1), channel_id=1, source_target_pairs={{4,0},{5,1},{6,2},{7,3},{12,8},{13,9},{14,10},{15,11},{20,16},{21,... | collective-permute-start | bytes 20447240 | tf_op jit(solution)/shard_map/ppermute | solution.py:23
  1330.8 17.9 %slice-start.6 = ((s8[13107200]{0:T(1024)(128)(4,1)}), s8[4194304]{0:T(1024)(128)(4,1)S(1)}, s32[]{:S(2)}) async-start(s8[13107200]{0:T(1024)(128)(4,1)} %bitcast.166), calls=%async_computation.11 | async-start | bytes 8388608
  1331.8 9.6 copy-start.15
  1331.8 17.0 %slice-start.7 = ((s8[13107200]{0:T(1024)(128)(4,1)}), s8[4194304]{0:T(1024)(128)(4,1)S(1)}, s32[]{:S(2)}) async-start(s8[13107200]{0:T(1024)(128)(4,1)} %bitcast.166), calls=%async_computation.12 | async-start | bytes 8388608
  1428.2 26.6 %slice-start.4 = ((s8[6553600]{0:T(1024)(128)(4,1)}), s8[4194304]{0:T(1024)(128)(4,1)S(1)}, s32[]{:S(2)}) async-start(s8[6553600]{0:T(1024)(128)(4,1)} %bitcast.164), calls=%async_computation.9 | async-start | bytes 8388608
  1430.2 24.5 %slice-start.5 = ((s8[6553600]{0:T(1024)(128)(4,1)}), s8[2359296]{0:T(1024)(128)(4,1)S(1)}, s32[]{:S(2)}) async-start(s8[6553600]{0:T(1024)(128)(4,1)} %bitcast.164), calls=%async_computation.10 | async-start | bytes 4718592
  (51 other events, 273.5 us)
Sparse Core Ops, SparseCore 0:
  9.6 270.7 all-gather.4
  281.9 98.0 all-gather.6
  381.6 347.1 all-gather.8
  730.3 360.8 all-gather.10
  1396.5 247.0 all-reduce.14

commit v2 on v1

v2 whole, which is shorter than its diff:
```python
from functools import partial

import jax
import jax.numpy as jnp
from jax import lax
from jax.experimental import pallas as pl
from jax.experimental.pallas import tpu as pltpu
from jax.sharding import PartitionSpec as P

HEADS = 25
HEAD_DIM = 64
ADAPTERS = 8
WINDOW = 1024
RANK = 16
EPSILON = 1e-05
MASKED = -1e30

PAIRS = (HEADS + 1) // 2
PADDED = PAIRS * 128
FACTOR = HEAD_DIM ** (-0.5)
SHARDS = 4
PARTS = 8
BLOCK = 256
FF_CHUNK = 1280
VMEM_LIMIT = 60 << 20

def product(left_side, right_side):
    return lax.dot_general(left_side, right_side, (((1,), (0,)), ((), ())), preferred_element_type=jnp.float32)


def product_transposed(left_side, right_side):
    return lax.dot_general(left_side, right_side, (((1,), (1,)), ((), ())), preferred_element_type=jnp.float32)


def product_outer(left_side, right_side):
    return lax.dot_general(left_side, right_side, (((0,), (0,)), ((), ())), preferred_element_type=jnp.float32)


def norm_forward(values, norm_gain, norm_shift):
    center = values - jnp.mean(values, axis=-1, keepdims=True)
    inverse = lax.rsqrt(jnp.mean(center * center, axis=-1, keepdims=True) + EPSILON)
    normed = center * inverse
    return (normed * norm_gain + norm_shift, normed, inverse)


def norm_backward(upstream, normed, inverse, norm_gain):
    scaled = upstream * norm_gain
    return inverse * (
        scaled
        - jnp.mean(scaled, axis=-1, keepdims=True)
        - normed * jnp.mean(scaled * normed, axis=-1, keepdims=True)
    )


def copy_piece(source, target, row, columns, sem):
    start = pl.multiple_of(row, 16)
    pltpu.make_async_copy(source, target.at[pl.ds(start, source.shape[0]), columns], sem).start()


def start_shard(pieces, place, distance, target, source_columns, columns, sem):
    own, rest, parts = pieces[0], pieces[1], pieces[2:]
    base = place[distance] * own.shape[0]
    if distance == 0:
        copy_piece(own.at[:, source_columns], target, base, columns, sem)
        return
    part_rows = parts[0].shape[1]
    for source in range(PARTS):
        row = base + place[SHARDS + source] * part_rows
        copy_piece(parts[source].at[distance - 1, :, source_columns], target, row, columns, sem)
    row = base + PARTS * part_rows
    copy_piece(rest.at[distance - 1, :, source_columns], target, row, columns, sem)


def start_columns(pieces, place, target, source_columns, columns, sem):
    for distance in range(SHARDS):
        start_shard(pieces, place, distance, target, source_columns, columns, sem)


def wait_rows(target, start, rows, columns, sem):
    whole = target.at[pl.ds(start, rows), columns]
    pltpu.make_async_copy(whole, whole, sem).wait()


def widen(wide, low):
    rows = wide.shape[0]
    fill = jnp.zeros((rows, PADDED - wide.shape[1] - low.shape[1]), jnp.bfloat16)
    return jnp.concatenate([wide, low, fill], axis=1)


def blocks_of(rows):
    return [pl.ds(start, BLOCK) for start in range(0, rows, BLOCK)]


HBM = pl.BlockSpec(memory_space=pl.ANY)


def whole_of(array):
    shape = array.shape
    return pl.BlockSpec(shape, lambda *_: (0,) * len(shape))


def call(kernel, name, grid, place, inputs, pieces, in_specs, outs, out_specs, scratch):
    return pl.pallas_call(
        kernel,
        grid_spec=pltpu.PrefetchScalarGridSpec(
            num_scalar_prefetch=1,
            grid=grid,
            in_specs=in_specs + [HBM] * len(pieces),
            out_specs=out_specs,
            scratch_shapes=scratch,
        ),
        out_shape=outs,
        compiler_params=pltpu.CompilerParams(vmem_limit_bytes=VMEM_LIMIT),
        name=name,
    )(place, *inputs, *pieces)


def out_of(shape, kind):
    return jax.ShapeDtypeStruct(shape, kind)


def column_block(rows, width):
    return pl.BlockSpec((rows, width), lambda c, *_: (0, c))


def row_block(width):
    return pl.BlockSpec((BLOCK, width), lambda r, *_: (r, 0))


def qkv_kernel(place, x_ref, gain, shift, bias, a_in, a_out, *more):
    pieces, (first_ref, low_ref, q_ref, kv_ref, w, wide, sems) = more[:-7], more[-7:]
    rows, features = x_ref.shape
    step, steps = pl.program_id(0), pl.num_programs(0)
    width = w.shape[2]

    def fetch(c):
        columns = pl.ds(pl.multiple_of(c * width, 128), width)
        start_columns(pieces, place, w.at[c % 2], columns, pl.ds(0, width), sems.at[c % 2])

    @pl.when(step == 0)
    def _():
        fetch(0)
        for slot in range(2):
            w[slot, pl.ds(features + RANK, PADDED - features - RANK), :] = jnp.zeros(
                (PADDED - features - RANK, width), jnp.bfloat16
            )
        for block in blocks_of(rows):
            normed_in, _, _ = norm_forward(x_ref[block, :].astype(jnp.float32), gain[...], shift[...])
            first = normed_in.astype(jnp.bfloat16)
            low = product_transposed(first, a_in[...]).astype(jnp.bfloat16)
            first_ref[block, :] = first
            low_ref[block, :] = low
            wide[block, :] = widen(first, low)

    @pl.when(step + 1 < steps)
    def _():
        fetch(step + 1)

    slot = lax.rem(step, 2)
    wait_rows(w.at[slot], 0, features, pl.ds(0, width), sems.at[slot])
    w[slot, pl.ds(features, RANK), :] = a_out[...]
    for block in blocks_of(rows):
        part = (product(wide[block, :], w[slot]) + bias[...]).astype(jnp.bfloat16)

        @pl.when(step == 0)
        def _():
            q_ref[block, :] = part

        @pl.when(step > 0)
        def _():
            kv_ref[block, :] = part


def qkv_call(place, x, gain, shift, bias, a_in, a_out, pieces):
    rows, features = x.shape
    steps = 3
    width = PADDED
    return call(
        qkv_kernel, "qkv", (steps,), place, [x, gain, shift, bias, a_in, a_out], pieces,
        [whole_of(x), whole_of(gain), whole_of(shift), column_block(1, width), whole_of(a_in), column_block(RANK, width)],
        [out_of((rows, features), jnp.bfloat16), out_of((rows, RANK), jnp.bfloat16), out_of((rows, width), jnp.bfloat16), out_of((rows, 2 * width), jnp.bfloat16)],
        [whole_of(x), pl.BlockSpec((rows, RANK), lambda *_: (0, 0)), pl.BlockSpec((rows, width), lambda *_: (0, 0)),
         pl.BlockSpec((rows, width), lambda c, *_: (0, jnp.maximum(c - 1, 0)))],
        [pltpu.VMEM((2, PADDED, width), jnp.bfloat16), pltpu.VMEM((rows, PADDED), jnp.bfloat16), pltpu.SemaphoreType.DMA((2,))],
    )


def out_kernel(place, x_ref, mixed_ref, gain, shift, bias, a_in, a_out, u_in, *more):
    pieces, (hidden_ref, second_ref, low_ref, up_low_ref, w, sem) = more[:-6], more[-6:]
    features = x_ref.shape[1]

    @pl.when(pl.program_id(0) == 0)
    def _():
        start_columns(pieces, place, w, pl.ds(0, features), pl.ds(0, features), sem)
        w[pl.ds(features, RANK), :] = a_out[...]
        w[pl.ds(features + RANK, PADDED - features - RANK), :] = jnp.zeros(
            (PADDED - features - RANK, features), jnp.bfloat16
        )
        wait_rows(w, 0, features, pl.ds(0, features), sem)

    mixed = mixed_ref[:, :features]
    low = product_transposed(mixed, a_in[...]).astype(jnp.bfloat16)
    hidden = x_ref[...].astype(jnp.float32) + (product(widen(mixed, low), w[...]) + bias[...])
    normed_mid, _, _ = norm_forward(hidden, gain[...], shift[...])
    second = normed_mid.astype(jnp.bfloat16)
    hidden_ref[...] = hidden
    second_ref[...] = second
    low_ref[...] = low
    up_low_ref[...] = product_transposed(second, u_in[...]).astype(jnp.bfloat16)


def out_call(place, x, mixed, gain, shift, bias, a_in, a_out, u_in, pieces):
    rows, features = x.shape
    return call(
        out_kernel, "out", (rows // BLOCK,), place, [x, mixed, gain, shift, bias, a_in, a_out, u_in], pieces,
        [row_block(features), row_block(PADDED)] + [whole_of(a) for a in (gain, shift, bias, a_in, a_out, u_in)],
        [out_of((rows, features), jnp.float32), out_of((rows, features), jnp.bfloat16), out_of((rows, RANK), jnp.bfloat16), out_of((rows, RANK), jnp.bfloat16)],
        [row_block(features), row_block(features), row_block(RANK), row_block(RANK)],
        [pltpu.VMEM((PADDED, features), jnp.bfloat16), pltpu.SemaphoreType.DMA(())],
    )


def fetch_down(pieces, place, w, sems):
    width = w.shape[1]
    for distance in range(SHARDS):
        start_shard(pieces, place, distance, w, pl.ds(0, width), pl.ds(0, width), sems.at[place[distance]])


def wait_down(step, w, sems):
    shard_rows = w.shape[0] // SHARDS
    for shard in range(SHARDS):
        first_step = max(0, -(-(shard * shard_rows - FF_CHUNK + 1) // FF_CHUNK))

        @pl.when(step == first_step)
        def _():
            wait_rows(w, shard * shard_rows, shard_rows, pl.ds(0, w.shape[1]), sems.at[shard])


def active_grad_kernel(place, cot_ref, a_in, a_out, *more):
    pieces, (g_ref, low_ref, w, sems) = more[:-4], more[-4:]
    rows, features = cot_ref.shape
    step = pl.program_id(0)

    @pl.when(step == 0)
    def _():
        fetch_down(pieces, place, w, sems)
        for block in blocks_of(rows):
            low_ref[block, :] = product_transposed(cot_ref[block, :], a_out[...]).astype(jnp.bfloat16)

    wait_down(step, w, sems)
    weight = w[pl.ds(pl.multiple_of(step * FF_CHUNK, FF_CHUNK), FF_CHUNK), :]
    for block in blocks_of(rows):
        g_ref[block, :] = (
            product_transposed(cot_ref[block, :], weight) + product(low_ref[block, :], a_in[...])
        ).astype(jnp.bfloat16)


def active_grad_call(place, cot, a_in, a_out, pieces):
    rows, features = cot.shape
    units = a_in.shape[1]
    return call(
        active_grad_kernel, "active_grad", (units // FF_CHUNK,), place, [cot, a_in, a_out], pieces,
        [whole_of(cot), column_block(RANK, FF_CHUNK), whole_of(a_out)],
        [out_of((rows, units), jnp.bfloat16), out_of((rows, RANK), jnp.bfloat16)],
        [column_block(rows, FF_CHUNK), pl.BlockSpec((rows, RANK), lambda *_: (0, 0))],
        [pltpu.VMEM((units, features), jnp.bfloat16), pltpu.SemaphoreType.DMA((SHARDS,))],
    )


GELU_A = 0.7978845608
GELU_B = 0.044715


def up_kernel(place, second_ref, up_low_ref, g_active_ref, g_low_ref, bias, u_out, d_in, *more):
    pieces, (active_ref, acc_ref, down_low_ref, g_up_out_ref, g_down_in_ref, w, wide, low_scr, sems) = more[:-9], more[-9:]
    rows, features = second_ref.shape
    step, steps = pl.program_id(0), pl.num_programs(0)
    width = w.shape[2]

    def fetch(c):
        columns = pl.ds(pl.multiple_of(c * width, 128), width)
        start_columns(pieces, place, w.at[c % 2], columns, pl.ds(0, width), sems.at[c % 2])

    @pl.when(step == 0)
    def _():
        fetch(0)
        for slot in range(2):
            w[slot, pl.ds(features + RANK, PADDED - features - RANK), :] = jnp.zeros(
                (PADDED - features - RANK, width), jnp.bfloat16
            )
        for block in blocks_of(rows):
            wide[block, :] = widen(second_ref[block, :], up_low_ref[block, :])

    @pl.when(step + 1 < steps)
    def _():
        fetch(step + 1)

    slot = lax.rem(step, 2)
    wait_rows(w.at[slot], 0, features, pl.ds(0, width), sems.at[slot])
    w[slot, pl.ds(features, RANK), :] = u_out[...]
    up_out_sum, down_in_sum = None, None
    for block in blocks_of(rows):
        upper = product(wide[block, :], w[slot]) + bias[...]
        square = upper * upper
        inner = jnp.tanh((GELU_A * upper) * (1.0 + GELU_B * square))
        half = 0.5 * (1.0 + inner)
        active = (upper * half).astype(jnp.bfloat16)
        slope = half + (0.5 * GELU_A) * upper * (1.0 - inner * inner) * (1.0 + (3.0 * GELU_B) * square)
        g_upper = (g_active_ref[block, :].astype(jnp.float32) * slope).astype(jnp.bfloat16)
        active_ref[block, :] = active
        acc = product_transposed(g_upper, w[slot])
        low = product_transposed(active, d_in[...])

        @pl.when(step == 0)
        def _():
            acc_ref[block, :] = acc
            low_scr[block, :] = low

        @pl.when(step > 0)
        def _():
            acc_ref[block, :] += acc
            low_scr[block, :] += low

        up_out = product_outer(up_low_ref[block, :], g_upper)
        down_in = product_outer(g_low_ref[block, :], active)
        up_out_sum = up_out if up_out_sum is None else up_out_sum + up_out
        down_in_sum = down_in if down_in_sum is None else down_in_sum + down_in
    g_up_out_ref[...] = up_out_sum
    g_down_in_ref[...] = down_in_sum

    @pl.when(step == steps - 1)
    def _():
        down_low_ref[...] = low_scr[...].astype(jnp.bfloat16)


def up_call(place, second, up_low, g_active, g_low, bias, u_out, d_in, pieces):
    rows, features = second.shape
    units = bias.shape[1]
    low_block = pl.BlockSpec((rows, RANK), lambda *_: (0, 0))
    return call(
        up_kernel, "up", (units // FF_CHUNK,), place, [second, up_low, g_active, g_low, bias, u_out, d_in], pieces,
        [whole_of(second), low_block, column_block(rows, FF_CHUNK), low_block,
         column_block(1, FF_CHUNK), column_block(RANK, FF_CHUNK), column_block(RANK, FF_CHUNK)],
        [out_of((rows, units), jnp.bfloat16), out_of((rows, PADDED), jnp.float32), out_of((rows, RANK), jnp.bfloat16),
         out_of((RANK, units), jnp.float32), out_of((RANK, units), jnp.float32)],
        [column_block(rows, FF_CHUNK), pl.BlockSpec((rows, PADDED), lambda *_: (0, 0)), low_block,
         column_block(RANK, FF_CHUNK), column_block(RANK, FF_CHUNK)],
        [pltpu.VMEM((2, PADDED, FF_CHUNK), jnp.bfloat16), pltpu.VMEM((rows, PADDED), jnp.bfloat16), pltpu.VMEM((rows, RANK), jnp.float32),
         pltpu.SemaphoreType.DMA((2,))],
    )


def out_grad_kernel(place, acc_ref, hidden_ref, second_ref, cot_ref, mixed_ref, low_ref, down_low_ref, gain, u_in, a_in, a_out, *more):
    pieces, (g_hidden_ref, g_mixed_ref, g_up_in, g_out_out, g_out_in, g_down_out, w, sem) = more[:-8], more[-8:]
    features = hidden_ref.shape[1]
    step = pl.program_id(0)

    @pl.when(step == 0)
    def _():
        start_columns(pieces, place, w, pl.ds(0, features), pl.ds(0, features), sem)
        w[pl.ds(features, RANK), :] = a_out[...]
        w[pl.ds(features + RANK, PADDED - features - RANK), :] = jnp.zeros(
            (PADDED - features - RANK, features), jnp.bfloat16
        )

    g_up_low = acc_ref[:, features : features + RANK].astype(jnp.bfloat16)
    g_second = acc_ref[:, :features] + product(g_up_low, u_in[...])
    _, normed, inverse = norm_forward(hidden_ref[...], gain[...], 0.0)
    cot = cot_ref[...]
    g_hidden = cot.astype(jnp.float32) + norm_backward(g_second, normed, inverse, gain[...])
    g_branch = g_hidden.astype(jnp.bfloat16)
    g_hidden_ref[...] = g_hidden

    @pl.when(step == 0)
    def _():
        wait_rows(w, 0, features, pl.ds(0, features), sem)

    back = product_transposed(g_branch, w[...])
    g_low = back[:, features : features + RANK].astype(jnp.bfloat16)
    g_mixed = back[:, :features] + product(g_low, a_in[...])
    g_mixed_ref[:, :features] = g_mixed.astype(jnp.bfloat16)
    g_mixed_ref[:, features:] = jnp.zeros((BLOCK, PADDED - features), jnp.bfloat16)
    sums = (
        product_outer(g_up_low, second_ref[...]),
        product_outer(low_ref[...], g_branch),
        product_outer(g_low, mixed_ref[:, :features]),
        product_outer(down_low_ref[...], cot),
    )
    for total, term in zip((g_up_in, g_out_out, g_out_in, g_down_out), sums):
        @pl.when(step == 0)
        def _():
            total[...] = term

        @pl.when(step > 0)
        def _():
            total[...] += term


def out_grad_call(place, acc, hidden, second, cot, mixed, low, down_low, gain, u_in, a_in, a_out, pieces):
    rows, features = hidden.shape
    small = pl.BlockSpec((RANK, features), lambda *_: (0, 0))
    return call(
        out_grad_kernel, "out_grad", (rows // BLOCK,), place,
        [acc, hidden, second, cot, mixed, low, down_low, gain, u_in, a_in, a_out], pieces,
        [row_block(PADDED), row_block(features), row_block(features), row_block(features), row_block(PADDED),
         row_block(RANK), row_block(RANK)] + [whole_of(a) for a in (gain, u_in, a_in, a_out)],
        [out_of((rows, features), jnp.float32), out_of((rows, PADDED), jnp.bfloat16)] + [out_of((RANK, features), jnp.float32)] * 4,
        [row_block(features), row_block(PADDED)] + [small] * 4,
        [pltpu.VMEM((PADDED, features), jnp.bfloat16), pltpu.SemaphoreType.DMA(())],
    )


def down_kernel(place, active_ref, hidden_ref, down_low_ref, bias, a_out, *more):
    pieces, (out_ref, w, acc, sems) = more[:-4], more[-4:]
    rows, features = hidden_ref.shape
    step, steps = pl.program_id(0), pl.num_programs(0)

    @pl.when(step == 0)
    def _():
        fetch_down(pieces, place, w, sems)
        for block in blocks_of(rows):
            acc[block, :] = product(down_low_ref[block, :], a_out[...]) + bias[...]

    wait_down(step, w, sems)
    weight = w[pl.ds(pl.multiple_of(step * FF_CHUNK, FF_CHUNK), FF_CHUNK), :]
    for block in blocks_of(rows):
        acc[block, :] += product(active_ref[block, :], weight)

    @pl.when(step == steps - 1)
    def _():
        for block in blocks_of(rows):
            out_ref[block, :] = (hidden_ref[block, :] + acc[block, :]).astype(jnp.bfloat16)


def down_call(place, active, hidden, down_low, bias, a_out, pieces):
    rows, features = hidden.shape
    units = active.shape[1]
    return call(
        down_kernel, "down", (units // FF_CHUNK,), place, [active, hidden, down_low, bias, a_out], pieces,
        [column_block(rows, FF_CHUNK), whole_of(hidden), pl.BlockSpec((rows, RANK), lambda *_: (0, 0)),
         whole_of(bias), whole_of(a_out)],
        out_of((rows, features), jnp.bfloat16),
        pl.BlockSpec((rows, features), lambda *_: (0, 0)),
        [pltpu.VMEM((units, features), jnp.bfloat16), pltpu.VMEM((rows, features), jnp.float32), pltpu.SemaphoreType.DMA((SHARDS,))],
    )


def tokens_grad_kernel(place, x_ref, first_ref, low_ref, g_hidden_ref, gain, a_in, a_out, near_ref, far_ref, *more):
    pieces, (out_ref, g_qkv_out, g_qkv_in, w, acc, sems) = more[:-6], more[-6:]
    rows, features = x_ref.shape
    step, steps = pl.program_id(0), pl.num_programs(0)
    width = w.shape[2]

    def fetch(c):
        columns = pl.ds(pl.multiple_of(c * width, 128), width)
        start_columns(pieces, place, w.at[c % 2], columns, pl.ds(0, width), sems.at[c % 2])

    @pl.when(step == 0)
    def _():
        fetch(0)
        for slot in range(2):
            w[slot, pl.ds(features + RANK, PADDED - features - RANK), :] = jnp.zeros(
                (PADDED - features - RANK, width), jnp.bfloat16
            )

    @pl.when(step + 1 < steps)
    def _():
        fetch(step + 1)

    slot = lax.rem(step, 2)
    wait_rows(w.at[slot], 0, features, pl.ds(0, width), sems.at[slot])
    w[slot, pl.ds(features, RANK), :] = a_out[...]
    qkv_out_sum = None
    for block in blocks_of(rows):
        far = jnp.where(step > 0, far_ref[block, :].astype(jnp.float32), 0.0)
        g = (near_ref[block, :].astype(jnp.float32) + far).astype(jnp.bfloat16)
        back = product_transposed(g, w[slot])

        @pl.when(step == 0)
        def _():
            acc[block, :] = back

        @pl.when(step > 0)
        def _():
            acc[block, :] += back

        term = product_outer(low_ref[block, :], g)
        qkv_out_sum = term if qkv_out_sum is None else qkv_out_sum + term
    g_qkv_out[...] = qkv_out_sum

    @pl.when(step == steps - 1)
    def _():
        qkv_in_sum = None
        for block in blocks_of(rows):
            g_low = acc[block, pl.ds(features, RANK)].astype(jnp.bfloat16)
            g_first = acc[block, pl.ds(0, features)] + product(g_low, a_in[...])
            _, normed, inverse = norm_forward(x_ref[block, :].astype(jnp.float32), gain[...], 0.0)
            out_ref[block, :] = g_hidden_ref[block, :] + norm_backward(g_first, normed, inverse, gain[...])
            term = product_outer(g_low, first_ref[block, :])
            qkv_in_sum = term if qkv_in_sum is None else qkv_in_sum + term
        g_qkv_in[...] = qkv_in_sum


def tokens_grad_call(place, x, first, low, g_hidden, gain, a_in, a_out, near, far, pieces):
    rows, features = x.shape
    steps = 3
    near_block = pl.BlockSpec((None, rows, PADDED), lambda c, *_: (c, 0, 0))
    far_block = pl.BlockSpec((None, rows, PADDED), lambda c, *_: (jnp.maximum(c - 1, 0), 0, 0))
    return call(
        tokens_grad_kernel, "tokens_grad", (steps,), place, [x, first, low, g_hidden, gain, a_in, a_out, near, far], pieces,
        [whole_of(x), whole_of(first), whole_of(low), whole_of(g_hidden), whole_of(gain), whole_of(a_in),
         column_block(RANK, PADDED), near_block, far_block],
        [out_of((rows, features), jnp.float32), out_of((RANK, steps * PADDED), jnp.float32), out_of((RANK, features), jnp.float32)],
        [pl.BlockSpec((rows, features), lambda *_: (0, 0)), column_block(RANK, PADDED),
         pl.BlockSpec((RANK, features), lambda *_: (0, 0))],
        [pltpu.VMEM((2, PADDED, PADDED), jnp.bfloat16), pltpu.VMEM((rows, PADDED), jnp.float32), pltpu.SemaphoreType.DMA((2,))],
    )


TILE = 256
REACH_TILES = WINDOW // TILE
SPAN_TILES = REACH_TILES + 1


def split_pair(pair):
    lane = lax.broadcasted_iota(jnp.int32, pair.shape, 1)
    zero = jnp.zeros_like(pair)
    return jnp.concatenate(
        [jnp.where(lane < HEAD_DIM, pair, zero), jnp.where(lane >= HEAD_DIM, pair, zero)], axis=0
    )


def join_pair(stacked):
    lane = lax.broadcasted_iota(jnp.int32, (TILE, 128), 1)
    return jnp.where(lane < HEAD_DIM, stacked[:TILE], stacked[TILE:])


def tile_bias(bounds, query_start, key_start):
    rows = query_start + lax.broadcasted_iota(jnp.int32, (TILE, 1), 0)
    columns = key_start + lax.broadcasted_iota(jnp.int32, (1, TILE), 1)
    row_doc = sum((rows >= bound).astype(jnp.int32) for bound in bounds)
    column_doc = sum((columns >= bound).astype(jnp.int32) for bound in bounds)
    shape = (TILE, TILE)
    distance = jnp.broadcast_to(rows, shape) - jnp.broadcast_to(columns, shape)
    same = jnp.broadcast_to(row_doc, shape) == jnp.broadcast_to(column_doc, shape)
    seen = jnp.broadcast_to(columns, shape) >= 0
    return jnp.where(same & seen & (distance >= 0) & (distance < WINDOW), 0.0, MASKED)


def fill_biases(meta, bias_scr, tiles):
    bounds = [meta[place] for place in range(3)]
    first = meta[3]

    def one(step, carry):
        tile = step // SPAN_TILES
        key_tile = tile + lax.rem(step, SPAN_TILES) - REACH_TILES
        bias_scr[step] = tile_bias(bounds, first + tile * TILE, first + key_tile * TILE)
        return carry

    lax.fori_loop(0, tiles * SPAN_TILES, one, 0)


def key_tile(far_ref, near_ref, tile):
    if tile < REACH_TILES:
        return far_ref[pl.ds(tile * TILE, TILE), :]
    return near_ref[pl.ds((tile - REACH_TILES) * TILE, TILE), :]


def attend_forward_kernel(tiles, meta, q_ref, k_far, v_far, k_near, v_near, o_ref, lse_ref, bias_scr, acc_scr):
    @pl.when(pl.program_id(0) == 0)
    def _():
        fill_biases(meta, bias_scr, tiles)

    ones = jnp.ones((TILE, 128), jnp.bfloat16)
    chunk = TILE // 2
    for tile in range(tiles):
        stacked = split_pair(q_ref[pl.ds(tile * TILE, TILE), :] * FACTOR)
        span = range(tile, tile + SPAN_TILES)
        keys = jnp.concatenate([key_tile(k_far, k_near, t) for t in span], axis=0)
        values = jnp.concatenate(
            [jnp.concatenate([key_tile(v_far, v_near, t), ones], axis=1) for t in span], axis=0
        )
        for part in range(2 * TILE // chunk):
            start = part * chunk
            bias_rows = pl.ds(start % TILE, chunk)
            bias = jnp.concatenate(
                [bias_scr[tile * SPAN_TILES + t, bias_rows, :] for t in range(SPAN_TILES)], axis=1
            )
            scores = product_transposed(stacked[start : start + chunk], keys) + bias
            highest = jnp.max(scores, axis=1, keepdims=True)
            mixed = product(jnp.exp(scores - highest).astype(jnp.bfloat16), values)
            summed = mixed[:, 128:]
            acc_scr[pl.ds(start, chunk), :] = mixed[:, :128] / summed
            lse_ref[pl.ds(tile * 2 * TILE + start, chunk), :] = highest + jnp.log(summed)
        o_ref[pl.ds(tile * TILE, TILE), :] = join_pair(acc_scr[...]).astype(jnp.bfloat16)


def pair_columns(rows, offset=0):
    return pl.BlockSpec((rows, 128), lambda j, *_: (0, offset + j))


def attend_forward(meta, queries, far, near):
    rows = queries.shape[0]
    tiles = rows // TILE
    return pl.pallas_call(
        partial(attend_forward_kernel, tiles),
        grid_spec=pltpu.PrefetchScalarGridSpec(
            num_scalar_prefetch=1,
            grid=(PAIRS,),
            in_specs=[
                pair_columns(rows), pair_columns(WINDOW), pair_columns(WINDOW, PAIRS),
                pair_columns(rows), pair_columns(rows, PAIRS),
            ],
            out_specs=[pair_columns(rows), pl.BlockSpec((None, 2 * rows, 128), lambda j, *_: (j, 0, 0))],
            scratch_shapes=[
                pltpu.VMEM((tiles * SPAN_TILES, TILE, TILE), jnp.float32),
                pltpu.VMEM((2 * TILE, 128), jnp.float32),
            ],
        ),
        out_shape=[
            jax.ShapeDtypeStruct((rows, PADDED), jnp.bfloat16),
            jax.ShapeDtypeStruct((PAIRS, 2 * rows, 128), jnp.float32),
        ],
        compiler_params=pltpu.CompilerParams(vmem_limit_bytes=VMEM_LIMIT),
        name="attend_forward",
    )(meta, queries, far, far, near, near)


def attend_backward_kernel(
    tiles, meta, q_ref, k_far, v_far, k_near, v_near, g_ref, o_ref, lse_ref,
    near_ref, far_ref, bias_scr, dq_scr, dkt, dvt,
):
    @pl.when(pl.program_id(0) == 0)
    def _():
        fill_biases(meta, bias_scr, tiles)

    dkt[...] = jnp.zeros_like(dkt)
    dvt[...] = jnp.zeros_like(dvt)
    for tile in range(tiles):
        rows = pl.ds(tile * TILE, TILE)
        queries = split_pair(q_ref[rows, :] * FACTOR)
        grads = split_pair(g_ref[rows, :])
        mixed = o_ref[rows, :].astype(jnp.float32)
        centered = jnp.sum(
            grads.astype(jnp.float32) * jnp.concatenate([mixed, mixed], axis=0), axis=1, keepdims=True
        )
        lse = lse_ref[pl.ds(tile * 2 * TILE, 2 * TILE), :]
        lse = jnp.concatenate([lse, lse], axis=1)
        queries_t = queries.T
        grads_t = grads.T
        dq_scr[...] = jnp.zeros_like(dq_scr)
        for t in range(SPAN_TILES):
            keys = key_tile(k_far, k_near, tile + t)
            bias = bias_scr[tile * SPAN_TILES + t]
            scores = product_transposed(queries, keys)
            chances = jnp.exp(scores + jnp.concatenate([bias, bias], axis=0) - lse)
            grad_chances = product_transposed(grads, key_tile(v_far, v_near, tile + t))
            grad_scores = (chances * (grad_chances - centered)).astype(jnp.bfloat16)
            dvt[tile + t] += product(grads_t, chances.astype(jnp.bfloat16))
            dkt[tile + t] += product(queries_t, grad_scores)
            dq_scr[...] += product(grad_scores, keys)
        near_ref[0, rows, :] = (join_pair(dq_scr[...]) * FACTOR).astype(jnp.bfloat16)
    for t in range(tiles + REACH_TILES):
        target, first = (far_ref, 0) if t < REACH_TILES else (near_ref, 1)
        rows = pl.ds((t if t < REACH_TILES else t - REACH_TILES) * TILE, TILE)
        target[first, rows, :] = dkt[t].T.astype(jnp.bfloat16)
        target[first + 1, rows, :] = dvt[t].T.astype(jnp.bfloat16)


def attend_backward(meta, queries, far, near, grad_mixed, mixed, lse):
    rows = queries.shape[0]
    tiles = rows // TILE
    return pl.pallas_call(
        partial(attend_backward_kernel, tiles),
        grid_spec=pltpu.PrefetchScalarGridSpec(
            num_scalar_prefetch=1,
            grid=(PAIRS,),
            in_specs=[
                pair_columns(rows), pair_columns(WINDOW), pair_columns(WINDOW, PAIRS),
                pair_columns(rows), pair_columns(rows, PAIRS), pair_columns(rows), pair_columns(rows),
                pl.BlockSpec((None, 2 * rows, 128), lambda j, *_: (j, 0, 0)),
            ],
            out_specs=[
                pl.BlockSpec((3, rows, 128), lambda j, *_: (0, 0, j)),
                pl.BlockSpec((2, WINDOW, 128), lambda j, *_: (0, 0, j)),
            ],
            scratch_shapes=[
                pltpu.VMEM((tiles * SPAN_TILES, TILE, TILE), jnp.float32),
                pltpu.VMEM((2 * TILE, 128), jnp.float32),
                pltpu.VMEM((tiles + REACH_TILES, 128, TILE), jnp.float32),
                pltpu.VMEM((tiles + REACH_TILES, 128, TILE), jnp.float32),
            ],
        ),
        out_shape=[
            jax.ShapeDtypeStruct((3, rows, PADDED), jnp.bfloat16),
            jax.ShapeDtypeStruct((2, WINDOW, PADDED), jnp.bfloat16),
        ],
        compiler_params=pltpu.CompilerParams(vmem_limit_bytes=VMEM_LIMIT),
        name="attend_backward",
    )(meta, queries, far, far, near, near, grad_mixed, mixed, lse)


def ring_pairs(size):
    return [(i, (i + 1) % size) for i in range(size)]


def plane_pairs(sizes):
    first, second = [], []
    cores = sizes["ctx"]
    for chip in range(sizes["dp"]):
        for core in range(cores):
            steps = (chip ^ 1, chip ^ 2) if core % 2 == 0 else (chip ^ 2, chip ^ 1)
            here = chip * cores + core
            first.append((here, steps[0] * cores + core))
            second.append((here, steps[1] * cores + core))
    return first, second


def swap_pairs(size):
    return [(i, i ^ 1) for i in range(size)]


def shifted(array, size, by):
    pairs = [(i, i + by) for i in range(size) if 0 <= i + by < size]
    return lax.ppermute(array, "ctx", pairs)


def place_of():
    chip, core, shard = lax.axis_index("dp"), lax.axis_index("ctx") % 2, lax.axis_index("wt")
    places = [(shard - distance) % SHARDS for distance in range(SHARDS)]
    for side in (core, 1 - core):
        near = jnp.where(side == 0, chip ^ 1, chip ^ 2)
        for where in (chip, near, near ^ 3, chip ^ 3):
            places.append(where * 2 + side)
    return jnp.stack(places).astype(jnp.int32)


def gather_shards(sizes, own, extra):
    rows = own.shape[0] // (PARTS * 16) * 16
    index = lax.axis_index("dp") * 2 + lax.axis_index("ctx") % 2
    moved = lax.dynamic_slice_in_dim(own, index * rows, rows, 0)
    moved = jnp.concatenate([moved, own[PARTS * rows :]] + extra, axis=0)
    steps = []
    for _ in range(SHARDS - 1):
        moved = lax.ppermute(moved, "wt", ring_pairs(sizes["wt"]))
        steps.append(moved)
    return rows, steps


def spread_parts(sizes, own, rows, steps):
    first, second = plane_pairs(sizes)
    swap = swap_pairs(sizes["ctx"])
    mine = jnp.stack([step[:rows] for step in steps])
    one = lax.ppermute(mine, ("dp", "ctx"), first)
    two = lax.ppermute(mine, ("dp", "ctx"), second)
    both = lax.ppermute(one, ("dp", "ctx"), second)
    parts = [mine, one, two, both]
    parts += [lax.ppermute(part, "ctx", swap) for part in parts]
    left = own.shape[0] - PARTS * rows
    rest = jnp.stack([step[rows : rows + left] for step in steps])
    return [own, rest, *parts]


def pad_thirds(array, features):
    pieces = []
    for third in range(3):
        piece = array[..., third * features : (third + 1) * features]
        pieces.append(jnp.pad(piece, [(0, 0)] * (array.ndim - 1) + [(0, PADDED - features)]))
    return jnp.concatenate(pieces, axis=-1)


def summed_adapters(sizes, terms, chosen):
    widths = [term.shape[1] for term in terms]
    flat = jnp.concatenate(terms, axis=1)
    if sizes["ctx"] == 2:
        flat = flat + lax.ppermute(flat, "ctx", swap_pairs(2))
    else:
        flat = lax.psum(flat, "ctx")
    ids = jnp.broadcast_to(chosen.astype(jnp.bfloat16), (RANK, 128))
    sent = jnp.concatenate([flat.astype(jnp.bfloat16), ids], axis=1)
    everyone = lax.all_gather(sent, ("dp", "wt"), axis=0)
    numbers = everyone[:, 0, sum(widths)].astype(jnp.int32)
    selector = (jnp.arange(ADAPTERS, dtype=jnp.int32)[:, None] == numbers[None, :]).astype(jnp.bfloat16)
    totals, start = [], 0
    for width in widths:
        part = everyone[:, :, start : start + width]
        totals.append(jnp.einsum("as,srn->arn", selector, part, preferred_element_type=jnp.float32))
        start += width
    return totals


def shards(
    sizes,
    tokens,
    cotangent,
    doc_lengths,
    adapter_ids,
    first_gain,
    first_shift,
    qkv_weight,
    qkv_bias,
    out_weight,
    out_bias,
    second_gain,
    second_shift,
    up_weight,
    up_bias,
    down_weight,
    down_bias,
    qkv_adapt_in,
    qkv_adapt_out,
    out_adapt_in,
    out_adapt_out,
    up_adapt_in,
    up_adapt_out,
    down_adapt_in,
    down_adapt_out,
):
    values, upstream = tokens[0], cotangent[0]
    row_count, feature_count = values.shape
    ctx = sizes["ctx"]
    place = place_of()

    vectors = [first_gain, first_shift, qkv_bias, out_bias, second_gain, second_shift, up_bias, down_bias]
    lengths = [vector.shape[0] for vector in vectors]
    own_qkv = pad_thirds(qkv_weight, feature_count)
    flat = jnp.concatenate(vectors)
    extra_rows = 16
    flat = jnp.pad(flat, (0, extra_rows * own_qkv.shape[1] - flat.shape[0])).reshape(extra_rows, -1)

    rows_qkv, steps_qkv = gather_shards(sizes, own_qkv, [flat])
    pieces_qkv = spread_parts(sizes, own_qkv, rows_qkv, steps_qkv)
    later = lax.optimization_barrier((out_weight, down_weight, up_weight, steps_qkv[-1]))
    out_own, down_own, up_own = later[:3]
    gathered = [gather_shards(sizes, out_own, [])]
    down_own, _ = lax.optimization_barrier((down_own, gathered[-1][1][-1]))
    gathered.append(gather_shards(sizes, down_own, []))
    up_own, _ = lax.optimization_barrier((up_own, gathered[-1][1][-1]))
    gathered.append(gather_shards(sizes, up_own, []))
    pieces_out = spread_parts(sizes, out_own, *gathered[0])
    pieces_down = spread_parts(sizes, down_own, *gathered[1])
    pieces_up = spread_parts(sizes, up_own, *gathered[2])

    extra_start = own_qkv.shape[0] - (PARTS - 1) * rows_qkv
    by_distance = jnp.stack([flat] + [step[extra_start:] for step in steps_qkv])
    order = (lax.axis_index("wt") - jnp.arange(SHARDS)) % SHARDS
    by_shard = jnp.take(by_distance, order, axis=0).reshape(SHARDS, -1).astype(jnp.float32)
    vectors, start = [], 0
    for length in lengths:
        vectors.append(by_shard[:, start : start + length].reshape(1, -1))
        start += length
    gain_one, shift_one, bias_qkv, bias_out, gain_two, shift_two, bias_up, bias_down = vectors
    bias_qkv = pad_thirds(bias_qkv, feature_count)

    chosen = adapter_ids[0, 0]

    def select(stacked):
        return lax.dynamic_index_in_dim(stacked, chosen, 0, keepdims=False)

    adapter_qkv_in = select(qkv_adapt_in)
    adapter_qkv_out = pad_thirds(select(qkv_adapt_out), feature_count)
    adapter_out_in = select(out_adapt_in)
    adapter_out_out = select(out_adapt_out)
    adapter_up_in = select(up_adapt_in)
    adapter_up_out = select(up_adapt_out)
    adapter_down_in = select(down_adapt_in)
    adapter_down_out = select(down_adapt_out)

    first_query = lax.axis_index("ctx") * row_count
    meta = jnp.concatenate([jnp.cumsum(doc_lengths[0])[:3], first_query[None]]).astype(jnp.int32)
    reach = -(-WINDOW // row_count)

    first_in, qkv_low, queries, near = qkv_call(
        place, values, gain_one, shift_one, bias_qkv, adapter_qkv_in, adapter_qkv_out, pieces_qkv
    )
    far = jnp.concatenate([shifted(near, ctx, offset) for offset in range(reach, 0, -1)], axis=0)
    mixed, logsums = attend_forward(meta, queries, far, near)
    hidden, second_in, out_low, up_low = out_call(
        place, values, mixed, gain_two, shift_two, bias_out, adapter_out_in, adapter_out_out, adapter_up_in, pieces_out
    )
    grad_active, grad_down_low = active_grad_call(place, upstream, adapter_down_in, adapter_down_out, pieces_down)
    active, grad_second, down_low, grad_up_out, grad_down_in = up_call(
        place, second_in, up_low, grad_active, grad_down_low, bias_up, adapter_up_out, adapter_down_in, pieces_up
    )
    grad_hidden, grad_mixed, grad_up_in, grad_out_out, grad_out_in, grad_down_out = out_grad_call(
        place, grad_second, hidden, second_in, upstream, mixed, out_low, down_low, gain_two,
        adapter_up_in, adapter_out_in, adapter_out_out, pieces_out,
    )
    total_up_out, total_down_in, total_up_in, total_out_out, total_out_in, total_down_out = summed_adapters(
        sizes, [grad_up_out, grad_down_in, grad_up_in, grad_out_out, grad_out_in, grad_down_out], chosen
    )
    near_grads, far_grads = attend_backward(meta, queries, far, near, grad_mixed, mixed, logsums)
    output = down_call(place, active, hidden, down_low, bias_down, adapter_down_out, pieces_down)
    moved = 0
    for offset in range(reach, 0, -1):
        first_row = (reach - offset) * row_count
        moved += shifted(far_grads[:, first_row : first_row + row_count], ctx, -offset)
    grad_input, grad_qkv_out, grad_qkv_in = tokens_grad_call(
        place, values, first_in, qkv_low, grad_hidden, gain_one, adapter_qkv_in, adapter_qkv_out,
        near_grads, moved, pieces_qkv,
    )
    total_qkv_out, total_qkv_in = summed_adapters(sizes, [grad_qkv_out, grad_qkv_in], chosen)
    total_qkv_out = jnp.concatenate(
        [total_qkv_out[..., third * PADDED : third * PADDED + feature_count] for third in range(3)], axis=-1
    )
    return (
        output[None],
        grad_input[None],
        total_qkv_in,
        total_qkv_out,
        total_out_in,
        total_out_out,
        total_up_in,
        total_up_out,
        total_down_in,
        total_down_out,
    )


def solution(mesh):
    return jax.shard_map(
        partial(shards, dict(mesh.shape)),
        mesh=mesh,
        in_specs=(
            P(("dp", "wt"), "ctx", None),
            P(("dp", "wt"), "ctx", None),
            P(("dp", "wt"), None),
            P(("dp", "wt"), None),
            P("wt"),
            P("wt"),
            P("wt", None),
            P("wt"),
            P("wt", None),
            P("wt"),
            P("wt"),
            P("wt"),
            P("wt", None),
            P("wt"),
            P("wt", None),
            P("wt"),
            P(),
            P(),
            P(),
            P(),
            P(),
            P(),
            P(),
            P(),
        ),
        out_specs=(
            P(("dp", "wt"), "ctx", None),
            P(("dp", "wt"), "ctx", None),
            P(),
            P(),
            P(),
            P(),
            P(),
            P(),
            P(),
            P(),
        ),
        check_vma=False,
    )
```

time: 1670 us -> 1010 us (0.60)
  waiting for transfers between devices: 991 us -> 377 us
  matrix products: 324 us -> 7.68 us
  Pallas kernels: 164 us -> 438 us
  local copies, waits for them, and re-layouts: 65.2 us -> 122 us
  other arithmetic: 60 us -> 15.5 us
  blocking collectives: 35.9 us -> 0 us
    all_gather x4 -> x2, waiting for transfers between devices: 808 us -> 134 us  [summed_adapters(): everyone = lax.all_gather(sent, ('dp', 'wt'), axis=0)]
    dot_general x32 -> x8, matrix products: 324 us -> 7.68 us  [summed_adapters(): jnp.einsum('as,srn->arn', selector, part, preferred_element_type=jnp.floa...]
    pallas_call x0 -> x7, Pallas kernels: none -> 278 us  [call(): pl.pallas_call(kernel, grid_spec=pltpu.PrefetchScalarGridSpec(num_scalar_...]
    ppermute x2 -> x44, waiting for transfers between devices: 0.01 us -> 243 us  [the longest x12 141 us: gather_shards(): moved = lax.ppermute(moved, 'wt', ring_pairs(sizes['wt']))]
    psum x1 -> x0, waiting for transfers between devices: 180 us -> none  [shards(): lax.psum((stacked_qkv_in, stacked_qkv_out, stacked_out_in, stacked_out_ou...]
    unnamed x1 -> x0, blocking collectives: 35.9 us -> none
    unnamed x162 -> x94, local copies, waits for them, and re-layouts: 27.6 us -> 52.4 us
    slice x2 -> x25, local copies, waits for them, and re-layouts: 4.96 us -> 22.7 us  [the longest x4 14.7 us: summed_adapters(): part = everyone[:, :, start:start + width]]
  transfers between devices with their start and end apart: 7 -> 46, of which waited for: 4 -> 24; matrix products, arithmetic and copies ran while one was open for 16% -> 9% of each run, Pallas kernels for 3% -> 18%
where the time goes in v2:
time: 1010 us; the launch traced here: 999 us
  Pallas kernels  438 us (43%)
  waiting for transfers between devices  377 us (37%)
  local copies, waits for them, and re-layouts  122 us (12%)
  starting transfers between devices  23.1 us (2%)
  between operations  15.8 us (2%)
  other arithmetic  15.5 us (2%)
    pallas_call x7, Pallas kernels, call(): pl.pallas_call(kernel, grid_spec=pltpu.PrefetchScalarGridSpec(num_scalar_...  278 us
    ppermute x12, waiting for transfers between devices, gather_shards(): moved = lax.ppermute(moved, 'wt', ring_pairs(sizes['wt']))  141 us
    all_gather x2, waiting for transfers between devices, summed_adapters(): everyone = lax.all_gather(sent, ('dp', 'wt'), axis=0)  134 us
    pallas_call x1, Pallas kernels, attend_backward(): pl.pallas_call(partial(attend_backward_kernel, tiles), grid_spec=pltpu.Pr...  107 us
    pallas_call x1, Pallas kernels, attend_forward(): pl.pallas_call(partial(attend_forward_kernel, tiles), grid_spec=pltpu.Pre...  53.7 us
    unnamed x94, local copies, waits for them, and re-layouts  52.4 us
    ppermute x4, waiting for transfers between devices, spread_parts(): both = lax.ppermute(one, ('dp', 'ctx'), second)  41.2 us
    ppermute x4, waiting for transfers between devices, spread_parts(): one = lax.ppermute(mine, ('dp', 'ctx'), first)  22.9 us
  transfers between devices with their start and end apart: 46, of which 24 were waited for; matrix products, arithmetic and copies ran while one was open for 9% of the time, Pallas kernels for 18%

profile of v2, /device:TPU:0, one launch (start us, length us, event | category | flops | bytes accessed | tf_op | source)
XLA Modules:
  0.0 998.5 jit_solution(15375378441162794669)
XLA Ops:
  45.2 20.1 %collective-permute-done.1 = bf16[80,4992]{1,0:T(8,128)(2,1)S(1)} collective-permute-done((bf16[80,4992]{1,0:T(8,128)(2,1)S(1)}, bf16[80,4992]{1,0:T(8,128)(2,1)S(1)}, u32[]{:S(2)}, u32[]{:S(2)}) %collective-permute-start.1) | collective-permute-done | bytes 798752 | tf_op jit(solution)/shard_map/ppermute | solution.py:745
  65.4 19.8 %collective-permute-done.2 = bf16[80,4992]{1,0:T(8,128)(2,1)S(1)} collective-permute-done((bf16[80,4992]{1,0:T(8,128)(2,1)S(1)}, bf16[80,4992]{1,0:T(8,128)(2,1)S(1)}, u32[]{:S(2)}, u32[]{:S(2)}) %collective-permute-start.2) | collective-permute-done | bytes 798752 | tf_op jit(solution)/shard_map/ppermute | solution.py:745
  97.9 7.8 collective-permute-done.12
  113.4 9.7 copy.58
  126.1 17.5 %collective-permute-done.21 = bf16[256,1600]{0,1:T(8,128)(2,1)S(1)} collective-permute-done((bf16[256,1600]{0,1:T(8,128)(2,1)S(1)}, bf16[256,1600]{0,1:T(8,128)(2,1)S(1)}, u32[]{:S(2)}, u32[]{:S(2)}) %collective-permute-start.21) | collective-permute-done | bytes 819232 | tf_op jit(solution)/shard_map/ppermute | solution.py:745
  144.3 17.7 %collective-permute-done.22 = bf16[256,1600]{0,1:T(8,128)(2,1)S(1)} collective-permute-done((bf16[256,1600]{0,1:T(8,128)(2,1)S(1)}, bf16[256,1600]{0,1:T(8,128)(2,1)S(1)}, u32[]{:S(2)}, u32[]{:S(2)}) %collective-permute-start.22) | collective-permute-done | bytes 819232 | tf_op jit(solution)/shard_map/ppermute | solution.py:745
  162.6 15.5 %collective-permute-done.23 = bf16[256,1600]{0,1:T(8,128)(2,1)S(1)} collective-permute-done((bf16[256,1600]{0,1:T(8,128)(2,1)S(1)}, bf16[256,1600]{0,1:T(8,128)(2,1)S(1)}, u32[]{:S(2)}, u32[]{:S(2)}) %collective-permute-start.23) | collective-permute-done | bytes 819232 | tf_op jit(solution)/shard_map/ppermute | solution.py:745
  203.1 34.9 %qkv.1 = (bf16[1024,1600]{1,0:T(8,128)(2,1)}, bf16[1024,16]{1,0:T(8,128)(2,1)}, bf16[1024,1664]{1,0:T(8,128)(2,1)}, bf16[1024,3328]{1,0:T(8,128)(2,1)}) custom-call(s32[12]{0:T(128)} %stack.159.place, bf16[1024,1600]{1,0:T(8,128)(2,1)} %bitcast.116, f32[1,1600]{1,0:T(1,128)} %reshape.126.gain, f32[1,1600]{1,0:T(1,128)} %reshape.127.shift, ...), custom_call_target="tpu_custom_call" | custom-call | tf_op jit(solution)/shard_map/qkv/pallas_call | solution.py:103
  239.2 21.4 %collective-permute-done.33 = bf16[64,6400]{1,0:T(8,128)(2,1)S(1)} collective-permute-done((bf16[64,6400]{1,0:T(8,128)(2,1)}, bf16[64,6400]{1,0:T(8,128)(2,1)S(1)}, u32[]{:S(2)}, u32[]{:S(2)}) %collective-permute-start.33) | collective-permute-done | bytes 819232 | tf_op jit(solution)/shard_map/ppermute | solution.py:745
  268.4 21.4 %collective-permute-done.24.more_3_ = bf16[3,192,1600]{2,1,0:T(8,128)(2,1)} collective-permute-done((bf16[3,192,1600]{2,1,0:T(8,128)(2,1)S(1)}, bf16[3,192,1600]{2,1,0:T(8,128)(2,1)}, u32[]{:S(2)}, u32[]{:S(2)}) %collective-permute-start.24) | collective-permute-done | bytes 1843232 | tf_op jit(solution)/shard_map/ppermute | solution.py:754
  310.5 21.9 %collective-permute-done.26.more_5_ = bf16[3,192,1600]{2,1,0:T(8,128)(2,1)} collective-permute-done((bf16[3,192,1600]{2,1,0:T(8,128)(2,1)}, bf16[3,192,1600]{2,1,0:T(8,128)(2,1)}, u32[]{:S(2)}, u32[]{:S(2)}) %collective-permute-start.26) | collective-permute-done | bytes 1843232 | tf_op jit(solution)/shard_map/ppermute | solution.py:756
  337.2 14.9 %collective-permute-done.35.more_4_ = bf16[3,48,6400]{2,1,0:T(8,128)(2,1)} collective-permute-done((bf16[3,48,6400]{2,1,0:T(8,128)(2,1)}, bf16[3,48,6400]{2,1,0:T(8,128)(2,1)}, u32[]{:S(2)}, u32[]{:S(2)}) %collective-permute-start.35) | collective-permute-done | bytes 1843232 | tf_op jit(solution)/shard_map/ppermute | solution.py:755
  352.7 19.2 %collective-permute-done.36.more_5_ = bf16[3,48,6400]{2,1,0:T(8,128)(2,1)} collective-permute-done((bf16[3,48,6400]{2,1,0:T(8,128)(2,1)}, bf16[3,48,6400]{2,1,0:T(8,128)(2,1)}, u32[]{:S(2)}, u32[]{:S(2)}) %collective-permute-start.36) | collective-permute-done | bytes 1843232 | tf_op jit(solution)/shard_map/ppermute | solution.py:756
  374.4 34.6 %active_grad.1 = (bf16[1024,6400]{1,0:T(8,128)(2,1)}, bf16[1024,16]{1,0:T(8,128)(2,1)}) custom-call(s32[12]{0:T(128)} %stack.159.place, bf16[1024,1600]{1,0:T(8,128)(2,1)} %bitcast.119, bf16[16,6400]{1,0:T(8,128)(2,1)} %get-tuple-element.124.a_in.d_in, bf16[16,1600]{1,0:T(8,128)(2,1)} %dynamic-slice_bitcast_fusion.3.a_out, bf16[1600,1600]{1,0:T(8,128)(2,1)} %more_0_.3, ...), custom_call_target="tpu_custom_call" | custom-call | tf_op jit(solution)/shard_map/active_grad/pallas_call | solution.py:103
  409.0 53.7 %attend_forward.1 = (bf16[1024,1664]{1,0:T(8,128)(2,1)}, f32[13,2048,128]{2,1,0:T(8,128)}) custom-call(s32[4]{0:T(128)} %pad_add_fusion.meta, bf16[1024,1664]{1,0:T(8,128)(2,1)} %get-tuple-element.43.q_ref, bf16[1024,3328]{1,0:T(8,128)(2,1)} %collective-permute-done.10.k_far.v_far, bf16[1024,3328]{1,0:T(8,128)(2,1)} %collective-permute-done.10.k_far.v_far, ...), custom_call_target="tpu_custom_call" | custom-call | tf_op jit(solution)/shard_map/attend_forward/pallas_call | solution.py:605
  463.5 18.1 %out.1 = (f32[1024,1600]{1,0:T(8,128)}, bf16[1024,1600]{1,0:T(8,128)(2,1)}, bf16[1024,16]{1,0:T(8,128)(2,1)}, bf16[1024,16]{1,0:T(8,128)(2,1)}) custom-call(s32[12]{0:T(128)} %stack.159.place, bf16[1024,1600]{1,0:T(8,128)(2,1)} %bitcast.117, bf16[1024,1664]{1,0:T(8,128)(2,1)} %get-tuple-element.45.mixed_ref.o_ref, f32[1,1600]{1,0:T(1,128)} %reshape.129.gain, ...), custom_call_target="tpu_custom_call" | custom-call | tf_op jit(solution)/shard_map/out/pallas_call | solution.py:103
  481.6 83.3 %up.1 = (bf16[1024,6400]{1,0:T(8,128)(2,1)}, f32[1024,1664]{1,0:T(8,128)}, bf16[1024,16]{1,0:T(8,128)(2,1)}, f32[16,6400]{1,0:T(8,128)}, f32[16,6400]{1,0:T(8,128)}) custom-call(s32[12]{0:T(128)} %stack.159.place, bf16[1024,1600]{1,0:T(8,128)(2,1)} %get-tuple-element.47.second_ref, bf16[1024,16]{1,0:T(8,128)(2,1)} %get-tuple-element.48.up_low_ref, ...), custom_call_target="tpu_custom_call" | custom-call | tf_op jit(solution)/shard_map/up/pallas_call | solution.py:103
  565.0 24.4 %out_grad.1 = (f32[1024,1600]{1,0:T(8,128)}, bf16[1024,1664]{1,0:T(8,128)(2,1)}, f32[16,1600]{1,0:T(8,128)}, f32[16,1600]{1,0:T(8,128)}, f32[16,1600]{1,0:T(8,128)}, /*index=5*/f32[16,1600]{1,0:T(8,128)}) custom-call(s32[12]{0:T(128)} %stack.159.place, f32[1024,1664]{1,0:T(8,128)} %get-tuple-element.60.acc_ref, f32[1024,1600]{1,0:T(8,128)} %get-tuple-element.56.hidden_ref, ...), custom_call_target="tpu_custom_call" | custom-call | tf_op jit(solution)/shard_map/out_grad/pallas_call | solution.py:103
  589.4 106.7 %attend_backward.1 = (bf16[3,1024,1664]{2,1,0:T(8,128)(2,1)}, bf16[2,1024,1664]{2,1,0:T(8,128)(2,1)}) custom-call(s32[4]{0:T(128)} %pad_add_fusion.meta, bf16[1024,1664]{1,0:T(8,128)(2,1)} %get-tuple-element.43.q_ref, bf16[1024,3328]{1,0:T(8,128)(2,1)} %collective-permute-done.10.k_far.v_far, bf16[1024,3328]{1,0:T(8,128)(2,1)} %collective-permute-done.10.k_far.v_far, ...), custom_call_target="tpu_custom_call" | custom-call | tf_op jit(solution)/shard_map/attend_backward/pallas_call | solution.py:673
  697.3 11.8 %collective-permute-done.41.far_ref = bf16[2,1024,1664]{2,1,0:T(8,128)(2,1)} collective-permute-done((bf16[2,1024,1664]{2,1,0:T(8,128)(2,1)}, bf16[2,1024,1664]{2,1,0:T(8,128)(2,1)}, u32[]{:S(2)}, u32[]{:S(2)}) %collective-permute-start.41) | collective-permute-done | bytes 6815776 | tf_op jit(solution)/shard_map/ppermute | solution.py:725
  709.2 47.7 %tokens_grad.1 = (f32[1024,1600]{1,0:T(8,128)}, f32[16,4992]{1,0:T(8,128)}, f32[16,1600]{1,0:T(8,128)}) custom-call(s32[12]{0:T(128)} %stack.159.place, bf16[1024,1600]{1,0:T(8,128)(2,1)} %bitcast.118, bf16[1024,1600]{1,0:T(8,128)(2,1)} %get-tuple-element.58.first_ref, bf16[1024,16]{1,0:T(8,128)(2,1)} %get-tuple-element.59.low_ref, ...), custom_call_target="tpu_custom_call" | custom-call | tf_op jit(solution)/shard_map/tokens_grad/pallas_call | solution.py:103
  766.7 34.5 %down.1 = bf16[1024,1600]{1,0:T(8,128)(2,1)} custom-call(s32[12]{0:T(128)} %stack.159.place, bf16[1024,6400]{1,0:T(8,128)(2,1)} %get-tuple-element.55.active_ref, f32[1024,1600]{1,0:T(8,128)} %get-tuple-element.56.hidden_ref, bf16[1024,16]{1,0:T(8,128)(2,1)} %get-tuple-element.57.down_low_ref, f32[1,1600]{1,0:T(1,128)} %reshape.133.bias, ...), custom_call_target="tpu_custom_call" | custom-call | tf_op jit(solution)/shard_map/down/pallas_call | solution.py:103
  814.4 20.6 %all-gather.5.cloned.1.call-done = bf16[256,6720]{1,0:T(8,128)(2,1)} async-done(((bf16[16,6720]{1,0:T(8,128)(2,1)}), bf16[256,6720]{1,0:T(8,128)(2,1)}) %all-gather.5.cloned.1.call-update) | async-done | bytes 3440656 | tf_op jit(solution)/shard_map/all_gather | solution.py:781
  850.0 113.4 %all-gather.7.cloned.1.call-done = bf16[256,19328]{1,0:T(8,128)(2,1)} async-done(((bf16[16,19328]{1,0:T(8,128)(2,1)}), bf16[256,19328]{1,0:T(8,128)(2,1)}) %all-gather.7.cloned.1.call-update) | async-done | bytes 9895952 | tf_op jit(solution)/shard_map/all_gather | solution.py:781
  (283 shorter events, 191.9 us)
Async XLA Ops:
  7.2 827.8 %all-gather.5.cloned.1.call-start = ((), (), s32[]{:S(2)}) async-start(), calls=%async_computation | async-start | bytes 3690496 | tf_op jit(solution)/shard_map/all_gather | solution.py:781
  86.6 105.6 %collective-permute-start.4 = (bf16[3,48,4992]{2,1,0:T(8,128)(2,1)}, bf16[3,48,4992]{2,1,0:T(8,128)(2,1)}, u32[]{:S(2)}, u32[]{:S(2)}) collective-permute-start(bf16[3,48,4992]{2,1,0:T(8,128)(2,1)} %pad_maximum_fusion.2.more_2_), channel_id=1, source_target_pairs={{0,16},{4,12},{8,24},{12,4},{16,0},{20,28},{24,8},{28,20},{1,17},{... | collective-permute-start | bytes 4313096 | tf_op jit(solution)/shard_map/ppermute | solution.py:755
  87.6 74.5 %collective-permute-start.3 = (bf16[3,48,4992]{2,1,0:T(8,128)(2,1)}, bf16[3,48,4992]{2,1,0:T(8,128)(2,1)}, u32[]{:S(2)}, u32[]{:S(2)}) collective-permute-start(bf16[3,48,4992]{2,1,0:T(8,128)(2,1)} %pad_maximum_fusion.2.more_2_), channel_id=1, source_target_pairs={{0,8},{4,20},{8,0},{12,28},{16,24},{20,4},{24,16},{28,12},{1,9},{5... | collective-permute-start | bytes 4313096 | tf_op jit(solution)/shard_map/ppermute | solution.py:754
  162.1 30.2 %collective-permute-start.5 = (bf16[3,48,4992]{2,1,0:T(8,128)(2,1)}, bf16[3,48,4992]{2,1,0:T(8,128)(2,1)}, u32[]{:S(2)}, u32[]{:S(2)}) collective-permute-start(bf16[3,48,4992]{2,1,0:T(8,128)(2,1)} %collective-permute-done.3.more_3_), channel_id=1, source_target_pairs={{0,16},{4,12},{8,24},{12,4},{16,0},{20,28},{24,8},{28,20},{1,17},{... | collective-permute-start | bytes 4313096 | tf_op jit(solution)/shard_map/ppermute | solution.py:756
  195.5 42.5 %collective-permute-start.32 = (bf16[64,6400]{1,0:T(8,128)(2,1)}, bf16[64,6400]{1,0:T(8,128)(2,1)}, u32[]{:S(2)}, u32[]{:S(2)}) collective-permute-start(bf16[64,6400]{1,0:T(8,128)(2,1)} %collective-permute-done.31), channel_id=1, source_target_pairs={{0,1},{1,2},{2,3},{3,0},{4,5},{5,6},{6,7},{7,4},{8,9},{9,10},{10,1... | collective-permute-start | bytes 2457608 | tf_op jit(solution)/shard_map/ppermute | solution.py:745
  197.2 64.2 %collective-permute-start.17 = (bf16[3,48,1600]{2,1,0:T(8,128)(2,1)S(1)}, bf16[3,48,1600]{2,1,0:T(8,128)(2,1)S(1)}, u32[]{:S(2)}, u32[]{:S(2)}) collective-permute-start(bf16[3,48,1600]{2,1,0:T(8,128)(2,1)S(1)} %pad_maximum_fusion.10.more_2_), channel_id=1, source_target_pairs={{0,4},{4,0},{1,5},{5,1},{2,6},{6,2},{3,7},{7,3},{8,12},{12,8},{9,1... | collective-permute-start | bytes 1382408 | tf_op jit(solution)/shard_map/ppermute | solution.py:758
  199.2 62.8 %collective-permute-start.19 = (bf16[3,48,1600]{2,1,0:T(8,128)(2,1)}, bf16[3,48,1600]{2,1,0:T(8,128)(2,1)}, u32[]{:S(2)}, u32[]{:S(2)}) collective-permute-start(bf16[3,48,1600]{2,1,0:T(8,128)(2,1)} %collective-permute-done.15.more_4_), channel_id=1, source_target_pairs={{0,4},{4,0},{1,5},{5,1},{2,6},{6,2},{3,7},{7,3},{8,12},{12,8},{9,1... | collective-permute-start | bytes 1382408 | tf_op jit(solution)/shard_map/ppermute | solution.py:758
  199.4 68.5 %collective-permute-start.18 = (bf16[3,48,1600]{2,1,0:T(8,128)(2,1)}, bf16[3,48,1600]{2,1,0:T(8,128)(2,1)}, u32[]{:S(2)}, u32[]{:S(2)}) collective-permute-start(bf16[3,48,1600]{2,1,0:T(8,128)(2,1)} %collective-permute-done.14.more_3_), channel_id=1, source_target_pairs={{0,4},{4,0},{1,5},{5,1},{2,6},{6,2},{3,7},{7,3},{8,12},{12,8},{9,1... | collective-permute-start | bytes 1382408 | tf_op jit(solution)/shard_map/ppermute | solution.py:758
  202.0 65.9 %collective-permute-start.25 = (bf16[3,192,1600]{2,1,0:T(8,128)(2,1)S(1)}, bf16[3,192,1600]{2,1,0:T(8,128)(2,1)}, u32[]{:S(2)}, u32[]{:S(2)}) collective-permute-start(bf16[3,192,1600]{2,1,0:T(8,128)(2,1)S(1)} %pad_maximum_fusion.more_2_), channel_id=1, source_target_pairs={{0,16},{4,12},{8,24},{12,4},{16,0},{20,28},{24,8},{28,20},{1,17},{... | collective-permute-start | bytes 5529608 | tf_op jit(solution)/shard_map/ppermute | solution.py:755
  260.7 29.1 %collective-permute-start.24 = (bf16[3,192,1600]{2,1,0:T(8,128)(2,1)S(1)}, bf16[3,192,1600]{2,1,0:T(8,128)(2,1)}, u32[]{:S(2)}, u32[]{:S(2)}) collective-permute-start(bf16[3,192,1600]{2,1,0:T(8,128)(2,1)S(1)} %pad_maximum_fusion.more_2_), channel_id=1, source_target_pairs={{0,8},{4,20},{8,0},{12,28},{16,24},{20,4},{24,16},{28,12},{1,9},{5... | collective-permute-start | bytes 5529608 | tf_op jit(solution)/shard_map/ppermute | solution.py:754
  261.5 29.0 %collective-permute-start.16 = (bf16[3,48,1600]{2,1,0:T(8,128)(2,1)}, bf16[3,48,1600]{2,1,0:T(8,128)(2,1)S(1)}, u32[]{:S(2)}, u32[]{:S(2)}) collective-permute-start(bf16[3,48,1600]{2,1,0:T(8,128)(2,1)} %collective-permute-done.14.more_3_), channel_id=1, source_target_pairs={{0,16},{4,12},{8,24},{12,4},{16,0},{20,28},{24,8},{28,20},{1,17},{... | collective-permute-start | bytes 1382408 | tf_op jit(solution)/shard_map/ppermute | solution.py:756
  262.1 110.8 %collective-permute-start.10 = (bf16[1024,3328]{1,0:T(8,128)(2,1)}, bf16[1024,3328]{1,0:T(8,128)(2,1)}, u32[]{:S(2)}, u32[]{:S(2)}) collective-permute-start(bf16[1024,3328]{1,0:T(8,128)(2,1)} %get-tuple-element.44.k_near.v_near), channel_id=1, source_target_pairs={{0,4},{1,5},{2,6},{3,7},{8,12},{9,13},{10,14},{11,15},{16,20},{17,... | collective-permute-start | bytes 20447240 | tf_op jit(solution)/shard_map/ppermute | solution.py:725
  267.9 41.3 %collective-permute-start.27 = (bf16[3,192,1600]{2,1,0:T(8,128)(2,1)S(1)}, bf16[3,192,1600]{2,1,0:T(8,128)(2,1)}, u32[]{:S(2)}, u32[]{:S(2)}) collective-permute-start(bf16[3,192,1600]{2,1,0:T(8,128)(2,1)S(1)} %pad_maximum_fusion.more_2_), channel_id=1, source_target_pairs={{0,4},{4,0},{1,5},{5,1},{2,6},{6,2},{3,7},{7,3},{8,12},{12,8},{9,1... | collective-permute-start | bytes 5529608 | tf_op jit(solution)/shard_map/ppermute | solution.py:758
  267.9 41.3 %collective-permute-start.29 = (bf16[3,192,1600]{2,1,0:T(8,128)(2,1)}, bf16[3,192,1600]{2,1,0:T(8,128)(2,1)}, u32[]{:S(2)}, u32[]{:S(2)}) collective-permute-start(bf16[3,192,1600]{2,1,0:T(8,128)(2,1)} %collective-permute-done.25.more_4_), channel_id=1, source_target_pairs={{0,4},{4,0},{1,5},{5,1},{2,6},{6,2},{3,7},{7,3},{8,12},{12,8},{9,1... | collective-permute-start | bytes 5529608 | tf_op jit(solution)/shard_map/ppermute | solution.py:758
  289.8 42.7 %collective-permute-start.26 = (bf16[3,192,1600]{2,1,0:T(8,128)(2,1)}, bf16[3,192,1600]{2,1,0:T(8,128)(2,1)}, u32[]{:S(2)}, u32[]{:S(2)}) collective-permute-start(bf16[3,192,1600]{2,1,0:T(8,128)(2,1)} %collective-permute-done.24.more_3_), channel_id=1, source_target_pairs={{0,16},{4,12},{8,24},{12,4},{16,0},{20,28},{24,8},{28,20},{1,17},{... | collective-permute-start | bytes 5529608 | tf_op jit(solution)/shard_map/ppermute | solution.py:756
  290.5 43.4 %collective-permute-start.34 = (bf16[3,48,6400]{2,1,0:T(8,128)(2,1)}, bf16[3,48,6400]{2,1,0:T(8,128)(2,1)}, u32[]{:S(2)}, u32[]{:S(2)}) collective-permute-start(bf16[3,48,6400]{2,1,0:T(8,128)(2,1)} %pad_maximum_fusion.1.more_2_), channel_id=1, source_target_pairs={{0,8},{4,20},{8,0},{12,28},{16,24},{20,4},{24,16},{28,12},{1,9},{5... | collective-permute-start | bytes 5529608 | tf_op jit(solution)/shard_map/ppermute | solution.py:754
  309.2 43.0 %collective-permute-start.35 = (bf16[3,48,6400]{2,1,0:T(8,128)(2,1)}, bf16[3,48,6400]{2,1,0:T(8,128)(2,1)}, u32[]{:S(2)}, u32[]{:S(2)}) collective-permute-start(bf16[3,48,6400]{2,1,0:T(8,128)(2,1)} %pad_maximum_fusion.1.more_2_), channel_id=1, source_target_pairs={{0,16},{4,12},{8,24},{12,4},{16,0},{20,28},{24,8},{28,20},{1,17},{... | collective-permute-start | bytes 5529608 | tf_op jit(solution)/shard_map/ppermute | solution.py:755
  334.0 38.0 %collective-permute-start.36 = (bf16[3,48,6400]{2,1,0:T(8,128)(2,1)}, bf16[3,48,6400]{2,1,0:T(8,128)(2,1)}, u32[]{:S(2)}, u32[]{:S(2)}) collective-permute-start(bf16[3,48,6400]{2,1,0:T(8,128)(2,1)} %collective-permute-done.34.more_3_), channel_id=1, source_target_pairs={{0,16},{4,12},{8,24},{12,4},{16,0},{20,28},{24,8},{28,20},{1,17},{... | collective-permute-start | bytes 5529608 | tf_op jit(solution)/shard_map/ppermute | solution.py:756
  337.1 144.4 %collective-permute-start.37 = (bf16[3,48,6400]{2,1,0:T(8,128)(2,1)}, bf16[3,48,6400]{2,1,0:T(8,128)(2,1)}, u32[]{:S(2)}, u32[]{:S(2)}) collective-permute-start(bf16[3,48,6400]{2,1,0:T(8,128)(2,1)} %pad_maximum_fusion.1.more_2_), channel_id=1, source_target_pairs={{0,4},{4,0},{1,5},{5,1},{2,6},{6,2},{3,7},{7,3},{8,12},{12,8},{9,1... | collective-permute-start | bytes 5529608 | tf_op jit(solution)/shard_map/ppermute | solution.py:758
  352.2 129.4 %collective-permute-start.38 = (bf16[3,48,6400]{2,1,0:T(8,128)(2,1)}, bf16[3,48,6400]{2,1,0:T(8,128)(2,1)}, u32[]{:S(2)}, u32[]{:S(2)}) collective-permute-start(bf16[3,48,6400]{2,1,0:T(8,128)(2,1)} %collective-permute-done.34.more_3_), channel_id=1, source_target_pairs={{0,4},{4,0},{1,5},{5,1},{2,6},{6,2},{3,7},{7,3},{8,12},{12,8},{9,1... | collective-permute-start | bytes 5529608 | tf_op jit(solution)/shard_map/ppermute | solution.py:758
  352.2 129.4 %collective-permute-start.39 = (bf16[3,48,6400]{2,1,0:T(8,128)(2,1)}, bf16[3,48,6400]{2,1,0:T(8,128)(2,1)}, u32[]{:S(2)}, u32[]{:S(2)}) collective-permute-start(bf16[3,48,6400]{2,1,0:T(8,128)(2,1)} %collective-permute-done.35.more_4_), channel_id=1, source_target_pairs={{0,4},{4,0},{1,5},{5,1},{2,6},{6,2},{3,7},{7,3},{8,12},{12,8},{9,1... | collective-permute-start | bytes 5529608 | tf_op jit(solution)/shard_map/ppermute | solution.py:758
  371.9 109.7 %collective-permute-start.40 = (bf16[3,48,6400]{2,1,0:T(8,128)(2,1)}, bf16[3,48,6400]{2,1,0:T(8,128)(2,1)}, u32[]{:S(2)}, u32[]{:S(2)}) collective-permute-start(bf16[3,48,6400]{2,1,0:T(8,128)(2,1)} %collective-permute-done.36.more_5_), channel_id=1, source_target_pairs={{0,4},{4,0},{1,5},{5,1},{2,6},{6,2},{3,7},{7,3},{8,12},{12,8},{9,1... | collective-permute-start | bytes 5529608 | tf_op jit(solution)/shard_map/ppermute | solution.py:758
  372.9 89.8 %collective-permute-start.20 = (bf16[3,48,1600]{2,1,0:T(8,128)(2,1)S(1)}, bf16[3,48,1600]{2,1,0:T(8,128)(2,1)S(1)}, u32[]{:S(2)}, u32[]{:S(2)}) collective-permute-start(bf16[3,48,1600]{2,1,0:T(8,128)(2,1)S(1)} %collective-permute-done.16.more_5_), channel_id=1, source_target_pairs={{0,4},{4,0},{1,5},{5,1},{2,6},{6,2},{3,7},{7,3},{8,12},{12,8},{9,1... | collective-permute-start | bytes 1382408 | tf_op jit(solution)/shard_map/ppermute | solution.py:758
  761.5 202.0 %all-gather.7.cloned.1.call-start = ((), (), s32[]{:S(2)}) async-start(), calls=%async_computation.1 | async-start | bytes 10514432 | tf_op jit(solution)/shard_map/all_gather | solution.py:781
  (62 other events, 977.7 us)
Sparse Core Ops, SparseCore 0:
  761.6 73.3 all-gather.4
  838.3 125.0 all-gather.6

commit v3 on v2

--- a/solution.py
+++ b/solution.py
@@ -58,17 +58,31 @@
 
 
 def start_shard(pieces, place, distance, target, source_columns, columns, sem):
-    own, rest, parts = pieces[0], pieces[1], pieces[2:]
+    own, steps = pieces[0], pieces[1:SHARDS]
+    together = len(steps[0].shape) == 3
+    parts = pieces[2:] if together else pieces[SHARDS:]
     base = place[distance] * own.shape[0]
     if distance == 0:
         copy_piece(own.at[:, source_columns], target, base, columns, sem)
         return
-    part_rows = parts[0].shape[1]
+    part_rows = own.shape[0] // (PARTS * 16) * 16
     for source in range(PARTS):
+        if len(parts) == PARTS:
+            part = parts[source].at[distance - 1, pl.ds(0, part_rows), source_columns]
+        else:
+            part = parts[(distance - 1) * PARTS + source].at[:, source_columns]
         row = base + place[SHARDS + source] * part_rows
-        copy_piece(parts[source].at[distance - 1, :, source_columns], target, row, columns, sem)
-    row = base + PARTS * part_rows
-    copy_piece(rest.at[distance - 1, :, source_columns], target, row, columns, sem)
+        copy_piece(part, target, row, columns, sem)
+    left = own.shape[0] - PARTS * part_rows
+    base += PARTS * part_rows
+    if left > RANK:
+        left //= SHARDS
+        for source in range(SHARDS):
+            rest = parts[source].at[distance - 1, pl.ds(part_rows, left), source_columns]
+            copy_piece(rest, target, base + place[SHARDS + source] // 2 * left, columns, sem)
+        return
+    step = steps[0].at[place[distance]] if together else steps[distance - 1]
+    copy_piece(step.at[pl.ds(part_rows, left), source_columns], target, base, columns, sem)
 
 
 def start_columns(pieces, place, target, source_columns, columns, sem):
@@ -99,7 +113,7 @@
     return pl.BlockSpec(shape, lambda *_: (0,) * len(shape))
 
 
-def call(kernel, name, grid, place, inputs, pieces, in_specs, outs, out_specs, scratch):
+def call(kernel, name, grid, place, inputs, pieces, in_specs, outs, out_specs, scratch, macs, aliases={}):
     return pl.pallas_call(
         kernel,
         grid_spec=pltpu.PrefetchScalarGridSpec(
@@ -110,7 +124,9 @@
             scratch_shapes=scratch,
         ),
         out_shape=outs,
+        input_output_aliases=aliases,
         compiler_params=pltpu.CompilerParams(vmem_limit_bytes=VMEM_LIMIT),
+        cost_estimate=pl.CostEstimate(flops=2 * macs, bytes_accessed=1 << 22, transcendentals=0),
         name=name,
     )(place, *inputs, *pieces)
 
@@ -119,6 +135,10 @@
     return jax.ShapeDtypeStruct(shape, kind)
 
 
+def picked(width, column=lambda *grid: 0):
+    return pl.BlockSpec((None, RANK, width), lambda c, place: (place[SHARDS + PARTS], 0, column(c)))
+
+
 def column_block(rows, width):
     return pl.BlockSpec((rows, width), lambda c, *_: (0, c))
 
@@ -127,23 +147,15 @@
     return pl.BlockSpec((BLOCK, width), lambda r, *_: (r, 0))
 
 
-def qkv_kernel(place, x_ref, gain, shift, bias, a_in, a_out, *more):
-    pieces, (first_ref, low_ref, q_ref, kv_ref, w, wide, sems) = more[:-7], more[-7:]
+def keys_kernel(place, x_ref, gain, shift, bias, a_in, a_out, *more):
+    pieces, (first_ref, low_ref, kv_ref, w, wide, sems) = more[:-6], more[-6:]
     rows, features = x_ref.shape
-    step, steps = pl.program_id(0), pl.num_programs(0)
-    width = w.shape[2]
-
-    def fetch(c):
-        columns = pl.ds(pl.multiple_of(c * width, 128), width)
-        start_columns(pieces, place, w.at[c % 2], columns, pl.ds(0, width), sems.at[c % 2])
-
-    @pl.when(step == 0)
-    def _():
-        fetch(0)
+
+    @pl.when(pl.program_id(0) == 0)
+    def _():
+        fetch_columns(pieces, place, w, sems, 0, 1)
         for slot in range(2):
-            w[slot, pl.ds(features + RANK, PADDED - features - RANK), :] = jnp.zeros(
-                (PADDED - features - RANK, width), jnp.bfloat16
-            )
+            clear_tail(w.at[slot], features)
         for block in blocks_of(rows):
             normed_in, _, _ = norm_forward(x_ref[block, :].astype(jnp.float32), gain[...], shift[...])
             first = normed_in.astype(jnp.bfloat16)
@@ -152,36 +164,75 @@
             low_ref[block, :] = low
             wide[block, :] = widen(first, low)
 
-    @pl.when(step + 1 < steps)
-    def _():
-        fetch(step + 1)
-
-    slot = lax.rem(step, 2)
-    wait_rows(w.at[slot], 0, features, pl.ds(0, width), sems.at[slot])
+    slot = next_columns(pieces, place, w, sems, features, 1)
     w[slot, pl.ds(features, RANK), :] = a_out[...]
     for block in blocks_of(rows):
-        part = (product(wide[block, :], w[slot]) + bias[...]).astype(jnp.bfloat16)
-
-        @pl.when(step == 0)
-        def _():
-            q_ref[block, :] = part
-
-        @pl.when(step > 0)
-        def _():
-            kv_ref[block, :] = part
-
-
-def qkv_call(place, x, gain, shift, bias, a_in, a_out, pieces):
+        kv_ref[block, :] = (product(wide[block, :], w[slot]) + bias[...]).astype(jnp.bfloat16)
+
+
+def fetch_columns(pieces, place, w, sems, c, offset=0):
+    width = w.shape[2]
+    columns = pl.ds(pl.multiple_of((c + offset) * width, 128), width)
+    start_columns(pieces, place, w.at[c % 2], columns, pl.ds(0, width), sems.at[c % 2])
+
+
+def next_columns(pieces, place, w, sems, features, offset=0):
+    step, steps = pl.program_id(0), pl.num_programs(0)
+
+    @pl.when(step + 1 < steps)
+    def _():
+        fetch_columns(pieces, place, w, sems, step + 1, offset)
+
+    slot = lax.rem(step, 2)
+    wait_rows(w.at[slot], 0, features, pl.ds(0, w.shape[2]), sems.at[slot])
+    return slot
+
+
+def clear_tail(w, features):
+    count = w.shape[0] - features - RANK
+    w[pl.ds(features + RANK, count), :] = jnp.zeros((count, w.shape[1]), jnp.bfloat16)
+
+
+def keys_call(place, x, gain, shift, bias, a_in, a_out, pieces):
     rows, features = x.shape
-    steps = 3
+    width = PADDED
+    third = lambda height: pl.BlockSpec((height, width), lambda c, *_: (0, c + 1))
+    return call(
+        keys_kernel, "keys", (2,), place, [x, gain, shift, bias, a_in, a_out], pieces,
+        [whole_of(x), whole_of(gain), whole_of(shift), third(1), picked(features), third(RANK)],
+        [out_of((rows, features), jnp.bfloat16), out_of((rows, RANK), jnp.bfloat16), out_of((rows, 2 * width), jnp.bfloat16)],
+        [whole_of(x), pl.BlockSpec((rows, RANK), lambda *_: (0, 0)), column_block(rows, width)],
+        [pltpu.VMEM((2, PADDED, width), jnp.bfloat16), pltpu.VMEM((rows, PADDED), jnp.bfloat16), pltpu.SemaphoreType.DMA((2,))],
+        rows * features * 2 * width,
+    )
+
+
+def queries_kernel(place, first_ref, low_ref, bias, a_out, *more):
+    pieces, (q_ref, w, sems) = more[:-3], more[-3:]
+    rows, features = first_ref.shape
+    width = w.shape[1]
+    halves = [pl.ds(0, width // 256 * 128), pl.ds(width // 256 * 128, width - width // 256 * 128)]
+    for half, columns in enumerate(halves):
+        start_columns(pieces, place, w, columns, columns, sems.at[half])
+    clear_tail(w, features)
+    w[pl.ds(features, RANK), :] = a_out[...]
+    for half, columns in enumerate(halves):
+        wait_rows(w, 0, features, columns, sems.at[half])
+        for block in blocks_of(rows):
+            wide = widen(first_ref[block, :], low_ref[block, :])
+            q_ref[block, columns] = (product(wide, w[:, columns]) + bias[:, columns]).astype(jnp.bfloat16)
+
+
+def queries_call(place, first, low, bias, a_out, pieces):
+    rows, features = first.shape
     width = PADDED
     return call(
-        qkv_kernel, "qkv", (steps,), place, [x, gain, shift, bias, a_in, a_out], pieces,
-        [whole_of(x), whole_of(gain), whole_of(shift), column_block(1, width), whole_of(a_in), column_block(RANK, width)],
-        [out_of((rows, features), jnp.bfloat16), out_of((rows, RANK), jnp.bfloat16), out_of((rows, width), jnp.bfloat16), out_of((rows, 2 * width), jnp.bfloat16)],
-        [whole_of(x), pl.BlockSpec((rows, RANK), lambda *_: (0, 0)), pl.BlockSpec((rows, width), lambda *_: (0, 0)),
-         pl.BlockSpec((rows, width), lambda c, *_: (0, jnp.maximum(c - 1, 0)))],
-        [pltpu.VMEM((2, PADDED, width), jnp.bfloat16), pltpu.VMEM((rows, PADDED), jnp.bfloat16), pltpu.SemaphoreType.DMA((2,))],
+        queries_kernel, "queries", (1,), place, [first, low, bias, a_out], pieces,
+        [whole_of(first), whole_of(low), column_block(1, width), column_block(RANK, width)],
+        out_of((rows, width), jnp.bfloat16),
+        column_block(rows, width),
+        [pltpu.VMEM((PADDED, width), jnp.bfloat16), pltpu.SemaphoreType.DMA((2,))],
+        rows * features * width,
     )
 
 
@@ -213,10 +264,11 @@
     rows, features = x.shape
     return call(
         out_kernel, "out", (rows // BLOCK,), place, [x, mixed, gain, shift, bias, a_in, a_out, u_in], pieces,
-        [row_block(features), row_block(PADDED)] + [whole_of(a) for a in (gain, shift, bias, a_in, a_out, u_in)],
+        [row_block(features), row_block(PADDED)] + [whole_of(a) for a in (gain, shift, bias)] + [picked(features)] * 3,
         [out_of((rows, features), jnp.float32), out_of((rows, features), jnp.bfloat16), out_of((rows, RANK), jnp.bfloat16), out_of((rows, RANK), jnp.bfloat16)],
         [row_block(features), row_block(features), row_block(RANK), row_block(RANK)],
         [pltpu.VMEM((PADDED, features), jnp.bfloat16), pltpu.SemaphoreType.DMA(())],
+        rows * features * features,
     )
 
 
@@ -226,28 +278,31 @@
         start_shard(pieces, place, distance, w, pl.ds(0, width), pl.ds(0, width), sems.at[place[distance]])
 
 
-def wait_down(step, w, sems):
+def wait_down(step, w, sems, first=0, last=None):
     shard_rows = w.shape[0] // SHARDS
+    last = w.shape[0] // FF_CHUNK if last is None else last
     for shard in range(SHARDS):
         first_step = max(0, -(-(shard * shard_rows - FF_CHUNK + 1) // FF_CHUNK))
+        first_step = min(max(first_step, first), last - 1)
 
         @pl.when(step == first_step)
         def _():
             wait_rows(w, shard * shard_rows, shard_rows, pl.ds(0, w.shape[1]), sems.at[shard])
 
 
-def active_grad_kernel(place, cot_ref, a_in, a_out, *more):
+def active_grad_kernel(first, last, place, cot_ref, a_in, a_out, *more):
     pieces, (g_ref, low_ref, w, sems) = more[:-4], more[-4:]
+    pieces = pieces[: len(pieces) - (2 if first else 0)]
     rows, features = cot_ref.shape
-    step = pl.program_id(0)
-
-    @pl.when(step == 0)
+    step = pl.program_id(0) + first
+
+    @pl.when(step == first)
     def _():
         fetch_down(pieces, place, w, sems)
         for block in blocks_of(rows):
             low_ref[block, :] = product_transposed(cot_ref[block, :], a_out[...]).astype(jnp.bfloat16)
 
-    wait_down(step, w, sems)
+    wait_down(step, w, sems, first, last)
     weight = w[pl.ds(pl.multiple_of(step * FF_CHUNK, FF_CHUNK), FF_CHUNK), :]
     for block in blocks_of(rows):
         g_ref[block, :] = (
@@ -255,15 +310,19 @@
         ).astype(jnp.bfloat16)
 
 
-def active_grad_call(place, cot, a_in, a_out, pieces):
+def active_grad_call(place, cot, a_in, a_out, pieces, first, last, written=()):
     rows, features = cot.shape
-    units = a_in.shape[1]
+    units = a_in.shape[2]
+    chunk = lambda height: pl.BlockSpec((height, FF_CHUNK), lambda c, *_: (0, c + first))
     return call(
-        active_grad_kernel, "active_grad", (units // FF_CHUNK,), place, [cot, a_in, a_out], pieces,
-        [whole_of(cot), column_block(RANK, FF_CHUNK), whole_of(a_out)],
+        partial(active_grad_kernel, first, last), "active_grad", (last - first,), place, [cot, a_in, a_out],
+        [*pieces, *written],
+        [whole_of(cot), picked(FF_CHUNK, lambda c: c + first), picked(features)],
         [out_of((rows, units), jnp.bfloat16), out_of((rows, RANK), jnp.bfloat16)],
-        [column_block(rows, FF_CHUNK), pl.BlockSpec((rows, RANK), lambda *_: (0, 0))],
+        [chunk(rows), pl.BlockSpec((rows, RANK), lambda *_: (0, 0))],
         [pltpu.VMEM((units, features), jnp.bfloat16), pltpu.SemaphoreType.DMA((SHARDS,))],
+        rows * features * FF_CHUNK * (last - first),
+        {4 + len(pieces) + place: place for place in range(len(written))},
     )
 
 
@@ -340,13 +399,14 @@
     return call(
         up_kernel, "up", (units // FF_CHUNK,), place, [second, up_low, g_active, g_low, bias, u_out, d_in], pieces,
         [whole_of(second), low_block, column_block(rows, FF_CHUNK), low_block,
-         column_block(1, FF_CHUNK), column_block(RANK, FF_CHUNK), column_block(RANK, FF_CHUNK)],
+         column_block(1, FF_CHUNK), picked(FF_CHUNK, lambda c: c), picked(FF_CHUNK, lambda c: c)],
         [out_of((rows, units), jnp.bfloat16), out_of((rows, PADDED), jnp.float32), out_of((rows, RANK), jnp.bfloat16),
          out_of((RANK, units), jnp.float32), out_of((RANK, units), jnp.float32)],
         [column_block(rows, FF_CHUNK), pl.BlockSpec((rows, PADDED), lambda *_: (0, 0)), low_block,
          column_block(RANK, FF_CHUNK), column_block(RANK, FF_CHUNK)],
         [pltpu.VMEM((2, PADDED, FF_CHUNK), jnp.bfloat16), pltpu.VMEM((rows, PADDED), jnp.bfloat16), pltpu.VMEM((rows, RANK), jnp.float32),
          pltpu.SemaphoreType.DMA((2,))],
+        2 * rows * features * units,
     )
 
 
@@ -403,10 +463,11 @@
         out_grad_kernel, "out_grad", (rows // BLOCK,), place,
         [acc, hidden, second, cot, mixed, low, down_low, gain, u_in, a_in, a_out], pieces,
         [row_block(PADDED), row_block(features), row_block(features), row_block(features), row_block(PADDED),
-         row_block(RANK), row_block(RANK)] + [whole_of(a) for a in (gain, u_in, a_in, a_out)],
+         row_block(RANK), row_block(RANK), whole_of(gain)] + [picked(features)] * 3,
         [out_of((rows, features), jnp.float32), out_of((rows, PADDED), jnp.bfloat16)] + [out_of((RANK, features), jnp.float32)] * 4,
         [row_block(features), row_block(PADDED)] + [small] * 4,
         [pltpu.VMEM((PADDED, features), jnp.bfloat16), pltpu.SemaphoreType.DMA(())],
+        rows * features * features,
     )
 
 
@@ -429,7 +490,7 @@
     @pl.when(step == steps - 1)
     def _():
         for block in blocks_of(rows):
-            out_ref[block, :] = (hidden_ref[block, :] + acc[block, :]).astype(jnp.bfloat16)
+            out_ref[:, block] = (hidden_ref[block, :] + acc[block, :]).astype(jnp.bfloat16).T
 
 
 def down_call(place, active, hidden, down_low, bias, a_out, pieces):
@@ -438,10 +499,11 @@
     return call(
         down_kernel, "down", (units // FF_CHUNK,), place, [active, hidden, down_low, bias, a_out], pieces,
         [column_block(rows, FF_CHUNK), whole_of(hidden), pl.BlockSpec((rows, RANK), lambda *_: (0, 0)),
-         whole_of(bias), whole_of(a_out)],
-        out_of((rows, features), jnp.bfloat16),
-        pl.BlockSpec((rows, features), lambda *_: (0, 0)),
+         whole_of(bias), picked(features)],
+        out_of((features, rows), jnp.bfloat16),
+        pl.BlockSpec((features, rows), lambda *_: (0, 0)),
         [pltpu.VMEM((units, features), jnp.bfloat16), pltpu.VMEM((rows, features), jnp.float32), pltpu.SemaphoreType.DMA((SHARDS,))],
+        rows * features * units,
     )
 
 
@@ -495,7 +557,7 @@
             g_low = acc[block, pl.ds(features, RANK)].astype(jnp.bfloat16)
             g_first = acc[block, pl.ds(0, features)] + product(g_low, a_in[...])
             _, normed, inverse = norm_forward(x_ref[block, :].astype(jnp.float32), gain[...], 0.0)
-            out_ref[block, :] = g_hidden_ref[block, :] + norm_backward(g_first, normed, inverse, gain[...])
+            out_ref[:, block] = (g_hidden_ref[block, :] + norm_backward(g_first, normed, inverse, gain[...])).T
             term = product_outer(g_low, first_ref[block, :])
             qkv_in_sum = term if qkv_in_sum is None else qkv_in_sum + term
         g_qkv_in[...] = qkv_in_sum
@@ -508,13 +570,66 @@
     far_block = pl.BlockSpec((None, rows, PADDED), lambda c, *_: (jnp.maximum(c - 1, 0), 0, 0))
     return call(
         tokens_grad_kernel, "tokens_grad", (steps,), place, [x, first, low, g_hidden, gain, a_in, a_out, near, far], pieces,
-        [whole_of(x), whole_of(first), whole_of(low), whole_of(g_hidden), whole_of(gain), whole_of(a_in),
+        [whole_of(x), whole_of(first), whole_of(low), whole_of(g_hidden), whole_of(gain), picked(features),
          column_block(RANK, PADDED), near_block, far_block],
-        [out_of((rows, features), jnp.float32), out_of((RANK, steps * PADDED), jnp.float32), out_of((RANK, features), jnp.float32)],
-        [pl.BlockSpec((rows, features), lambda *_: (0, 0)), column_block(RANK, PADDED),
+        [out_of((features, rows), jnp.float32), out_of((RANK, steps * PADDED), jnp.float32), out_of((RANK, features), jnp.float32)],
+        [pl.BlockSpec((features, rows), lambda *_: (0, 0)), column_block(RANK, PADDED),
          pl.BlockSpec((RANK, features), lambda *_: (0, 0))],
         [pltpu.VMEM((2, PADDED, PADDED), jnp.bfloat16), pltpu.VMEM((rows, PADDED), jnp.float32), pltpu.SemaphoreType.DMA((2,))],
-    )
+        rows * features * steps * PADDED,
+    )
+
+
+def combine_kernel(widths, numbers, *refs):
+    parts, totals = refs[: -len(widths)], refs[-len(widths) :]
+    sequences, _, part_width = parts[0].shape
+    half_width = part_width - 128
+
+    def add(halves):
+        start = 0
+        for total, spans in zip(totals, widths):
+            into = 0
+            for width in spans:
+                done = 0
+                while done < width:
+                    half, at = divmod(start + done, half_width)
+                    size = min(width - done, half_width - at)
+                    for sequence in range(sequences):
+                        target = (numbers[sequence], slice(None), pl.ds(into + done, size))
+                        total[target] += halves[half][sequence, :, pl.ds(at, size)].astype(jnp.float32)
+                    done += size
+                into += width
+                start += -(-width // 128) * 128
+
+    for total in totals:
+        total[...] = jnp.zeros_like(total)
+    turned = numbers[sequences]
+
+    @pl.when(turned == 0)
+    def _():
+        add(parts)
+
+    if len(parts) == 2:
+        @pl.when(turned == 1)
+        def _():
+            add(parts[::-1])
+
+
+def combine_call(numbers, parts, widths):
+    shapes = [(ADAPTERS, RANK, sum(spans)) for spans in widths]
+    return pl.pallas_call(
+        partial(combine_kernel, widths),
+        grid_spec=pltpu.PrefetchScalarGridSpec(
+            num_scalar_prefetch=1,
+            grid=(1,),
+            in_specs=[whole_of(part) for part in parts],
+            out_specs=[pl.BlockSpec(shape, lambda *_: (0, 0, 0)) for shape in shapes],
+        ),
+        out_shape=[out_of(shape, jnp.float32) for shape in shapes],
+        compiler_params=pltpu.CompilerParams(vmem_limit_bytes=VMEM_LIMIT),
+        cost_estimate=pl.CostEstimate(flops=1 << 30, bytes_accessed=1 << 22, transcendentals=0),
+        name="combine",
+    )(numbers, *parts)
 
 
 TILE = 256
@@ -566,7 +681,9 @@
     return near_ref[pl.ds((tile - REACH_TILES) * TILE, TILE), :]
 
 
-def attend_forward_kernel(tiles, meta, q_ref, k_far, v_far, k_near, v_near, o_ref, lse_ref, bias_scr, acc_scr):
+def attend_forward_kernel(tiles, meta, q_ref, k_far, v_far, k_near, v_near, *more):
+    o_ref, lse_ref, bias_scr, acc_scr = more[-4:]
+
     @pl.when(pl.program_id(0) == 0)
     def _():
         fill_biases(meta, bias_scr, tiles)
@@ -599,19 +716,27 @@
     return pl.BlockSpec((rows, 128), lambda j, *_: (0, offset + j))
 
 
-def attend_forward(meta, queries, far, near):
+def attention_cost(products, pairs, rows):
+    macs = products * pairs * 2 * rows * SPAN_TILES * TILE * 256
+    return pl.CostEstimate(flops=2 * macs, bytes_accessed=1 << 24, transcendentals=0)
+
+
+def attend_forward(meta, queries, far, near, start, pairs, written=()):
     rows = queries.shape[0]
     tiles = rows // TILE
     return pl.pallas_call(
         partial(attend_forward_kernel, tiles),
         grid_spec=pltpu.PrefetchScalarGridSpec(
             num_scalar_prefetch=1,
-            grid=(PAIRS,),
+            grid=(pairs,),
             in_specs=[
-                pair_columns(rows), pair_columns(WINDOW), pair_columns(WINDOW, PAIRS),
-                pair_columns(rows), pair_columns(rows, PAIRS),
+                pair_columns(rows, start), pair_columns(WINDOW, start), pair_columns(WINDOW, PAIRS + start),
+                pair_columns(rows, start), pair_columns(rows, PAIRS + start),
+            ] + [pl.BlockSpec(memory_space=pl.ANY)] * len(written),
+            out_specs=[
+                pair_columns(rows, start),
+                pl.BlockSpec((None, 2 * rows, 128), lambda j, *_: (start + j, 0, 0)),
             ],
-            out_specs=[pair_columns(rows), pl.BlockSpec((None, 2 * rows, 128), lambda j, *_: (j, 0, 0))],
             scratch_shapes=[
                 pltpu.VMEM((tiles * SPAN_TILES, TILE, TILE), jnp.float32),
                 pltpu.VMEM((2 * TILE, 128), jnp.float32),
@@ -621,9 +746,11 @@
             jax.ShapeDtypeStruct((rows, PADDED), jnp.bfloat16),
             jax.ShapeDtypeStruct((PAIRS, 2 * rows, 128), jnp.float32),
         ],
+        input_output_aliases={6 + place: place for place in range(len(written))},
         compiler_params=pltpu.CompilerParams(vmem_limit_bytes=VMEM_LIMIT),
+        cost_estimate=attention_cost(2, pairs, rows),
         name="attend_forward",
-    )(meta, queries, far, far, near, near)
+    )(meta, queries, far, far, near, near, *written)
 
 
 def attend_backward_kernel(
@@ -696,6 +823,7 @@
             jax.ShapeDtypeStruct((2, WINDOW, PADDED), jnp.bfloat16),
         ],
         compiler_params=pltpu.CompilerParams(vmem_limit_bytes=VMEM_LIMIT),
+        cost_estimate=attention_cost(5, PAIRS, rows),
         name="attend_backward",
     )(meta, queries, far, far, near, near, grad_mixed, mixed, lse)
 
@@ -725,40 +853,70 @@
     return lax.ppermute(array, "ctx", pairs)
 
 
-def place_of():
+def place_of(chosen):
     chip, core, shard = lax.axis_index("dp"), lax.axis_index("ctx") % 2, lax.axis_index("wt")
     places = [(shard - distance) % SHARDS for distance in range(SHARDS)]
     for side in (core, 1 - core):
         near = jnp.where(side == 0, chip ^ 1, chip ^ 2)
         for where in (chip, near, near ^ 3, chip ^ 3):
             places.append(where * 2 + side)
-    return jnp.stack(places).astype(jnp.int32)
-
-
-def gather_shards(sizes, own, extra):
+    return jnp.stack([*places, chosen]).astype(jnp.int32)
+
+
+def after(array, *others):
+    return lax.optimization_barrier((array, *others))[0]
+
+
+def after_all(arrays, *others):
+    return lax.optimization_barrier((*arrays, *others))[: len(arrays)]
+
+
+def own_part(own):
     rows = own.shape[0] // (PARTS * 16) * 16
-    index = lax.axis_index("dp") * 2 + lax.axis_index("ctx") % 2
-    moved = lax.dynamic_slice_in_dim(own, index * rows, rows, 0)
-    moved = jnp.concatenate([moved, own[PARTS * rows :]] + extra, axis=0)
+    chip, core = lax.axis_index("dp"), lax.axis_index("ctx") % 2
+    left = own.shape[0] - PARTS * rows
+    first = PARTS * rows
+    if left > RANK:
+        left //= SHARDS
+        first += chip * left
+    mine = lax.dynamic_slice_in_dim(own, (chip * 2 + core) * rows, rows, 0)
+    return jnp.concatenate([mine, lax.dynamic_slice_in_dim(own, first, left, 0)], axis=0)
+
+
+def eighth(own, moved):
+    rows = own.shape[0] // (PARTS * 16) * 16
+    return moved if own.shape[0] - PARTS * rows > RANK else moved[:rows]
+
+
+def ring(sizes, moved):
     steps = []
     for _ in range(SHARDS - 1):
         moved = lax.ppermute(moved, "wt", ring_pairs(sizes["wt"]))
         steps.append(moved)
-    return rows, steps
-
-
-def spread_parts(sizes, own, rows, steps):
+    return steps
+
+
+def direct(sizes, moved):
+    size = sizes["wt"]
+    return [
+        lax.ppermute(moved, "wt", [(i, (i + distance) % size) for i in range(size)])
+        for distance in range(1, SHARDS)
+    ]
+
+
+def plane_start(sizes, mine):
     first, second = plane_pairs(sizes)
+    return [mine, lax.ppermute(mine, ("dp", "ctx"), first), lax.ppermute(mine, ("dp", "ctx"), second)]
+
+
+def plane_end(sizes, parts):
+    _, second = plane_pairs(sizes)
+    return [*parts, lax.ppermute(parts[1], ("dp", "ctx"), second)]
+
+
+def swap_cores(sizes, parts):
     swap = swap_pairs(sizes["ctx"])
-    mine = jnp.stack([step[:rows] for step in steps])
-    one = lax.ppermute(mine, ("dp", "ctx"), first)
-    two = lax.ppermute(mine, ("dp", "ctx"), second)
-    both = lax.ppermute(one, ("dp", "ctx"), second)
-    parts = [mine, one, two, both]
-    parts += [lax.ppermute(part, "ctx", swap) for part in parts]
-    left = own.shape[0] - PARTS * rows
-    rest = jnp.stack([step[rows : rows + left] for step in steps])
-    return [own, rest, *parts]
+    return [*parts, *[lax.ppermute(part, "ctx", swap) for part in parts]]
 
 
 def pad_thirds(array, features):
@@ -769,24 +927,37 @@
     return jnp.concatenate(pieces, axis=-1)
 
 
-def summed_adapters(sizes, terms, chosen):
-    widths = [term.shape[1] for term in terms]
-    flat = jnp.concatenate(terms, axis=1)
-    if sizes["ctx"] == 2:
-        flat = flat + lax.ppermute(flat, "ctx", swap_pairs(2))
+def send_adapters(sizes, terms, chosen):
+    flat = jnp.concatenate(
+        [jnp.pad(term, ((0, 0), (0, -term.shape[1] % 128))) for term in terms], axis=1
+    )
+    paired = sizes["ctx"] == 2
+    if paired:
+        half = flat.shape[1] // 2
+        core = lax.axis_index("ctx")
+        kept = lax.dynamic_slice_in_dim(flat, core * half, half, 1)
+        given = lax.dynamic_slice_in_dim(flat, (1 - core) * half, half, 1)
+        flat = kept + lax.ppermute(given, "ctx", swap_pairs(2))
     else:
         flat = lax.psum(flat, "ctx")
     ids = jnp.broadcast_to(chosen.astype(jnp.bfloat16), (RANK, 128))
-    sent = jnp.concatenate([flat.astype(jnp.bfloat16), ids], axis=1)
-    everyone = lax.all_gather(sent, ("dp", "wt"), axis=0)
-    numbers = everyone[:, 0, sum(widths)].astype(jnp.int32)
-    selector = (jnp.arange(ADAPTERS, dtype=jnp.int32)[:, None] == numbers[None, :]).astype(jnp.bfloat16)
-    totals, start = [], 0
-    for width in widths:
-        part = everyone[:, :, start : start + width]
-        totals.append(jnp.einsum("as,srn->arn", selector, part, preferred_element_type=jnp.float32))
-        start += width
-    return totals
+    return jnp.concatenate([flat.astype(jnp.bfloat16), ids], axis=1)
+
+
+def share_adapters(sent):
+    return lax.all_gather(sent, ("dp", "wt"), axis=0)
+
+
+def sequence_numbers(sizes, everyone):
+    numbers = everyone[:, 0, -1].astype(jnp.int32)
+    turned = lax.axis_index("ctx") if sizes["ctx"] == 2 else 0
+    return jnp.concatenate([numbers, jnp.full((1,), turned, jnp.int32)])
+
+
+def both_halves(sizes, everyone):
+    if sizes["ctx"] != 2:
+        return [everyone]
+    return [everyone, lax.ppermute(everyone, "ctx", swap_pairs(2))]
 
 
 def shards(
@@ -816,33 +987,40 @@
     down_adapt_in,
     down_adapt_out,
 ):
-    values, upstream = tokens[0], cotangent[0]
-    row_count, feature_count = values.shape
+    row_count, feature_count = tokens.shape[1:]
     ctx = sizes["ctx"]
-    place = place_of()
+    chosen = adapter_ids[0, 0]
+    place = place_of(chosen)
 
     vectors = [first_gain, first_shift, qkv_bias, out_bias, second_gain, second_shift, up_bias, down_bias]
     lengths = [vector.shape[0] for vector in vectors]
-    own_qkv = pad_thirds(qkv_weight, feature_count)
     flat = jnp.concatenate(vectors)
-    extra_rows = 16
-    flat = jnp.pad(flat, (0, extra_rows * own_qkv.shape[1] - flat.shape[0])).reshape(extra_rows, -1)
-
-    rows_qkv, steps_qkv = gather_shards(sizes, own_qkv, [flat])
-    pieces_qkv = spread_parts(sizes, own_qkv, rows_qkv, steps_qkv)
-    later = lax.optimization_barrier((out_weight, down_weight, up_weight, steps_qkv[-1]))
-    out_own, down_own, up_own = later[:3]
-    gathered = [gather_shards(sizes, out_own, [])]
-    down_own, _ = lax.optimization_barrier((down_own, gathered[-1][1][-1]))
-    gathered.append(gather_shards(sizes, down_own, []))
-    up_own, _ = lax.optimization_barrier((up_own, gathered[-1][1][-1]))
-    gathered.append(gather_shards(sizes, up_own, []))
-    pieces_out = spread_parts(sizes, out_own, *gathered[0])
-    pieces_down = spread_parts(sizes, down_own, *gathered[1])
-    pieces_up = spread_parts(sizes, up_own, *gathered[2])
-
-    extra_start = own_qkv.shape[0] - (PARTS - 1) * rows_qkv
-    by_distance = jnp.stack([flat] + [step[extra_start:] for step in steps_qkv])
+    extra_rows = -(-flat.shape[0] // (3 * PADDED))
+    flat = jnp.pad(flat, (0, extra_rows * 3 * PADDED - flat.shape[0])).reshape(extra_rows, -1)
+
+    part_qkv = jnp.concatenate([pad_thirds(own_part(qkv_weight), feature_count), flat], axis=0)
+    steps_qkv = ring(sizes, part_qkv)
+    parts_qkv = []
+    for step in steps_qkv:
+        parts_qkv += swap_cores(sizes, plane_end(sizes, plane_start(sizes, eighth(qkv_weight, step))))
+    own_qkv = pad_thirds(after(qkv_weight, steps_qkv[0]), feature_count)
+    pieces_qkv = [own_qkv, *steps_qkv, *parts_qkv]
+    values, adapter_qkv_out = after_all([tokens[0], qkv_adapt_out], steps_qkv[1])
+    upstream = after(cotangent[0], steps_qkv[-1])
+    adapter_qkv_out = pad_thirds(
+        lax.dynamic_index_in_dim(adapter_qkv_out, chosen, 0, keepdims=False), feature_count
+    )
+
+    def stacked(own, steps):
+        return jnp.stack([eighth(own, step) for step in steps])
+
+    steps_out = direct(sizes, after(own_part(out_weight), steps_qkv[-1]))
+    parts_out = plane_start(sizes, stacked(out_weight, steps_out))
+    part_down = own_part(down_weight)
+    folded = after(part_down.reshape(4, -1, feature_count), *steps_out)
+    turn = partial(lax.ppermute, axis_name="wt", perm=ring_pairs(sizes["wt"]))
+
+    by_distance = jnp.stack([flat] + [step[-extra_rows:] for step in steps_qkv])
     order = (lax.axis_index("wt") - jnp.arange(SHARDS)) % SHARDS
     by_shard = jnp.take(by_distance, order, axis=0).reshape(SHARDS, -1).astype(jnp.float32)
     vectors, start = [], 0
@@ -852,60 +1030,95 @@
     gain_one, shift_one, bias_qkv, bias_out, gain_two, shift_two, bias_up, bias_down = vectors
     bias_qkv = pad_thirds(bias_qkv, feature_count)
 
-    chosen = adapter_ids[0, 0]
-
-    def select(stacked):
-        return lax.dynamic_index_in_dim(stacked, chosen, 0, keepdims=False)
-
-    adapter_qkv_in = select(qkv_adapt_in)
-    adapter_qkv_out = pad_thirds(select(qkv_adapt_out), feature_count)
-    adapter_out_in = select(out_adapt_in)
-    adapter_out_out = select(out_adapt_out)
-    adapter_up_in = select(up_adapt_in)
-    adapter_up_out = select(up_adapt_out)
-    adapter_down_in = select(down_adapt_in)
-    adapter_down_out = select(down_adapt_out)
-
     first_query = lax.axis_index("ctx") * row_count
     meta = jnp.concatenate([jnp.cumsum(doc_lengths[0])[:3], first_query[None]]).astype(jnp.int32)
     reach = -(-WINDOW // row_count)
 
-    first_in, qkv_low, queries, near = qkv_call(
-        place, values, gain_one, shift_one, bias_qkv, adapter_qkv_in, adapter_qkv_out, pieces_qkv
-    )
+    first_in, qkv_low, near = keys_call(
+        place, after(values, upstream, *steps_out), gain_one, shift_one, bias_qkv, qkv_adapt_in, adapter_qkv_out, pieces_qkv
+    )
+    steps_down = [turn(folded)]
+    *parts_out[1:], steps_down[0], near = after_all([*parts_out[1:], steps_down[0], near], near)
+
     far = jnp.concatenate([shifted(near, ctx, offset) for offset in range(reach, 0, -1)], axis=0)
-    mixed, logsums = attend_forward(meta, queries, far, near)
+    every_up = lax.all_gather(after(own_part(up_weight), steps_down[0]), "wt", axis=0)
+    parts_out = plane_end(sizes, parts_out)
+    steps_down.append(turn(steps_down[0]))
+    queries = queries_call(
+        place, after(first_in, parts_out[1], steps_down[0]), qkv_low, bias_qkv, adapter_qkv_out, pieces_qkv
+    )
+    *parts_out[3:], steps_down[1] = after_all([*parts_out[3:], steps_down[1]], queries)
+
+    parts_out = swap_cores(sizes, parts_out)
+    steps_down.append(turn(steps_down[1]))
+    pairs = PAIRS // 2 + 1
+    written = attend_forward(meta, after(queries, parts_out[3], steps_down[1]), far, near, 0, pairs)
+    steps_down[2], *parts_out[4:] = after_all([steps_down[2], *parts_out[4:]], written[0])
+
+    steps_down = [step.reshape(part_down.shape) for step in steps_down]
+    parts_down = plane_start(sizes, stacked(down_weight, steps_down))
+    mixed, logsums = attend_forward(
+        meta, after(queries, steps_down[2]), far, near, pairs, PAIRS - pairs, written
+    )
+    *parts_down[1:], every_up = after_all([*parts_down[1:], every_up], mixed)
+
+    parts_down = plane_end(sizes, parts_down)
+    steps_up = [lax.dynamic_index_in_dim(every_up, place[k], 0, keepdims=False) for k in range(1, SHARDS)]
+    parts_up = plane_start(sizes, stacked(up_weight, steps_up))
+    pieces_out = [out_weight, *steps_out, *parts_out]
     hidden, second_in, out_low, up_low = out_call(
-        place, values, mixed, gain_two, shift_two, bias_out, adapter_out_in, adapter_out_out, adapter_up_in, pieces_out
-    )
-    grad_active, grad_down_low = active_grad_call(place, upstream, adapter_down_in, adapter_down_out, pieces_down)
+        place, values, after(mixed, *parts_down[1:3], every_up), gain_two, shift_two, bias_out, out_adapt_in,
+        out_adapt_out, up_adapt_in, pieces_out,
+    )
+    parts_down[3] = after(parts_down[3], hidden)
+
+    pieces_down = [down_weight, *steps_down, *swap_cores(sizes, parts_down)]
+    written = active_grad_call(
+        place, after(upstream, hidden), down_adapt_in, down_adapt_out, pieces_down, 0, 2
+    )
+    parts_up[1:] = after_all(parts_up[1:], written[0])
+    parts_up = plane_end(sizes, parts_up)
+    grad_active, grad_down_low = active_grad_call(
+        place, after(upstream, *parts_up[1:3]), down_adapt_in, down_adapt_out, pieces_down, 2, 5, written
+    )
+    parts_up[3] = after(parts_up[3], grad_active)
+    pieces_up = [up_weight, every_up, *swap_cores(sizes, parts_up)]
     active, grad_second, down_low, grad_up_out, grad_down_in = up_call(
-        place, second_in, up_low, grad_active, grad_down_low, bias_up, adapter_up_out, adapter_down_in, pieces_up
+        place, second_in, up_low, grad_active, grad_down_low, bias_up, up_adapt_out, down_adapt_in, pieces_up
     )
     grad_hidden, grad_mixed, grad_up_in, grad_out_out, grad_out_in, grad_down_out = out_grad_call(
         place, grad_second, hidden, second_in, upstream, mixed, out_low, down_low, gain_two,
-        adapter_up_in, adapter_out_in, adapter_out_out, pieces_out,
-    )
-    total_up_out, total_down_in, total_up_in, total_out_out, total_out_in, total_down_out = summed_adapters(
-        sizes, [grad_up_out, grad_down_in, grad_up_in, grad_out_out, grad_out_in, grad_down_out], chosen
-    )
-    near_grads, far_grads = attend_backward(meta, queries, far, near, grad_mixed, mixed, logsums)
-    output = down_call(place, active, hidden, down_low, bias_down, adapter_down_out, pieces_down)
+        up_adapt_in, out_adapt_in, out_adapt_out, pieces_out,
+    )
+    terms = [grad_up_out, grad_down_in, grad_up_in, grad_out_out, grad_out_in, grad_down_out]
+    widths = [(term.shape[1],) for term in terms]
+    sent = send_adapters(sizes, terms, chosen)
+    everyone = share_adapters(sent)
+    near_grads, far_grads = attend_backward(meta, queries, far, near, after(grad_mixed, sent), mixed, logsums)
+    everyone = after(everyone, near_grads)
     moved = 0
     for offset in range(reach, 0, -1):
         first_row = (reach - offset) * row_count
         moved += shifted(far_grads[:, first_row : first_row + row_count], ctx, -offset)
+    halves = both_halves(sizes, everyone)
+    numbers = sequence_numbers(sizes, everyone)
     grad_input, grad_qkv_out, grad_qkv_in = tokens_grad_call(
-        place, values, first_in, qkv_low, grad_hidden, gain_one, adapter_qkv_in, adapter_qkv_out,
-        near_grads, moved, pieces_qkv,
-    )
-    total_qkv_out, total_qkv_in = summed_adapters(sizes, [grad_qkv_out, grad_qkv_in], chosen)
-    total_qkv_out = jnp.concatenate(
-        [total_qkv_out[..., third * PADDED : third * PADDED + feature_count] for third in range(3)], axis=-1
-    )
+        place, values, first_in, qkv_low, grad_hidden, gain_one, qkv_adapt_in, adapter_qkv_out,
+        after(near_grads, everyone), moved, pieces_qkv,
+    )
+    last_sent = send_adapters(sizes, [grad_qkv_out, grad_qkv_in], chosen)
+    last_everyone = share_adapters(last_sent)
+    numbers, active = after_all([numbers, active], last_sent)
+    totals = combine_call(numbers, halves, widths)
+    total_up_out, total_down_in, total_up_in, total_out_out, total_out_in, total_down_out = totals
+    output = down_call(
+        place, after(active, *totals), hidden, down_low, bias_down, down_adapt_out, pieces_down
+    )
+    last_halves = both_halves(sizes, after(last_everyone, output))
+    total_qkv_out, total_qkv_in = combine_call(numbers, last_halves, [(feature_count,) * 3, (feature_count,)])
     return (
-        output[None],
-        grad_input[None],
+        output.T[None],
+        grad_input.T[None],
         total_qkv_in,
         total_qkv_out,
         total_out_in,

time: 1010 us -> 756 us (0.75)
  waiting for transfers between devices: 377 us -> 157 us
  local copies, waits for them, and re-layouts: 122 us -> 50.2 us
  Pallas kernels: 438 us -> 474 us
  starting transfers between devices: 23.1 us -> 38.7 us
    all_gather x2 -> x3, waiting for transfers between devices: 134 us -> 21.1 us  [the longest x2 21.1 us: share_adapters(): return lax.all_gather(sent, ('dp', 'wt'), axis=0)]
    ppermute x42 -> x55, waiting for transfers between devices: 231 us -> 128 us  [the longest x6 54.6 us: plane_start(): lax.ppermute(mine, ('dp', 'ctx'), first)]
    unnamed x94 -> x88, local copies, waits for them, and re-layouts: 52.4 us -> 21.3 us
    slice x17 -> x4, local copies, waits for them, and re-layouts: 20 us -> 2.44 us  [eighth(): return moved if own.shape[0] - PARTS * rows > RANK else moved[:rows]]
    pallas_call x0 -> x2, Pallas kernels: none -> 16.4 us  [combine_call(): pl.pallas_call(partial(combine_kernel, widths), grid_spec=pltpu.PrefetchS...]
    ppermute x42 -> x55, starting transfers between devices: 17.3 us -> 32.8 us  [the longest x6 7.26 us: plane_start(): lax.ppermute(mine, ('dp', 'ctx'), first)]
    pallas_call x7 -> x9, Pallas kernels: 278 us -> 292 us  [call(): pl.pallas_call(kernel, grid_spec=pltpu.PrefetchScalarGridSpec(num_scalar_...]
    pallas_call x1 -> x2, Pallas kernels: 53.7 us -> 59 us  [attend_forward(): pl.pallas_call(partial(attend_forward_kernel, tiles), grid_spec=pltpu.Pre...]
  transfers between devices with their start and end apart: 46 -> 60, of which waited for: 24 -> 21; matrix products, arithmetic and copies ran while one was open for 9% -> 6% of each run, Pallas kernels for 18% -> 48%
where the time goes in v3:
time: 756 us; the launch traced here: 750 us
  Pallas kernels  474 us (63%)
  waiting for transfers between devices  157 us (21%)
  local copies, waits for them, and re-layouts  50.2 us (7%)
  starting transfers between devices  38.7 us (5%)
  between operations  15.7 us (2%)
  other arithmetic  13.3 us (2%)
    pallas_call x9, Pallas kernels, call(): pl.pallas_call(kernel, grid_spec=pltpu.PrefetchScalarGridSpec(num_scalar_...  292 us
    pallas_call x1, Pallas kernels, attend_backward(): pl.pallas_call(partial(attend_backward_kernel, tiles), grid_spec=pltpu.Pr...  107 us
    pallas_call x2, Pallas kernels, attend_forward(): pl.pallas_call(partial(attend_forward_kernel, tiles), grid_spec=pltpu.Pre...  59 us
    ppermute x6, waiting for transfers between devices, plane_start(): lax.ppermute(mine, ('dp', 'ctx'), first)  54.6 us
    ppermute x3, waiting for transfers between devices, ring(): moved = lax.ppermute(moved, 'wt', ring_pairs(sizes['wt']))  29.2 us
    unnamed x88, local copies, waits for them, and re-layouts  21.3 us
    all_gather x2, waiting for transfers between devices, share_adapters(): return lax.all_gather(sent, ('dp', 'wt'), axis=0)  21.1 us
    pallas_call x2, Pallas kernels, combine_call(): pl.pallas_call(partial(combine_kernel, widths), grid_spec=pltpu.PrefetchS...  16.4 us
  transfers between devices with their start and end apart: 60, of which 21 were waited for; matrix products, arithmetic and copies ran while one was open for 6% of the time, Pallas kernels for 48%

profile of v3, /device:TPU:0, one launch (start us, length us, event | category | flops | bytes accessed | tf_op | source)
XLA Modules:
  0.0 749.9 jit_solution(6914561505390217659)
XLA Ops:
  20.0 5.5 copy.43
  42.1 8.9 %collective-permute-done.6.more_5_ = bf16[48,4992]{1,0:T(8,128)(2,1)} collective-permute-done((bf16[48,4992]{1,0:T(8,128)(2,1)}, bf16[48,4992]{1,0:T(8,128)(2,1)}, u32[]{:S(2)}, u32[]{:S(2)}) %collective-permute-start.6) | collective-permute-done | bytes 479264 | tf_op jit(solution)/shard_map/ppermute | solution.py:909
  51.9 8.4 %collective-permute-done.1.more_2_ = bf16[66,4992]{1,0:T(8,128)(2,1)S(1)} collective-permute-done((bf16[66,4992]{1,0:T(8,128)(2,1)S(1)}, bf16[66,4992]{1,0:T(8,128)(2,1)S(1)}, u32[]{:S(2)}, u32[]{:S(2)}) %collective-permute-start.1) | collective-permute-done | bytes 658976 | tf_op jit(solution)/shard_map/ppermute | solution.py:894
  61.3 18.7 %collective-permute-done.2.more_3_ = bf16[66,4992]{1,0:T(8,128)(2,1)S(1)} collective-permute-done((bf16[66,4992]{1,0:T(8,128)(2,1)S(1)}, bf16[66,4992]{1,0:T(8,128)(2,1)S(1)}, u32[]{:S(2)}, u32[]{:S(2)}) %collective-permute-start.2) | collective-permute-done | bytes 658976 | tf_op jit(solution)/shard_map/ppermute | solution.py:894
  85.1 8.3 %collective-permute-done.13.more_13_ = bf16[48,4992]{1,0:T(8,128)(2,1)S(1)} collective-permute-done((bf16[48,4992]{1,0:T(8,128)(2,1)S(1)}, bf16[48,4992]{1,0:T(8,128)(2,1)S(1)}, u32[]{:S(2)}, u32[]{:S(2)}) %collective-permute-start.13) | collective-permute-done | bytes 479264 | tf_op jit(solution)/shard_map/ppermute | solution.py:909
  102.7 6.2 collective-permute-done.4.more_2_
  129.3 23.2 %keys.1 = (bf16[1024,1600]{1,0:T(8,128)(2,1)}, bf16[1024,16]{1,0:T(8,128)(2,1)}, bf16[1024,3328]{1,0:T(8,128)(2,1)}) custom-call(s32[13]{0:T(128)} %stack.84.place, bf16[1024,1600]{1,0:T(8,128)(2,1)} %bitcast.59, f32[1,1600]{1,0:T(1,128)} %reshape.132.gain, f32[1,1600]{1,0:T(1,128)} %reshape.133.shift, f32[1,4992]{1,0:T(1,128)} %fusion.24.bias, ...), custom_call_target="tpu_custom_call" | custom-call | flops 10905190400 | bytes 4194304 | tf_op jit(solution)/shard_map/keys/pallas_call | solution.py:117
  163.7 13.0 %queries.1.q_ref = bf16[1024,1664]{1,0:T(8,128)(2,1)} custom-call(s32[13]{0:T(128)} %stack.84.place, bf16[1024,1600]{1,0:T(8,128)(2,1)} %get-tuple-element.99.first_ref, bf16[1024,16]{1,0:T(8,128)(2,1)} %get-tuple-element.100.low_ref, f32[1,4992]{1,0:T(1,128)} %fusion.24.bias, bf16[16,4992]{1,0:T(8,128)(2,1)} %fusion.22.a_out, ...), custom_call_target="tpu_custom_call" | custom-call | flops 5452595200 | bytes 4194304 | tf_op jit(solution)/shard_map/queries/pallas_call | solution.py:117
  176.9 7.5 collective-permute-done.31
  186.1 31.3 %attend_forward.2 = (bf16[1024,1664]{1,0:T(8,128)(2,1)}, f32[13,2048,128]{2,1,0:T(8,128)}) custom-call(s32[4]{0:T(128)} %pad_add_fusion.meta, bf16[1024,1664]{1,0:T(8,128)(2,1)} %queries.1.q_ref, bf16[1024,3328]{1,0:T(8,128)(2,1)} %collective-permute-done.37.k_far.v_far, bf16[1024,3328]{1,0:T(8,128)(2,1)} %collective-permute-done.37.k_far.v_far, ...), custom_call_target="tpu_custom_call" | custom-call | flops 18790481920 | bytes 16777216 | tf_op jit(solution)/shard_map/attend_forward/pallas_call | solution.py:727
  224.4 27.6 %attend_forward.3 = (bf16[1024,1664]{1,0:T(8,128)(2,1)}, f32[13,2048,128]{2,1,0:T(8,128)}) custom-call(s32[4]{0:T(128)} %pad_add_fusion.meta, bf16[1024,1664]{1,0:T(8,128)(2,1)} %queries.1.q_ref, bf16[1024,3328]{1,0:T(8,128)(2,1)} %collective-permute-done.37.k_far.v_far, ...), custom_call_target="tpu_custom_call", output_to_operand_aliasing={{0}: (6, {}), {1}: (7, {})} | custom-call | flops 16106127360 | bytes 16777216 | tf_op jit(solution)/shard_map/attend_forward/pallas_call | solution.py:727
  252.0 16.5 %collective-permute-done.38.more_5_ = bf16[3,208,1600]{2,1,0:T(8,128)(2,1)} collective-permute-done((bf16[3,208,1600]{2,1,0:T(8,128)(2,1)}, bf16[3,208,1600]{2,1,0:T(8,128)(2,1)}, u32[]{:S(2)}, u32[]{:S(2)}) %collective-permute-start.38) | collective-permute-done | bytes 1996832 | tf_op jit(solution)/shard_map/ppermute | solution.py:909
  271.4 18.3 %out.1 = (f32[1024,1600]{1,0:T(8,128)}, bf16[1024,1600]{1,0:T(8,128)(2,1)}, bf16[1024,16]{1,0:T(8,128)(2,1)}, bf16[1024,16]{1,0:T(8,128)(2,1)}) custom-call(s32[13]{0:T(128)} %stack.84.place, bf16[1024,1600]{1,0:T(8,128)(2,1)} %bitcast.60, bf16[1024,1664]{1,0:T(8,128)(2,1)} %get-tuple-element.115.mixed_ref.o_ref, f32[1,1600]{1,0:T(1,128)} %reshape.137.gain, ...), custom_call_target="tpu_custom_call" | custom-call | flops 5242880000 | bytes 4194304 | tf_op jit(solution)/shard_map/out/pallas_call | solution.py:117
  301.7 18.0 %active_grad.2 = (bf16[1024,6400]{1,0:T(8,128)(2,1)}, bf16[1024,16]{1,0:T(8,128)(2,1)}) custom-call(s32[13]{0:T(128)} %stack.84.place, bf16[1024,1600]{1,0:T(8,128)(2,1)} %bitcast.53, bf16[8,16,6400]{2,1,0:T(8,128)(2,1)} %d_in.1, bf16[8,16,1600]{2,1,0:T(8,128)(2,1)} %a_out.9, bf16[1600,1600]{1,0:T(8,128)(2,1)} %more_0_.11, ...), custom_call_target="tpu_custom_call" | custom-call | flops 8388608000 | bytes 4194304 | tf_op jit(solution)/shard_map/active_grad/pallas_call | solution.py:117
  319.8 20.8 %collective-permute-done.40.more_3_ = bf16[3,48,6400]{2,1,0:T(8,128)(2,1)} collective-permute-done((bf16[3,48,6400]{2,1,0:T(8,128)(2,1)}, bf16[3,48,6400]{2,1,0:T(8,128)(2,1)}, u32[]{:S(2)}, u32[]{:S(2)}) %collective-permute-start.40) | collective-permute-done | bytes 1843232 | tf_op jit(solution)/shard_map/ppermute | solution.py:909
  342.1 28.2 %active_grad.3 = (bf16[1024,6400]{1,0:T(8,128)(2,1)}, bf16[1024,16]{1,0:T(8,128)(2,1)}) custom-call(s32[13]{0:T(128)} %stack.84.place, bf16[1024,1600]{1,0:T(8,128)(2,1)} %bitcast.54, bf16[8,16,6400]{2,1,0:T(8,128)(2,1)} %d_in.1, bf16[8,16,1600]{2,1,0:T(8,128)(2,1)} %a_out.9, ...), custom_call_target="tpu_custom_call", output_to_operand_aliasing={{0}: (16, {}), {1}: (17, {})} | custom-call | flops 12582912000 | bytes 4194304 | tf_op jit(solution)/shard_map/active_grad/pallas_call | solution.py:117
  374.3 84.1 %up.1 = (bf16[1024,6400]{1,0:T(8,128)(2,1)}, f32[1024,1664]{1,0:T(8,128)}, bf16[1024,16]{1,0:T(8,128)(2,1)}, f32[16,6400]{1,0:T(8,128)}, f32[16,6400]{1,0:T(8,128)}) custom-call(s32[13]{0:T(128)} %stack.84.place, bf16[1024,1600]{1,0:T(8,128)(2,1)} %get-tuple-element.120.second_ref, bf16[1024,16]{1,0:T(8,128)(2,1)} %get-tuple-element.121.up_low_ref, ...), custom_call_target="tpu_custom_call" | custom-call | flops 41943040000 | bytes 4194304 | tf_op jit(solution)/shard_map/up/pallas_call | solution.py:117
  460.5 24.5 %out_grad.1 = (f32[1024,1600]{1,0:T(8,128)}, bf16[1024,1664]{1,0:T(8,128)(2,1)}, f32[16,1600]{1,0:T(8,128)}, f32[16,1600]{1,0:T(8,128)}, f32[16,1600]{1,0:T(8,128)}, /*index=5*/f32[16,1600]{1,0:T(8,128)}) custom-call(s32[13]{0:T(128)} %stack.84.place, f32[1024,1664]{1,0:T(8,128)} %get-tuple-element.135.acc_ref, f32[1024,1600]{1,0:T(8,128)} %get-tuple-element.122.hidden_ref, ...), custom_call_target="tpu_custom_call" | custom-call | flops 5242880000 | bytes 4194304 | tf_op jit(solution)/shard_map/out_grad/pallas_call | solution.py:117
  491.7 106.7 %attend_backward.1 = (bf16[3,1024,1664]{2,1,0:T(8,128)(2,1)}, bf16[2,1024,1664]{2,1,0:T(8,128)(2,1)}) custom-call(s32[4]{0:T(128)} %pad_add_fusion.meta, bf16[1024,1664]{1,0:T(8,128)(2,1)} %queries.1.q_ref, bf16[1024,3328]{1,0:T(8,128)(2,1)} %collective-permute-done.37.k_far.v_far, bf16[1024,3328]{1,0:T(8,128)(2,1)} %collective-permute-done.37.k_far.v_far, ...), custom_call_target="tpu_custom_call" | custom-call | flops 87241523200 | bytes 16777216 | tf_op jit(solution)/shard_map/attend_backward/pallas_call | solution.py:800
  603.5 7.9 %collective-permute-done.53.far_ref = bf16[2,1024,1664]{2,1,0:T(8,128)(2,1)} collective-permute-done((bf16[2,1024,1664]{2,1,0:T(8,128)(2,1)}, bf16[2,1024,1664]{2,1,0:T(8,128)(2,1)}, u32[]{:S(2)}, u32[]{:S(2)}) %collective-permute-start.53) | collective-permute-done | bytes 6815776 | tf_op jit(solution)/shard_map/ppermute | solution.py:853
  611.5 48.1 %tokens_grad.1 = (f32[1600,1024]{1,0:T(8,128)}, f32[16,4992]{1,0:T(8,128)}, f32[16,1600]{1,0:T(8,128)}) custom-call(s32[13]{0:T(128)} %stack.84.place, bf16[1024,1600]{1,0:T(8,128)(2,1)} %bitcast.61, bf16[1024,1600]{1,0:T(8,128)(2,1)} %get-tuple-element.99.first_ref, bf16[1024,16]{1,0:T(8,128)(2,1)} %get-tuple-element.100.low_ref, ...), custom_call_target="tpu_custom_call" | custom-call | flops 16357785600 | bytes 4194304 | tf_op jit(solution)/shard_map/tokens_grad/pallas_call | solution.py:117
  665.4 11.0 %combine.2 = (f32[8,16,6400]{2,1,0:T(8,128)}, f32[8,16,6400]{2,1,0:T(8,128)}, f32[8,16,1600]{2,1,0:T(8,128)}, f32[8,16,1600]{2,1,0:T(8,128)}, f32[8,16,1600]{2,1,0:T(8,128)}, /*index=5*/f32[8,16,1600]{2,1,0:T(8,128)}) custom-call(s32[17]{0:T(128)} %pad_add_fusion.1.numbers, bf16[16,16,9856]{2,1,0:T(8,128)(2,1)} %bitcast.58, ...), custom_call_target="tpu_custom_call" | custom-call | flops 1073741824 | bytes 4194304 | tf_op jit(solution)/shard_map/combine/pallas_call | solution.py:620
  676.4 35.0 %down.1 = bf16[1600,1024]{1,0:T(8,128)(2,1)} custom-call(s32[13]{0:T(128)} %stack.84.place, bf16[1024,6400]{1,0:T(8,128)(2,1)} %get-tuple-element.161.active_ref, f32[1024,1600]{1,0:T(8,128)} %get-tuple-element.122.hidden_ref, bf16[1024,16]{1,0:T(8,128)(2,1)} %get-tuple-element.137.down_low_ref, f32[1,1600]{1,0:T(1,128)} %reshape.143.bias, ...), custom_call_target="tpu_custom_call" | custom-call | flops 20971520000 | bytes 4194304 | tf_op jit(solution)/shard_map/down/pallas_call | solution.py:117
  711.4 21.1 %all-gather.11.cloned.1.call-done = bf16[256,3456]{1,0:T(8,128)(2,1)} async-done(((bf16[16,3456]{1,0:T(8,128)(2,1)}), bf16[256,3456]{1,0:T(8,128)(2,1)}) %all-gather.11.cloned.1.call-update) | async-done | bytes 1769488 | tf_op jit(solution)/shard_map/all_gather | solution.py:948
  (287 shorter events, 135.2 us)
Async XLA Ops:
  7.3 244.7 %all-gather.7.cloned.1.call-start = ((), (), s32[]{:S(2)}) async-start(), calls=%async_computation | async-start | bytes 4096000 | tf_op jit(solution)/shard_map/all_gather | solution.py:1044
  40.0 41.9 %collective-permute-start.9 = (bf16[48,4992]{1,0:T(8,128)(2,1)}, bf16[48,4992]{1,0:T(8,128)(2,1)}, u32[]{:S(2)}, u32[]{:S(2)}) collective-permute-start(bf16[48,4992]{1,0:T(8,128)(2,1)} %slice.165.more_4_), channel_id=1, source_target_pairs={{0,4},{4,0},{1,5},{5,1},{2,6},{6,2},{3,7},{7,3},{8,12},{12,8},{9,1... | collective-permute-start | bytes 1437704 | tf_op jit(solution)/shard_map/ppermute | solution.py:919
  51.1 31.4 %collective-permute-start.8 = (bf16[48,4992]{1,0:T(8,128)(2,1)}, bf16[48,4992]{1,0:T(8,128)(2,1)}, u32[]{:S(2)}, u32[]{:S(2)}) collective-permute-start(bf16[48,4992]{1,0:T(8,128)(2,1)} %collective-permute-done.6.more_5_), channel_id=1, source_target_pairs={{0,16},{4,12},{8,24},{12,4},{16,0},{20,28},{24,8},{28,20},{1,17},{... | collective-permute-start | bytes 1437704 | tf_op jit(solution)/shard_map/ppermute | solution.py:914
  51.4 31.1 %collective-permute-start.10 = (bf16[48,4992]{1,0:T(8,128)(2,1)}, bf16[48,4992]{1,0:T(8,128)(2,1)}, u32[]{:S(2)}, u32[]{:S(2)}) collective-permute-start(bf16[48,4992]{1,0:T(8,128)(2,1)} %collective-permute-done.6.more_5_), channel_id=1, source_target_pairs={{0,4},{4,0},{1,5},{5,1},{2,6},{6,2},{3,7},{7,3},{8,12},{12,8},{9,1... | collective-permute-start | bytes 1437704 | tf_op jit(solution)/shard_map/ppermute | solution.py:919
  51.4 31.7 %collective-permute-start.11 = (bf16[48,4992]{1,0:T(8,128)(2,1)}, bf16[48,4992]{1,0:T(8,128)(2,1)}, u32[]{:S(2)}, u32[]{:S(2)}) collective-permute-start(bf16[48,4992]{1,0:T(8,128)(2,1)} %collective-permute-done.7.more_6_), channel_id=1, source_target_pairs={{0,4},{4,0},{1,5},{5,1},{2,6},{6,2},{3,7},{7,3},{8,12},{12,8},{9,1... | collective-permute-start | bytes 1437704 | tf_op jit(solution)/shard_map/ppermute | solution.py:919
  152.6 33.5 %collective-permute-start.37 = (bf16[1024,3328]{1,0:T(8,128)(2,1)}, bf16[1024,3328]{1,0:T(8,128)(2,1)}, u32[]{:S(2)}, u32[]{:S(2)}) collective-permute-start(bf16[1024,3328]{1,0:T(8,128)(2,1)} %get-tuple-element.105.k_near.v_near), channel_id=1, source_target_pairs={{0,4},{1,5},{2,6},{3,7},{8,12},{9,13},{10,14},{11,15},{16,20},{17,... | collective-permute-start | bytes 20447240 | tf_op jit(solution)/shard_map/ppermute | solution.py:853
  159.8 57.6 %collective-permute-start.33 = (bf16[3,48,1600]{2,1,0:T(8,128)(2,1)S(1)}, bf16[3,48,1600]{2,1,0:T(8,128)(2,1)}, u32[]{:S(2)}, u32[]{:S(2)}) collective-permute-start(bf16[3,48,1600]{2,1,0:T(8,128)(2,1)S(1)} %pad_maximum_fusion.3.more_4_), channel_id=1, source_target_pairs={{0,4},{4,0},{1,5},{5,1},{2,6},{6,2},{3,7},{7,3},{8,12},{12,8},{9,1... | collective-permute-start | bytes 1382408 | tf_op jit(solution)/shard_map/ppermute | solution.py:919
  161.2 56.2 %collective-permute-start.34 = (bf16[3,48,1600]{2,1,0:T(8,128)(2,1)}, bf16[3,48,1600]{2,1,0:T(8,128)(2,1)}, u32[]{:S(2)}, u32[]{:S(2)}) collective-permute-start(bf16[3,48,1600]{2,1,0:T(8,128)(2,1)} %collective-permute-done.27.more_5_), channel_id=1, source_target_pairs={{0,4},{4,0},{1,5},{5,1},{2,6},{6,2},{3,7},{7,3},{8,12},{12,8},{9,1... | collective-permute-start | bytes 1382408 | tf_op jit(solution)/shard_map/ppermute | solution.py:919
  162.6 437.1 %all-gather.9.cloned.1.call-start = ((), (), s32[]{:S(2)}) async-start(), calls=%async_computation.1 | async-start | bytes 5361664 | tf_op jit(solution)/shard_map/all_gather | solution.py:948
  176.8 40.7 %collective-permute-start.35 = (bf16[3,48,1600]{2,1,0:T(8,128)(2,1)}, bf16[3,48,1600]{2,1,0:T(8,128)(2,1)}, u32[]{:S(2)}, u32[]{:S(2)}) collective-permute-start(bf16[3,48,1600]{2,1,0:T(8,128)(2,1)} %collective-permute-done.28.more_6_), channel_id=1, source_target_pairs={{0,4},{4,0},{1,5},{5,1},{2,6},{6,2},{3,7},{7,3},{8,12},{12,8},{9,1... | collective-permute-start | bytes 1382408 | tf_op jit(solution)/shard_map/ppermute | solution.py:919
  184.4 34.9 %collective-permute-start.32 = (bf16[4,52,1600]{2,0,1:T(4,128)(2,1)S(1)}, bf16[4,52,1600]{2,0,1:T(4,128)(2,1)}, u32[]{:S(2)}, u32[]{:S(2)}) collective-permute-start(bf16[4,52,1600]{2,0,1:T(4,128)(2,1)S(1)} %collective-permute-done.31), channel_id=1, source_target_pairs={{0,1},{1,2},{2,3},{3,0},{4,5},{5,6},{6,7},{7,4},{8,9},{9,10},{10,1... | collective-permute-start | bytes 1996808 | tf_op jit(solution)/shard_map/ppermute | solution.py:1053
  186.1 31.4 %collective-permute-start.36 = (bf16[3,48,1600]{2,1,0:T(8,128)(2,1)}, bf16[3,48,1600]{2,1,0:T(8,128)(2,1)S(1)}, u32[]{:S(2)}, u32[]{:S(2)}) collective-permute-start(bf16[3,48,1600]{2,1,0:T(8,128)(2,1)} %collective-permute-done.30.more_7_), channel_id=1, source_target_pairs={{0,4},{4,0},{1,5},{5,1},{2,6},{6,2},{3,7},{7,3},{8,12},{12,8},{9,1... | collective-permute-start | bytes 1382408 | tf_op jit(solution)/shard_map/ppermute | solution.py:919
  221.7 46.8 %collective-permute-start.38 = (bf16[3,208,1600]{2,1,0:T(8,128)(2,1)}, bf16[3,208,1600]{2,1,0:T(8,128)(2,1)}, u32[]{:S(2)}, u32[]{:S(2)}) collective-permute-start(bf16[3,208,1600]{2,1,0:T(8,128)(2,1)} %constant_dynamic-update-slice_fusion.more_4_), channel_id=1, source_target_pairs={{0,8},{4,20},{8,0},{12,28},{16,24},{20,4},{24,16},{28,12},{1,9},{5... | collective-permute-start | bytes 5990408 | tf_op jit(solution)/shard_map/ppermute | solution.py:909
  223.2 45.3 %collective-permute-start.39 = (bf16[3,208,1600]{2,1,0:T(8,128)(2,1)}, bf16[3,208,1600]{2,1,0:T(8,128)(2,1)}, u32[]{:S(2)}, u32[]{:S(2)}) collective-permute-start(bf16[3,208,1600]{2,1,0:T(8,128)(2,1)} %constant_dynamic-update-slice_fusion.more_4_), channel_id=1, source_target_pairs={{0,16},{4,12},{8,24},{12,4},{16,0},{20,28},{24,8},{28,20},{1,17},{... | collective-permute-start | bytes 5990408 | tf_op jit(solution)/shard_map/ppermute | solution.py:909
  270.8 30.9 %collective-permute-start.44 = (bf16[3,208,1600]{2,1,0:T(8,128)(2,1)}, bf16[3,208,1600]{2,1,0:T(8,128)(2,1)}, u32[]{:S(2)}, u32[]{:S(2)}) collective-permute-start(bf16[3,208,1600]{2,1,0:T(8,128)(2,1)} %collective-permute-done.38.more_5_), channel_id=1, source_target_pairs={{0,4},{4,0},{1,5},{5,1},{2,6},{6,2},{3,7},{7,3},{8,12},{12,8},{9,1... | collective-permute-start | bytes 5990408 | tf_op jit(solution)/shard_map/ppermute | solution.py:919
  271.4 30.4 %collective-permute-start.45 = (bf16[3,208,1600]{2,1,0:T(8,128)(2,1)}, bf16[3,208,1600]{2,1,0:T(8,128)(2,1)}, u32[]{:S(2)}, u32[]{:S(2)}) collective-permute-start(bf16[3,208,1600]{2,1,0:T(8,128)(2,1)} %collective-permute-done.39.more_6_), channel_id=1, source_target_pairs={{0,4},{4,0},{1,5},{5,1},{2,6},{6,2},{3,7},{7,3},{8,12},{12,8},{9,1... | collective-permute-start | bytes 5990408 | tf_op jit(solution)/shard_map/ppermute | solution.py:919
  297.7 42.9 %collective-permute-start.40 = (bf16[3,48,6400]{2,1,0:T(8,128)(2,1)}, bf16[3,48,6400]{2,1,0:T(8,128)(2,1)}, u32[]{:S(2)}, u32[]{:S(2)}) collective-permute-start(bf16[3,48,6400]{2,1,0:T(8,128)(2,1)} %pad_maximum_fusion.more_2_), channel_id=1, source_target_pairs={{0,8},{4,20},{8,0},{12,28},{16,24},{20,4},{24,16},{28,12},{1,9},{5... | collective-permute-start | bytes 5529608 | tf_op jit(solution)/shard_map/ppermute | solution.py:909
  299.2 41.4 %collective-permute-start.41 = (bf16[3,48,6400]{2,1,0:T(8,128)(2,1)}, bf16[3,48,6400]{2,1,0:T(8,128)(2,1)}, u32[]{:S(2)}, u32[]{:S(2)}) collective-permute-start(bf16[3,48,6400]{2,1,0:T(8,128)(2,1)} %pad_maximum_fusion.more_2_), channel_id=1, source_target_pairs={{0,16},{4,12},{8,24},{12,4},{16,0},{20,28},{24,8},{28,20},{1,17},{... | collective-permute-start | bytes 5529608 | tf_op jit(solution)/shard_map/ppermute | solution.py:909
  340.6 29.7 %collective-permute-start.47 = (bf16[3,48,6400]{2,1,0:T(8,128)(2,1)}, bf16[3,48,6400]{2,1,0:T(8,128)(2,1)S(1)}, u32[]{:S(2)}, u32[]{:S(2)}) collective-permute-start(bf16[3,48,6400]{2,1,0:T(8,128)(2,1)} %collective-permute-done.40.more_3_), channel_id=1, source_target_pairs={{0,16},{4,12},{8,24},{12,4},{16,0},{20,28},{24,8},{28,20},{1,17},{... | collective-permute-start | bytes 5529608 | tf_op jit(solution)/shard_map/ppermute | solution.py:914
  340.9 30.5 %collective-permute-start.48 = (bf16[3,48,6400]{2,1,0:T(8,128)(2,1)}, bf16[3,48,6400]{2,1,0:T(8,128)(2,1)}, u32[]{:S(2)}, u32[]{:S(2)}) collective-permute-start(bf16[3,48,6400]{2,1,0:T(8,128)(2,1)} %pad_maximum_fusion.more_2_), channel_id=1, source_target_pairs={{0,4},{4,0},{1,5},{5,1},{2,6},{6,2},{3,7},{7,3},{8,12},{12,8},{9,1... | collective-permute-start | bytes 5529608 | tf_op jit(solution)/shard_map/ppermute | solution.py:919
  341.6 29.8 %collective-permute-start.49 = (bf16[3,48,6400]{2,1,0:T(8,128)(2,1)}, bf16[3,48,6400]{2,1,0:T(8,128)(2,1)}, u32[]{:S(2)}, u32[]{:S(2)}) collective-permute-start(bf16[3,48,6400]{2,1,0:T(8,128)(2,1)} %collective-permute-done.40.more_3_), channel_id=1, source_target_pairs={{0,4},{4,0},{1,5},{5,1},{2,6},{6,2},{3,7},{7,3},{8,12},{12,8},{9,1... | collective-permute-start | bytes 5529608 | tf_op jit(solution)/shard_map/ppermute | solution.py:919
  341.6 29.8 %collective-permute-start.50 = (bf16[3,48,6400]{2,1,0:T(8,128)(2,1)}, bf16[3,48,6400]{2,1,0:T(8,128)(2,1)}, u32[]{:S(2)}, u32[]{:S(2)}) collective-permute-start(bf16[3,48,6400]{2,1,0:T(8,128)(2,1)} %collective-permute-done.41.more_4_), channel_id=1, source_target_pairs={{0,4},{4,0},{1,5},{5,1},{2,6},{6,2},{3,7},{7,3},{8,12},{12,8},{9,1... | collective-permute-start | bytes 5529608 | tf_op jit(solution)/shard_map/ppermute | solution.py:919
  491.6 240.9 %all-gather.11.cloned.1.call-start = ((), (), s32[]{:S(2)}) async-start(), calls=%async_computation.2 | async-start | bytes 1880064 | tf_op jit(solution)/shard_map/all_gather | solution.py:948
  599.6 65.8 %collective-permute-start.55 = (bf16[16,16,9856]{2,1,0:T(8,128)(2,1)}, bf16[16,16,9856]{2,1,0:T(8,128)(2,1)}, u32[]{:S(2)}, u32[]{:S(2)}) collective-permute-start(bf16[16,16,9856]{2,1,0:T(8,128)(2,1)} %bitcast.56), channel_id=1, source_target_pairs={{0,4},{4,0},{1,5},{5,1},{2,6},{6,2},{3,7},{7,3},{8,12},{12,8},{9,1... | collective-permute-start | bytes 15138824 | tf_op jit(solution)/shard_map/ppermute | solution.py:960
  (78 other events, 1186.7 us)
Sparse Core Ops, SparseCore 0:
  162.7 85.0 all-gather.6
  491.7 93.9 all-gather.8
  663.0 69.4 all-gather.10

commit v4 on v3

--- a/solution.py
+++ b/solution.py
@@ -272,18 +272,26 @@
     )
 
 
-def fetch_down(pieces, place, w, sems):
+def fetch_down(pieces, place, w, sems, first=0, last=None):
     width = w.shape[1]
-    for distance in range(SHARDS):
-        start_shard(pieces, place, distance, w, pl.ds(0, width), pl.ds(0, width), sems.at[place[distance]])
+    shard_rows = w.shape[0] // SHARDS
+    last = w.shape[0] // FF_CHUNK if last is None else last
+    for shard in range(SHARDS):
+        if shard * shard_rows >= last * FF_CHUNK or (shard + 1) * shard_rows <= first * FF_CHUNK:
+            continue
+        for distance in range(SHARDS):
+            @pl.when(place[distance] == shard)
+            def _():
+                start_shard(pieces, place, distance, w, pl.ds(0, width), pl.ds(0, width), sems.at[shard])
 
 
 def wait_down(step, w, sems, first=0, last=None):
     shard_rows = w.shape[0] // SHARDS
     last = w.shape[0] // FF_CHUNK if last is None else last
     for shard in range(SHARDS):
-        first_step = max(0, -(-(shard * shard_rows - FF_CHUNK + 1) // FF_CHUNK))
-        first_step = min(max(first_step, first), last - 1)
+        if shard * shard_rows >= last * FF_CHUNK or (shard + 1) * shard_rows <= first * FF_CHUNK:
+            continue
+        first_step = max(first, -(-(shard * shard_rows - FF_CHUNK + 1) // FF_CHUNK))
 
         @pl.when(step == first_step)
         def _():
@@ -298,7 +306,7 @@
 
     @pl.when(step == first)
     def _():
-        fetch_down(pieces, place, w, sems)
+        fetch_down(pieces, place, w, sems, first, last)
         for block in blocks_of(rows):
             low_ref[block, :] = product_transposed(cot_ref[block, :], a_out[...]).astype(jnp.bfloat16)
 
@@ -331,7 +339,7 @@
 
 
 def up_kernel(place, second_ref, up_low_ref, g_active_ref, g_low_ref, bias, u_out, d_in, *more):
-    pieces, (active_ref, acc_ref, down_low_ref, g_up_out_ref, g_down_in_ref, w, wide, low_scr, sems) = more[:-9], more[-9:]
+    pieces, (active_ref, acc_ref, down_low_ref, g_up_out_ref, g_down_in_ref, w, wide, low_scr, g_scr, sems) = more[:-10], more[-10:]
     rows, features = second_ref.shape
     step, steps = pl.program_id(0), pl.num_programs(0)
     width = w.shape[2]
@@ -347,6 +355,8 @@
             w[slot, pl.ds(features + RANK, PADDED - features - RANK), :] = jnp.zeros(
                 (PADDED - features - RANK, width), jnp.bfloat16
             )
+        acc_ref[...] = jnp.zeros_like(acc_ref)
+        low_scr[...] = jnp.zeros_like(low_scr)
         for block in blocks_of(rows):
             wide[block, :] = widen(second_ref[block, :], up_low_ref[block, :])
 
@@ -357,35 +367,24 @@
     slot = lax.rem(step, 2)
     wait_rows(w.at[slot], 0, features, pl.ds(0, width), sems.at[slot])
     w[slot, pl.ds(features, RANK), :] = u_out[...]
-    up_out_sum, down_in_sum = None, None
-    for block in blocks_of(rows):
-        upper = product(wide[block, :], w[slot]) + bias[...]
+    blocks = blocks_of(rows)
+    ahead = product(wide[blocks[0], :], w[slot])
+    for number, block in enumerate(blocks):
+        upper = ahead + bias[...]
+        if number + 1 < len(blocks):
+            ahead = product(wide[blocks[number + 1], :], w[slot])
         square = upper * upper
-        inner = jnp.tanh((GELU_A * upper) * (1.0 + GELU_B * square))
-        half = 0.5 * (1.0 + inner)
+        inner = jnp.tanh(upper * (GELU_A + (GELU_A * GELU_B) * square))
+        half = 0.5 + 0.5 * inner
         active = (upper * half).astype(jnp.bfloat16)
-        slope = half + (0.5 * GELU_A) * upper * (1.0 - inner * inner) * (1.0 + (3.0 * GELU_B) * square)
+        slope = half + upper * (1.0 - inner * inner) * (0.5 * GELU_A + (1.5 * GELU_A * GELU_B) * square)
         g_upper = (g_active_ref[block, :].astype(jnp.float32) * slope).astype(jnp.bfloat16)
         active_ref[block, :] = active
-        acc = product_transposed(g_upper, w[slot])
-        low = product_transposed(active, d_in[...])
-
-        @pl.when(step == 0)
-        def _():
-            acc_ref[block, :] = acc
-            low_scr[block, :] = low
-
-        @pl.when(step > 0)
-        def _():
-            acc_ref[block, :] += acc
-            low_scr[block, :] += low
-
-        up_out = product_outer(up_low_ref[block, :], g_upper)
-        down_in = product_outer(g_low_ref[block, :], active)
-        up_out_sum = up_out if up_out_sum is None else up_out_sum + up_out
-        down_in_sum = down_in if down_in_sum is None else down_in_sum + down_in
-    g_up_out_ref[...] = up_out_sum
-    g_down_in_ref[...] = down_in_sum
+        g_scr[block, :] = g_upper
+        acc_ref[block, :] += product_transposed(g_upper, w[slot])
+        low_scr[block, :] += product_transposed(active, d_in[...])
+    g_up_out_ref[...] = product_outer(up_low_ref[...], g_scr[...])
+    g_down_in_ref[...] = product_outer(g_low_ref[...], active_ref[...])
 
     @pl.when(step == steps - 1)
     def _():
@@ -405,7 +404,7 @@
         [column_block(rows, FF_CHUNK), pl.BlockSpec((rows, PADDED), lambda *_: (0, 0)), low_block,
          column_block(RANK, FF_CHUNK), column_block(RANK, FF_CHUNK)],
         [pltpu.VMEM((2, PADDED, FF_CHUNK), jnp.bfloat16), pltpu.VMEM((rows, PADDED), jnp.bfloat16), pltpu.VMEM((rows, RANK), jnp.float32),
-         pltpu.SemaphoreType.DMA((2,))],
+         pltpu.VMEM((rows, FF_CHUNK), jnp.bfloat16), pltpu.SemaphoreType.DMA((2,))],
         2 * rows * features * units,
     )
 
@@ -472,13 +471,15 @@
 
 
 def down_kernel(place, active_ref, hidden_ref, down_low_ref, bias, a_out, *more):
-    pieces, (out_ref, w, acc, sems) = more[:-4], more[-4:]
+    pieces, (out_ref, w, acc, hidden, sems, late) = more[:-6], more[-6:]
     rows, features = hidden_ref.shape
     step, steps = pl.program_id(0), pl.num_programs(0)
+    copy = pltpu.make_async_copy(hidden_ref, hidden, late)
 
     @pl.when(step == 0)
     def _():
         fetch_down(pieces, place, w, sems)
+        copy.start()
         for block in blocks_of(rows):
             acc[block, :] = product(down_low_ref[block, :], a_out[...]) + bias[...]
 
@@ -489,8 +490,9 @@
 
     @pl.when(step == steps - 1)
     def _():
+        copy.wait()
         for block in blocks_of(rows):
-            out_ref[:, block] = (hidden_ref[block, :] + acc[block, :]).astype(jnp.bfloat16).T
+            out_ref[:, block] = (hidden[block, :] + acc[block, :]).astype(jnp.bfloat16).T
 
 
 def down_call(place, active, hidden, down_low, bias, a_out, pieces):
@@ -498,68 +500,56 @@
     units = active.shape[1]
     return call(
         down_kernel, "down", (units // FF_CHUNK,), place, [active, hidden, down_low, bias, a_out], pieces,
-        [column_block(rows, FF_CHUNK), whole_of(hidden), pl.BlockSpec((rows, RANK), lambda *_: (0, 0)),
+        [column_block(rows, FF_CHUNK), HBM, pl.BlockSpec((rows, RANK), lambda *_: (0, 0)),
          whole_of(bias), picked(features)],
         out_of((features, rows), jnp.bfloat16),
         pl.BlockSpec((features, rows), lambda *_: (0, 0)),
-        [pltpu.VMEM((units, features), jnp.bfloat16), pltpu.VMEM((rows, features), jnp.float32), pltpu.SemaphoreType.DMA((SHARDS,))],
+        [pltpu.VMEM((units, features), jnp.bfloat16), pltpu.VMEM((rows, features), jnp.float32), pltpu.VMEM((rows, features), jnp.float32),
+         pltpu.SemaphoreType.DMA((SHARDS,)), pltpu.SemaphoreType.DMA(())],
         rows * features * units,
     )
 
 
 def tokens_grad_kernel(place, x_ref, first_ref, low_ref, g_hidden_ref, gain, a_in, a_out, near_ref, far_ref, *more):
-    pieces, (out_ref, g_qkv_out, g_qkv_in, w, acc, sems) = more[:-6], more[-6:]
+    pieces, (out_ref, g_qkv_out, g_qkv_in, w, acc, x, first, g_hidden, sems, late) = more[:-10], more[-10:]
     rows, features = x_ref.shape
     step, steps = pl.program_id(0), pl.num_programs(0)
-    width = w.shape[2]
-
-    def fetch(c):
-        columns = pl.ds(pl.multiple_of(c * width, 128), width)
-        start_columns(pieces, place, w.at[c % 2], columns, pl.ds(0, width), sems.at[c % 2])
+    pairs = ((x_ref, x), (first_ref, first), (g_hidden_ref, g_hidden))
+    copies = [pltpu.make_async_copy(*pair, late.at[number]) for number, pair in enumerate(pairs)]
 
     @pl.when(step == 0)
     def _():
-        fetch(0)
+        fetch_columns(pieces, place, w, sems, 0)
         for slot in range(2):
-            w[slot, pl.ds(features + RANK, PADDED - features - RANK), :] = jnp.zeros(
-                (PADDED - features - RANK, width), jnp.bfloat16
-            )
-
-    @pl.when(step + 1 < steps)
-    def _():
-        fetch(step + 1)
-
-    slot = lax.rem(step, 2)
-    wait_rows(w.at[slot], 0, features, pl.ds(0, width), sems.at[slot])
+            clear_tail(w.at[slot], features)
+        acc[...] = jnp.zeros_like(acc)
+
+    @pl.when(step == 1)
+    def _():
+        for copy in copies:
+            copy.start()
+
+    slot = next_columns(pieces, place, w, sems, features)
     w[slot, pl.ds(features, RANK), :] = a_out[...]
-    qkv_out_sum = None
+    scale = jnp.where(step > 0, 1.0, 0.0)
+    qkv_out_sum = jnp.zeros(g_qkv_out.shape, jnp.float32)
     for block in blocks_of(rows):
-        far = jnp.where(step > 0, far_ref[block, :].astype(jnp.float32), 0.0)
-        g = (near_ref[block, :].astype(jnp.float32) + far).astype(jnp.bfloat16)
-        back = product_transposed(g, w[slot])
-
-        @pl.when(step == 0)
-        def _():
-            acc[block, :] = back
-
-        @pl.when(step > 0)
-        def _():
-            acc[block, :] += back
-
-        term = product_outer(low_ref[block, :], g)
-        qkv_out_sum = term if qkv_out_sum is None else qkv_out_sum + term
+        g = (near_ref[block, :].astype(jnp.float32) + scale * far_ref[block, :].astype(jnp.float32)).astype(jnp.bfloat16)
+        acc[block, :] += product_transposed(g, w[slot])
+        qkv_out_sum += product_outer(low_ref[block, :], g)
     g_qkv_out[...] = qkv_out_sum
 
     @pl.when(step == steps - 1)
     def _():
-        qkv_in_sum = None
+        for copy in copies:
+            copy.wait()
+        qkv_in_sum = jnp.zeros((RANK, features), jnp.float32)
         for block in blocks_of(rows):
             g_low = acc[block, pl.ds(features, RANK)].astype(jnp.bfloat16)
             g_first = acc[block, pl.ds(0, features)] + product(g_low, a_in[...])
-            _, normed, inverse = norm_forward(x_ref[block, :].astype(jnp.float32), gain[...], 0.0)
-            out_ref[:, block] = (g_hidden_ref[block, :] + norm_backward(g_first, normed, inverse, gain[...])).T
-            term = product_outer(g_low, first_ref[block, :])
-            qkv_in_sum = term if qkv_in_sum is None else qkv_in_sum + term
+            _, normed, inverse = norm_forward(x[block, :].astype(jnp.float32), gain[...], 0.0)
+            out_ref[:, block] = (g_hidden[block, :] + norm_backward(g_first, normed, inverse, gain[...])).T
+            qkv_in_sum += product_outer(g_low, first[block, :])
         g_qkv_in[...] = qkv_in_sum
 
 
@@ -570,12 +560,14 @@
     far_block = pl.BlockSpec((None, rows, PADDED), lambda c, *_: (jnp.maximum(c - 1, 0), 0, 0))
     return call(
         tokens_grad_kernel, "tokens_grad", (steps,), place, [x, first, low, g_hidden, gain, a_in, a_out, near, far], pieces,
-        [whole_of(x), whole_of(first), whole_of(low), whole_of(g_hidden), whole_of(gain), picked(features),
+        [HBM, HBM, whole_of(low), HBM, whole_of(gain), picked(features),
          column_block(RANK, PADDED), near_block, far_block],
         [out_of((features, rows), jnp.float32), out_of((RANK, steps * PADDED), jnp.float32), out_of((RANK, features), jnp.float32)],
         [pl.BlockSpec((features, rows), lambda *_: (0, 0)), column_block(RANK, PADDED),
          pl.BlockSpec((RANK, features), lambda *_: (0, 0))],
-        [pltpu.VMEM((2, PADDED, PADDED), jnp.bfloat16), pltpu.VMEM((rows, PADDED), jnp.float32), pltpu.SemaphoreType.DMA((2,))],
+        [pltpu.VMEM((2, PADDED, PADDED), jnp.bfloat16), pltpu.VMEM((rows, PADDED), jnp.float32),
+         pltpu.VMEM((rows, features), jnp.bfloat16), pltpu.VMEM((rows, features), jnp.bfloat16), pltpu.VMEM((rows, features), jnp.float32),
+         pltpu.SemaphoreType.DMA((2,)), pltpu.SemaphoreType.DMA((3,))],
         rows * features * steps * PADDED,
     )
 

time: 756 us -> 736 us (0.974)
  Pallas kernels: 474 us -> 452 us
    pallas_call x9, Pallas kernels: 292 us -> 270 us  [call(): pl.pallas_call(kernel, grid_spec=pltpu.PrefetchScalarGridSpec(num_scalar_...]
  transfers between devices with their start and end apart: 60 -> 60, of which waited for: 21 -> 21; matrix products, arithmetic and copies ran while one was open for 6% -> 6% of each run, Pallas kernels for 48% -> 47%
where the time goes in v4:
time: 736 us; the launch traced here: 730 us
  Pallas kernels  452 us (61%)
  waiting for transfers between devices  159 us (22%)
  local copies, waits for them, and re-layouts  50.2 us (7%)
  starting transfers between devices  38.7 us (5%)
  between operations  15.7 us (2%)
  other arithmetic  13.3 us (2%)
    pallas_call x9, Pallas kernels, call(): pl.pallas_call(kernel, grid_spec=pltpu.PrefetchScalarGridSpec(num_scalar_...  270 us
    pallas_call x1, Pallas kernels, attend_backward(): pl.pallas_call(partial(attend_backward_kernel, tiles), grid_spec=pltpu.Pr...  107 us
    pallas_call x2, Pallas kernels, attend_forward(): pl.pallas_call(partial(attend_forward_kernel, tiles), grid_spec=pltpu.Pre...  59 us
    ppermute x6, waiting for transfers between devices, plane_start(): lax.ppermute(mine, ('dp', 'ctx'), first)  54.6 us
    ppermute x3, waiting for transfers between devices, ring(): moved = lax.ppermute(moved, 'wt', ring_pairs(sizes['wt']))  29.2 us
    all_gather x2, waiting for transfers between devices, share_adapters(): return lax.all_gather(sent, ('dp', 'wt'), axis=0)  23.2 us
    unnamed x88, local copies, waits for them, and re-layouts  21.3 us
    pallas_call x2, Pallas kernels, combine_call(): pl.pallas_call(partial(combine_kernel, widths), grid_spec=pltpu.PrefetchS...  16.5 us
  transfers between devices with their start and end apart: 60, of which 21 were waited for; matrix products, arithmetic and copies ran while one was open for 6% of the time, Pallas kernels for 47%

profile of v4, /device:TPU:0, one launch (start us, length us, event | category | flops | bytes accessed | tf_op | source)
XLA Modules:
  0.0 729.6 jit_solution(3669363632101261391)
XLA Ops:
  20.0 5.5 copy.43
  42.1 8.9 %collective-permute-done.6.more_5_ = bf16[48,4992]{1,0:T(8,128)(2,1)} collective-permute-done((bf16[48,4992]{1,0:T(8,128)(2,1)}, bf16[48,4992]{1,0:T(8,128)(2,1)}, u32[]{:S(2)}, u32[]{:S(2)}) %collective-permute-start.6) | collective-permute-done | bytes 479264 | tf_op jit(solution)/shard_map/ppermute | solution.py:901
  51.9 8.4 %collective-permute-done.1.more_2_ = bf16[66,4992]{1,0:T(8,128)(2,1)S(1)} collective-permute-done((bf16[66,4992]{1,0:T(8,128)(2,1)S(1)}, bf16[66,4992]{1,0:T(8,128)(2,1)S(1)}, u32[]{:S(2)}, u32[]{:S(2)}) %collective-permute-start.1) | collective-permute-done | bytes 658976 | tf_op jit(solution)/shard_map/ppermute | solution.py:886
  61.3 18.7 %collective-permute-done.2.more_3_ = bf16[66,4992]{1,0:T(8,128)(2,1)S(1)} collective-permute-done((bf16[66,4992]{1,0:T(8,128)(2,1)S(1)}, bf16[66,4992]{1,0:T(8,128)(2,1)S(1)}, u32[]{:S(2)}, u32[]{:S(2)}) %collective-permute-start.2) | collective-permute-done | bytes 658976 | tf_op jit(solution)/shard_map/ppermute | solution.py:886
  85.1 8.3 %collective-permute-done.13.more_13_ = bf16[48,4992]{1,0:T(8,128)(2,1)S(1)} collective-permute-done((bf16[48,4992]{1,0:T(8,128)(2,1)S(1)}, bf16[48,4992]{1,0:T(8,128)(2,1)S(1)}, u32[]{:S(2)}, u32[]{:S(2)}) %collective-permute-start.13) | collective-permute-done | bytes 479264 | tf_op jit(solution)/shard_map/ppermute | solution.py:901
  102.7 6.2 collective-permute-done.4.more_2_
  129.3 23.2 %keys.1 = (bf16[1024,1600]{1,0:T(8,128)(2,1)}, bf16[1024,16]{1,0:T(8,128)(2,1)}, bf16[1024,3328]{1,0:T(8,128)(2,1)}) custom-call(s32[13]{0:T(128)} %stack.84.place, bf16[1024,1600]{1,0:T(8,128)(2,1)} %bitcast.59, f32[1,1600]{1,0:T(1,128)} %reshape.132.gain, f32[1,1600]{1,0:T(1,128)} %reshape.133.shift, f32[1,4992]{1,0:T(1,128)} %fusion.24.bias, ...), custom_call_target="tpu_custom_call" | custom-call | flops 10905190400 | bytes 4194304 | tf_op jit(solution)/shard_map/keys/pallas_call | solution.py:117
  163.7 13.0 %queries.1.q_ref = bf16[1024,1664]{1,0:T(8,128)(2,1)} custom-call(s32[13]{0:T(128)} %stack.84.place, bf16[1024,1600]{1,0:T(8,128)(2,1)} %get-tuple-element.99.first_ref, bf16[1024,16]{1,0:T(8,128)(2,1)} %get-tuple-element.100.low_ref, f32[1,4992]{1,0:T(1,128)} %fusion.24.bias, bf16[16,4992]{1,0:T(8,128)(2,1)} %fusion.22.a_out, ...), custom_call_target="tpu_custom_call" | custom-call | flops 5452595200 | bytes 4194304 | tf_op jit(solution)/shard_map/queries/pallas_call | solution.py:117
  176.9 7.5 %collective-permute-done.31 = bf16[4,52,1600]{2,0,1:T(4,128)(2,1)S(1)} collective-permute-done((bf16[4,52,1600]{2,0,1:T(4,128)(2,1)S(1)}, bf16[4,52,1600]{2,0,1:T(4,128)(2,1)S(1)}, u32[]{:S(2)}, u32[]{:S(2)}) %collective-permute-start.31) | collective-permute-done | bytes 665632 | tf_op jit(solution)/shard_map/ppermute | solution.py:1038
  186.1 31.3 %attend_forward.2 = (bf16[1024,1664]{1,0:T(8,128)(2,1)}, f32[13,2048,128]{2,1,0:T(8,128)}) custom-call(s32[4]{0:T(128)} %pad_add_fusion.meta, bf16[1024,1664]{1,0:T(8,128)(2,1)} %queries.1.q_ref, bf16[1024,3328]{1,0:T(8,128)(2,1)} %collective-permute-done.37.k_far.v_far, bf16[1024,3328]{1,0:T(8,128)(2,1)} %collective-permute-done.37.k_far.v_far, ...), custom_call_target="tpu_custom_call" | custom-call | flops 18790481920 | bytes 16777216 | tf_op jit(solution)/shard_map/attend_forward/pallas_call | solution.py:719
  224.4 27.6 %attend_forward.3 = (bf16[1024,1664]{1,0:T(8,128)(2,1)}, f32[13,2048,128]{2,1,0:T(8,128)}) custom-call(s32[4]{0:T(128)} %pad_add_fusion.meta, bf16[1024,1664]{1,0:T(8,128)(2,1)} %queries.1.q_ref, bf16[1024,3328]{1,0:T(8,128)(2,1)} %collective-permute-done.37.k_far.v_far, ...), custom_call_target="tpu_custom_call", output_to_operand_aliasing={{0}: (6, {}), {1}: (7, {})} | custom-call | flops 16106127360 | bytes 16777216 | tf_op jit(solution)/shard_map/attend_forward/pallas_call | solution.py:719
  252.0 16.5 %collective-permute-done.38.more_5_ = bf16[3,208,1600]{2,1,0:T(8,128)(2,1)} collective-permute-done((bf16[3,208,1600]{2,1,0:T(8,128)(2,1)}, bf16[3,208,1600]{2,1,0:T(8,128)(2,1)}, u32[]{:S(2)}, u32[]{:S(2)}) %collective-permute-start.38) | collective-permute-done | bytes 1996832 | tf_op jit(solution)/shard_map/ppermute | solution.py:901
  271.4 18.3 %out.1 = (f32[1024,1600]{1,0:T(8,128)}, bf16[1024,1600]{1,0:T(8,128)(2,1)}, bf16[1024,16]{1,0:T(8,128)(2,1)}, bf16[1024,16]{1,0:T(8,128)(2,1)}) custom-call(s32[13]{0:T(128)} %stack.84.place, bf16[1024,1600]{1,0:T(8,128)(2,1)} %bitcast.60, bf16[1024,1664]{1,0:T(8,128)(2,1)} %get-tuple-element.115.mixed_ref.o_ref, f32[1,1600]{1,0:T(1,128)} %reshape.137.gain, ...), custom_call_target="tpu_custom_call" | custom-call | flops 5242880000 | bytes 4194304 | tf_op jit(solution)/shard_map/out/pallas_call | solution.py:117
  301.7 18.0 %active_grad.2 = (bf16[1024,6400]{1,0:T(8,128)(2,1)}, bf16[1024,16]{1,0:T(8,128)(2,1)}) custom-call(s32[13]{0:T(128)} %stack.84.place, bf16[1024,1600]{1,0:T(8,128)(2,1)} %bitcast.53, bf16[8,16,6400]{2,1,0:T(8,128)(2,1)} %d_in.1, bf16[8,16,1600]{2,1,0:T(8,128)(2,1)} %a_out.9, bf16[1600,1600]{1,0:T(8,128)(2,1)} %more_0_.11, ...), custom_call_target="tpu_custom_call" | custom-call | flops 8388608000 | bytes 4194304 | tf_op jit(solution)/shard_map/active_grad/pallas_call | solution.py:117
  319.7 20.8 %collective-permute-done.40.more_3_ = bf16[3,48,6400]{2,1,0:T(8,128)(2,1)} collective-permute-done((bf16[3,48,6400]{2,1,0:T(8,128)(2,1)}, bf16[3,48,6400]{2,1,0:T(8,128)(2,1)}, u32[]{:S(2)}, u32[]{:S(2)}) %collective-permute-start.40) | collective-permute-done | bytes 1843232 | tf_op jit(solution)/shard_map/ppermute | solution.py:901
  342.1 25.2 %active_grad.3 = (bf16[1024,6400]{1,0:T(8,128)(2,1)}, bf16[1024,16]{1,0:T(8,128)(2,1)}) custom-call(s32[13]{0:T(128)} %stack.84.place, bf16[1024,1600]{1,0:T(8,128)(2,1)} %bitcast.54, bf16[8,16,6400]{2,1,0:T(8,128)(2,1)} %d_in.1, bf16[8,16,1600]{2,1,0:T(8,128)(2,1)} %a_out.9, ...), custom_call_target="tpu_custom_call", output_to_operand_aliasing={{0}: (16, {}), {1}: (17, {})} | custom-call | flops 12582912000 | bytes 4194304 | tf_op jit(solution)/shard_map/active_grad/pallas_call | solution.py:117
  371.3 75.9 %up.1 = (bf16[1024,6400]{1,0:T(8,128)(2,1)}, f32[1024,1664]{1,0:T(8,128)}, bf16[1024,16]{1,0:T(8,128)(2,1)}, f32[16,6400]{1,0:T(8,128)}, f32[16,6400]{1,0:T(8,128)}) custom-call(s32[13]{0:T(128)} %stack.84.place, bf16[1024,1600]{1,0:T(8,128)(2,1)} %get-tuple-element.120.second_ref, bf16[1024,16]{1,0:T(8,128)(2,1)} %get-tuple-element.121.up_low_ref, ...), custom_call_target="tpu_custom_call" | custom-call | flops 41943040000 | bytes 4194304 | tf_op jit(solution)/shard_map/up/pallas_call | solution.py:117
  449.3 24.5 %out_grad.1 = (f32[1024,1600]{1,0:T(8,128)}, bf16[1024,1664]{1,0:T(8,128)(2,1)}, f32[16,1600]{1,0:T(8,128)}, f32[16,1600]{1,0:T(8,128)}, f32[16,1600]{1,0:T(8,128)}, /*index=5*/f32[16,1600]{1,0:T(8,128)}) custom-call(s32[13]{0:T(128)} %stack.84.place, f32[1024,1664]{1,0:T(8,128)} %get-tuple-element.135.acc_ref, f32[1024,1600]{1,0:T(8,128)} %get-tuple-element.122.hidden_ref, ...), custom_call_target="tpu_custom_call" | custom-call | flops 5242880000 | bytes 4194304 | tf_op jit(solution)/shard_map/out_grad/pallas_call | solution.py:117
  480.4 106.7 %attend_backward.1 = (bf16[3,1024,1664]{2,1,0:T(8,128)(2,1)}, bf16[2,1024,1664]{2,1,0:T(8,128)(2,1)}) custom-call(s32[4]{0:T(128)} %pad_add_fusion.meta, bf16[1024,1664]{1,0:T(8,128)(2,1)} %queries.1.q_ref, bf16[1024,3328]{1,0:T(8,128)(2,1)} %collective-permute-done.37.k_far.v_far, bf16[1024,3328]{1,0:T(8,128)(2,1)} %collective-permute-done.37.k_far.v_far, ...), custom_call_target="tpu_custom_call" | custom-call | flops 87241523200 | bytes 16777216 | tf_op jit(solution)/shard_map/attend_backward/pallas_call | solution.py:792
  592.3 7.9 %collective-permute-done.53.far_ref = bf16[2,1024,1664]{2,1,0:T(8,128)(2,1)} collective-permute-done((bf16[2,1024,1664]{2,1,0:T(8,128)(2,1)}, bf16[2,1024,1664]{2,1,0:T(8,128)(2,1)}, u32[]{:S(2)}, u32[]{:S(2)}) %collective-permute-start.53) | collective-permute-done | bytes 6815776 | tf_op jit(solution)/shard_map/ppermute | solution.py:845
  600.2 39.0 %tokens_grad.1 = (f32[1600,1024]{1,0:T(8,128)}, f32[16,4992]{1,0:T(8,128)}, f32[16,1600]{1,0:T(8,128)}) custom-call(s32[13]{0:T(128)} %stack.84.place, bf16[1024,1600]{1,0:T(8,128)(2,1)} %bitcast.61, bf16[1024,1600]{1,0:T(8,128)(2,1)} %get-tuple-element.99.first_ref, bf16[1024,16]{1,0:T(8,128)(2,1)} %get-tuple-element.100.low_ref, ...), custom_call_target="tpu_custom_call" | custom-call | flops 16357785600 | bytes 4194304 | tf_op jit(solution)/shard_map/tokens_grad/pallas_call | solution.py:117
  645.2 11.0 %combine.2 = (f32[8,16,6400]{2,1,0:T(8,128)}, f32[8,16,6400]{2,1,0:T(8,128)}, f32[8,16,1600]{2,1,0:T(8,128)}, f32[8,16,1600]{2,1,0:T(8,128)}, f32[8,16,1600]{2,1,0:T(8,128)}, /*index=5*/f32[8,16,1600]{2,1,0:T(8,128)}) custom-call(s32[17]{0:T(128)} %pad_add_fusion.1.numbers, bf16[16,16,9856]{2,1,0:T(8,128)(2,1)} %bitcast.58, ...), custom_call_target="tpu_custom_call" | custom-call | flops 1073741824 | bytes 4194304 | tf_op jit(solution)/shard_map/combine/pallas_call | solution.py:612
  656.2 32.9 %down.1 = bf16[1600,1024]{1,0:T(8,128)(2,1)} custom-call(s32[13]{0:T(128)} %stack.84.place, bf16[1024,6400]{1,0:T(8,128)(2,1)} %get-tuple-element.161.active_ref, f32[1024,1600]{1,0:T(8,128)} %get-tuple-element.122.hidden_ref, bf16[1024,16]{1,0:T(8,128)(2,1)} %get-tuple-element.137.down_low_ref, f32[1,1600]{1,0:T(1,128)} %reshape.143.bias, ...), custom_call_target="tpu_custom_call" | custom-call | flops 20971520000 | bytes 4194304 | tf_op jit(solution)/shard_map/down/pallas_call | solution.py:117
  689.1 23.2 %all-gather.11.cloned.1.call-done = bf16[256,3456]{1,0:T(8,128)(2,1)} async-done(((bf16[16,3456]{1,0:T(8,128)(2,1)}), bf16[256,3456]{1,0:T(8,128)(2,1)}) %all-gather.11.cloned.1.call-update) | async-done | bytes 1769488 | tf_op jit(solution)/shard_map/all_gather | solution.py:940
  (287 shorter events, 135.2 us)
Async XLA Ops:
  7.3 244.7 %all-gather.7.cloned.1.call-start = ((), (), s32[]{:S(2)}) async-start(), calls=%async_computation | async-start | bytes 4096000 | tf_op jit(solution)/shard_map/all_gather | solution.py:1036
  40.0 41.9 %collective-permute-start.9 = (bf16[48,4992]{1,0:T(8,128)(2,1)}, bf16[48,4992]{1,0:T(8,128)(2,1)}, u32[]{:S(2)}, u32[]{:S(2)}) collective-permute-start(bf16[48,4992]{1,0:T(8,128)(2,1)} %slice.165.more_4_), channel_id=1, source_target_pairs={{0,4},{4,0},{1,5},{5,1},{2,6},{6,2},{3,7},{7,3},{8,12},{12,8},{9,1... | collective-permute-start | bytes 1437704 | tf_op jit(solution)/shard_map/ppermute | solution.py:911
  51.1 31.4 %collective-permute-start.8 = (bf16[48,4992]{1,0:T(8,128)(2,1)}, bf16[48,4992]{1,0:T(8,128)(2,1)}, u32[]{:S(2)}, u32[]{:S(2)}) collective-permute-start(bf16[48,4992]{1,0:T(8,128)(2,1)} %collective-permute-done.6.more_5_), channel_id=1, source_target_pairs={{0,16},{4,12},{8,24},{12,4},{16,0},{20,28},{24,8},{28,20},{1,17},{... | collective-permute-start | bytes 1437704 | tf_op jit(solution)/shard_map/ppermute | solution.py:906
  51.4 31.1 %collective-permute-start.10 = (bf16[48,4992]{1,0:T(8,128)(2,1)}, bf16[48,4992]{1,0:T(8,128)(2,1)}, u32[]{:S(2)}, u32[]{:S(2)}) collective-permute-start(bf16[48,4992]{1,0:T(8,128)(2,1)} %collective-permute-done.6.more_5_), channel_id=1, source_target_pairs={{0,4},{4,0},{1,5},{5,1},{2,6},{6,2},{3,7},{7,3},{8,12},{12,8},{9,1... | collective-permute-start | bytes 1437704 | tf_op jit(solution)/shard_map/ppermute | solution.py:911
  51.4 31.7 %collective-permute-start.11 = (bf16[48,4992]{1,0:T(8,128)(2,1)}, bf16[48,4992]{1,0:T(8,128)(2,1)}, u32[]{:S(2)}, u32[]{:S(2)}) collective-permute-start(bf16[48,4992]{1,0:T(8,128)(2,1)} %collective-permute-done.7.more_6_), channel_id=1, source_target_pairs={{0,4},{4,0},{1,5},{5,1},{2,6},{6,2},{3,7},{7,3},{8,12},{12,8},{9,1... | collective-permute-start | bytes 1437704 | tf_op jit(solution)/shard_map/ppermute | solution.py:911
  123.0 29.5 %collective-permute-start.27 = (bf16[3,48,1600]{2,1,0:T(8,128)(2,1)S(1)}, bf16[3,48,1600]{2,1,0:T(8,128)(2,1)}, u32[]{:S(2)}, u32[]{:S(2)}) collective-permute-start(bf16[3,48,1600]{2,1,0:T(8,128)(2,1)S(1)} %pad_maximum_fusion.3.more_4_), channel_id=1, source_target_pairs={{0,8},{4,20},{8,0},{12,28},{16,24},{20,4},{24,16},{28,12},{1,9},{5... | collective-permute-start | bytes 1382408 | tf_op jit(solution)/shard_map/ppermute | solution.py:901
  123.8 28.8 %collective-permute-start.28 = (bf16[3,48,1600]{2,1,0:T(8,128)(2,1)S(1)}, bf16[3,48,1600]{2,1,0:T(8,128)(2,1)}, u32[]{:S(2)}, u32[]{:S(2)}) collective-permute-start(bf16[3,48,1600]{2,1,0:T(8,128)(2,1)S(1)} %pad_maximum_fusion.3.more_4_), channel_id=1, source_target_pairs={{0,16},{4,12},{8,24},{12,4},{16,0},{20,28},{24,8},{28,20},{1,17},{... | collective-permute-start | bytes 1382408 | tf_op jit(solution)/shard_map/ppermute | solution.py:901
  124.7 27.9 %collective-permute-start.29 = (bf16[4,52,1600]{2,0,1:T(4,128)(2,1)S(1)}, bf16[4,52,1600]{2,0,1:T(4,128)(2,1)S(1)}, u32[]{:S(2)}, u32[]{:S(2)}) collective-permute-start(bf16[4,52,1600]{2,0,1:T(4,128)(2,1)S(1)} %copy.44), channel_id=1, source_target_pairs={{0,1},{1,2},{2,3},{3,0},{4,5},{5,6},{6,7},{7,4},{8,9},{9,10},{10,1... | collective-permute-start | bytes 1996808 | tf_op jit(solution)/shard_map/ppermute | solution.py:1032
  152.6 33.5 %collective-permute-start.37 = (bf16[1024,3328]{1,0:T(8,128)(2,1)}, bf16[1024,3328]{1,0:T(8,128)(2,1)}, u32[]{:S(2)}, u32[]{:S(2)}) collective-permute-start(bf16[1024,3328]{1,0:T(8,128)(2,1)} %get-tuple-element.105.k_near.v_near), channel_id=1, source_target_pairs={{0,4},{1,5},{2,6},{3,7},{8,12},{9,13},{10,14},{11,15},{16,20},{17,... | collective-permute-start | bytes 20447240 | tf_op jit(solution)/shard_map/ppermute | solution.py:845
  159.8 57.6 %collective-permute-start.33 = (bf16[3,48,1600]{2,1,0:T(8,128)(2,1)S(1)}, bf16[3,48,1600]{2,1,0:T(8,128)(2,1)}, u32[]{:S(2)}, u32[]{:S(2)}) collective-permute-start(bf16[3,48,1600]{2,1,0:T(8,128)(2,1)S(1)} %pad_maximum_fusion.3.more_4_), channel_id=1, source_target_pairs={{0,4},{4,0},{1,5},{5,1},{2,6},{6,2},{3,7},{7,3},{8,12},{12,8},{9,1... | collective-permute-start | bytes 1382408 | tf_op jit(solution)/shard_map/ppermute | solution.py:911
  161.2 56.2 %collective-permute-start.34 = (bf16[3,48,1600]{2,1,0:T(8,128)(2,1)}, bf16[3,48,1600]{2,1,0:T(8,128)(2,1)}, u32[]{:S(2)}, u32[]{:S(2)}) collective-permute-start(bf16[3,48,1600]{2,1,0:T(8,128)(2,1)} %collective-permute-done.27.more_5_), channel_id=1, source_target_pairs={{0,4},{4,0},{1,5},{5,1},{2,6},{6,2},{3,7},{7,3},{8,12},{12,8},{9,1... | collective-permute-start | bytes 1382408 | tf_op jit(solution)/shard_map/ppermute | solution.py:911
  162.6 425.8 %all-gather.9.cloned.1.call-start = ((), (), s32[]{:S(2)}) async-start(), calls=%async_computation.1 | async-start | bytes 5361664 | tf_op jit(solution)/shard_map/all_gather | solution.py:940
  176.8 40.7 %collective-permute-start.35 = (bf16[3,48,1600]{2,1,0:T(8,128)(2,1)}, bf16[3,48,1600]{2,1,0:T(8,128)(2,1)}, u32[]{:S(2)}, u32[]{:S(2)}) collective-permute-start(bf16[3,48,1600]{2,1,0:T(8,128)(2,1)} %collective-permute-done.28.more_6_), channel_id=1, source_target_pairs={{0,4},{4,0},{1,5},{5,1},{2,6},{6,2},{3,7},{7,3},{8,12},{12,8},{9,1... | collective-permute-start | bytes 1382408 | tf_op jit(solution)/shard_map/ppermute | solution.py:911
  184.4 34.9 %collective-permute-start.32 = (bf16[4,52,1600]{2,0,1:T(4,128)(2,1)S(1)}, bf16[4,52,1600]{2,0,1:T(4,128)(2,1)}, u32[]{:S(2)}, u32[]{:S(2)}) collective-permute-start(bf16[4,52,1600]{2,0,1:T(4,128)(2,1)S(1)} %collective-permute-done.31), channel_id=1, source_target_pairs={{0,1},{1,2},{2,3},{3,0},{4,5},{5,6},{6,7},{7,4},{8,9},{9,10},{10,1... | collective-permute-start | bytes 1996808 | tf_op jit(solution)/shard_map/ppermute | solution.py:1045
  186.1 31.4 %collective-permute-start.36 = (bf16[3,48,1600]{2,1,0:T(8,128)(2,1)}, bf16[3,48,1600]{2,1,0:T(8,128)(2,1)S(1)}, u32[]{:S(2)}, u32[]{:S(2)}) collective-permute-start(bf16[3,48,1600]{2,1,0:T(8,128)(2,1)} %collective-permute-done.30.more_7_), channel_id=1, source_target_pairs={{0,4},{4,0},{1,5},{5,1},{2,6},{6,2},{3,7},{7,3},{8,12},{12,8},{9,1... | collective-permute-start | bytes 1382408 | tf_op jit(solution)/shard_map/ppermute | solution.py:911
  221.7 46.8 %collective-permute-start.38 = (bf16[3,208,1600]{2,1,0:T(8,128)(2,1)}, bf16[3,208,1600]{2,1,0:T(8,128)(2,1)}, u32[]{:S(2)}, u32[]{:S(2)}) collective-permute-start(bf16[3,208,1600]{2,1,0:T(8,128)(2,1)} %constant_dynamic-update-slice_fusion.more_4_), channel_id=1, source_target_pairs={{0,8},{4,20},{8,0},{12,28},{16,24},{20,4},{24,16},{28,12},{1,9},{5... | collective-permute-start | bytes 5990408 | tf_op jit(solution)/shard_map/ppermute | solution.py:901
  223.2 45.3 %collective-permute-start.39 = (bf16[3,208,1600]{2,1,0:T(8,128)(2,1)}, bf16[3,208,1600]{2,1,0:T(8,128)(2,1)}, u32[]{:S(2)}, u32[]{:S(2)}) collective-permute-start(bf16[3,208,1600]{2,1,0:T(8,128)(2,1)} %constant_dynamic-update-slice_fusion.more_4_), channel_id=1, source_target_pairs={{0,16},{4,12},{8,24},{12,4},{16,0},{20,28},{24,8},{28,20},{1,17},{... | collective-permute-start | bytes 5990408 | tf_op jit(solution)/shard_map/ppermute | solution.py:901
  270.8 28.3 %collective-permute-start.43 = (bf16[3,208,1600]{2,1,0:T(8,128)(2,1)}, bf16[3,208,1600]{2,1,0:T(8,128)(2,1)}, u32[]{:S(2)}, u32[]{:S(2)}) collective-permute-start(bf16[3,208,1600]{2,1,0:T(8,128)(2,1)} %constant_dynamic-update-slice_fusion.more_4_), channel_id=1, source_target_pairs={{0,4},{4,0},{1,5},{5,1},{2,6},{6,2},{3,7},{7,3},{8,12},{12,8},{9,1... | collective-permute-start | bytes 5990408 | tf_op jit(solution)/shard_map/ppermute | solution.py:911
  270.8 30.9 %collective-permute-start.44 = (bf16[3,208,1600]{2,1,0:T(8,128)(2,1)}, bf16[3,208,1600]{2,1,0:T(8,128)(2,1)}, u32[]{:S(2)}, u32[]{:S(2)}) collective-permute-start(bf16[3,208,1600]{2,1,0:T(8,128)(2,1)} %collective-permute-done.38.more_5_), channel_id=1, source_target_pairs={{0,4},{4,0},{1,5},{5,1},{2,6},{6,2},{3,7},{7,3},{8,12},{12,8},{9,1... | collective-permute-start | bytes 5990408 | tf_op jit(solution)/shard_map/ppermute | solution.py:911
  271.4 30.4 %collective-permute-start.45 = (bf16[3,208,1600]{2,1,0:T(8,128)(2,1)}, bf16[3,208,1600]{2,1,0:T(8,128)(2,1)}, u32[]{:S(2)}, u32[]{:S(2)}) collective-permute-start(bf16[3,208,1600]{2,1,0:T(8,128)(2,1)} %collective-permute-done.39.more_6_), channel_id=1, source_target_pairs={{0,4},{4,0},{1,5},{5,1},{2,6},{6,2},{3,7},{7,3},{8,12},{12,8},{9,1... | collective-permute-start | bytes 5990408 | tf_op jit(solution)/shard_map/ppermute | solution.py:911
  297.7 42.9 %collective-permute-start.40 = (bf16[3,48,6400]{2,1,0:T(8,128)(2,1)}, bf16[3,48,6400]{2,1,0:T(8,128)(2,1)}, u32[]{:S(2)}, u32[]{:S(2)}) collective-permute-start(bf16[3,48,6400]{2,1,0:T(8,128)(2,1)} %pad_maximum_fusion.more_2_), channel_id=1, source_target_pairs={{0,8},{4,20},{8,0},{12,28},{16,24},{20,4},{24,16},{28,12},{1,9},{5... | collective-permute-start | bytes 5529608 | tf_op jit(solution)/shard_map/ppermute | solution.py:901
  299.2 41.4 %collective-permute-start.41 = (bf16[3,48,6400]{2,1,0:T(8,128)(2,1)}, bf16[3,48,6400]{2,1,0:T(8,128)(2,1)}, u32[]{:S(2)}, u32[]{:S(2)}) collective-permute-start(bf16[3,48,6400]{2,1,0:T(8,128)(2,1)} %pad_maximum_fusion.more_2_), channel_id=1, source_target_pairs={{0,16},{4,12},{8,24},{12,4},{16,0},{20,28},{24,8},{28,20},{1,17},{... | collective-permute-start | bytes 5529608 | tf_op jit(solution)/shard_map/ppermute | solution.py:901
  480.4 231.9 %all-gather.11.cloned.1.call-start = ((), (), s32[]{:S(2)}) async-start(), calls=%async_computation.2 | async-start | bytes 1880064 | tf_op jit(solution)/shard_map/all_gather | solution.py:940
  588.4 56.7 %collective-permute-start.55 = (bf16[16,16,9856]{2,1,0:T(8,128)(2,1)}, bf16[16,16,9856]{2,1,0:T(8,128)(2,1)}, u32[]{:S(2)}, u32[]{:S(2)}) collective-permute-start(bf16[16,16,9856]{2,1,0:T(8,128)(2,1)} %bitcast.56), channel_id=1, source_target_pairs={{0,4},{4,0},{1,5},{5,1},{2,6},{6,2},{3,7},{7,3},{8,12},{12,8},{9,1... | collective-permute-start | bytes 15138824 | tf_op jit(solution)/shard_map/ppermute | solution.py:952
  (78 other events, 1176.9 us)
Sparse Core Ops, SparseCore 0:
  162.7 85.0 all-gather.6
  480.5 93.9 all-gather.8
  642.8 69.4 all-gather.10

commit v5 on v4

--- a/solution.py
+++ b/solution.py
@@ -329,7 +329,7 @@
         [out_of((rows, units), jnp.bfloat16), out_of((rows, RANK), jnp.bfloat16)],
         [chunk(rows), pl.BlockSpec((rows, RANK), lambda *_: (0, 0))],
         [pltpu.VMEM((units, features), jnp.bfloat16), pltpu.SemaphoreType.DMA((SHARDS,))],
-        rows * features * FF_CHUNK * (last - first),
+        rows * features * FF_CHUNK * (last - first) if first else RANK,
         {4 + len(pieces) + place: place for place in range(len(written))},
     )
 
@@ -992,9 +992,11 @@
 
     part_qkv = jnp.concatenate([pad_thirds(own_part(qkv_weight), feature_count), flat], axis=0)
     steps_qkv = ring(sizes, part_qkv)
-    parts_qkv = []
+    parts_qkv, before = [], []
     for step in steps_qkv:
-        parts_qkv += swap_cores(sizes, plane_end(sizes, plane_start(sizes, eighth(qkv_weight, step))))
+        parts = plane_start(sizes, after(eighth(qkv_weight, step), *before))
+        before = parts[1:]
+        parts_qkv += swap_cores(sizes, plane_end(sizes, parts))
     own_qkv = pad_thirds(after(qkv_weight, steps_qkv[0]), feature_count)
     pieces_qkv = [own_qkv, *steps_qkv, *parts_qkv]
     values, adapter_qkv_out = after_all([tokens[0], qkv_adapt_out], steps_qkv[1])
@@ -1043,7 +1045,7 @@
 
     parts_out = swap_cores(sizes, parts_out)
     steps_down.append(turn(steps_down[1]))
-    pairs = PAIRS // 2 + 1
+    pairs = PAIRS * 2 // 5
     written = attend_forward(meta, after(queries, parts_out[3], steps_down[1]), far, near, 0, pairs)
     steps_down[2], *parts_out[4:] = after_all([steps_down[2], *parts_out[4:]], written[0])
 

time: 736 us -> 751 us (1.020)
  starting transfers between devices: 38.7 us -> 51.1 us
    ppermute x6, waiting for transfers between devices: 54.6 us -> 31.9 us  [plane_start(): lax.ppermute(mine, ('dp', 'ctx'), first)]
    all_gather x2, waiting for transfers between devices: 23.2 us -> 30.8 us  [share_adapters(): return lax.all_gather(sent, ('dp', 'wt'), axis=0)]
    unnamed x88 -> x92, local copies, waits for them, and re-layouts: 21.3 us -> 20.6 us
  transfers between devices with their start and end apart: 60 -> 60, of which waited for: 21 -> 21; matrix products, arithmetic and copies ran while one was open for 6% -> 7% of each run, Pallas kernels for 47% -> 47%
where the time goes in v5:
time: 751 us; the launch traced here: 744 us
  Pallas kernels  452 us (60%)
  waiting for transfers between devices  162 us (22%)
  starting transfers between devices  51.1 us (7%)
  local copies, waits for them, and re-layouts  50.2 us (7%)
  between operations  15.8 us (2%)
  other arithmetic  13.2 us (2%)
    pallas_call x9, Pallas kernels, call(): pl.pallas_call(kernel, grid_spec=pltpu.PrefetchScalarGridSpec(num_scalar_...  270 us
    pallas_call x1, Pallas kernels, attend_backward(): pl.pallas_call(partial(attend_backward_kernel, tiles), grid_spec=pltpu.Pr...  107 us
    pallas_call x2, Pallas kernels, attend_forward(): pl.pallas_call(partial(attend_forward_kernel, tiles), grid_spec=pltpu.Pre...  58.9 us
    ppermute x3, waiting for transfers between devices, ring(): moved = lax.ppermute(moved, 'wt', ring_pairs(sizes['wt']))  33.6 us
    ppermute x6, waiting for transfers between devices, plane_start(): lax.ppermute(mine, ('dp', 'ctx'), first)  31.9 us
    all_gather x2, waiting for transfers between devices, share_adapters(): return lax.all_gather(sent, ('dp', 'wt'), axis=0)  30.8 us
    unnamed x92, local copies, waits for them, and re-layouts  20.6 us
    pallas_call x2, Pallas kernels, combine_call(): pl.pallas_call(partial(combine_kernel, widths), grid_spec=pltpu.PrefetchS...  16.5 us
  transfers between devices with their start and end apart: 60, of which 21 were waited for; matrix products, arithmetic and copies ran while one was open for 7% of the time, Pallas kernels for 47%

profile of v5, /device:TPU:0, one launch (start us, length us, event | category | flops | bytes accessed | tf_op | source)
XLA Modules:
  0.0 744.2 jit_solution(3835874234703008461)
XLA Ops:
  13.9 5.5 copy.42
  20.0 5.5 copy.43
  47.4 12.8 %collective-permute-done.1.more_2_ = bf16[66,4992]{1,0:T(8,128)(2,1)S(1)} collective-permute-done((bf16[66,4992]{1,0:T(8,128)(2,1)S(1)}, bf16[66,4992]{1,0:T(8,128)(2,1)S(1)}, u32[]{:S(2)}, u32[]{:S(2)}) %collective-permute-start.1) | collective-permute-done | bytes 658976 | tf_op jit(solution)/shard_map/ppermute | solution.py:886
  62.0 18.7 %collective-permute-done.2.more_3_ = bf16[66,4992]{1,0:T(8,128)(2,1)S(1)} collective-permute-done((bf16[66,4992]{1,0:T(8,128)(2,1)S(1)}, bf16[66,4992]{1,0:T(8,128)(2,1)S(1)}, u32[]{:S(2)}, u32[]{:S(2)}) %collective-permute-start.2) | collective-permute-done | bytes 658976 | tf_op jit(solution)/shard_map/ppermute | solution.py:886
  83.6 5.9 collective-permute-done.14.more_14_
  101.0 8.2 %collective-permute-done.4.more_2_ = bf16[64,1600]{1,0:T(8,128)(2,1)S(1)} collective-permute-done((bf16[64,1600]{1,0:T(8,128)(2,1)}, bf16[64,1600]{1,0:T(8,128)(2,1)S(1)}, u32[]{:S(2)}, u32[]{:S(2)}) %collective-permute-start.4) | collective-permute-done | bytes 204832 | tf_op jit(solution)/shard_map/ppermute | solution.py:894
  130.7 23.2 %keys.1 = (bf16[1024,1600]{1,0:T(8,128)(2,1)}, bf16[1024,16]{1,0:T(8,128)(2,1)}, bf16[1024,3328]{1,0:T(8,128)(2,1)}) custom-call(s32[13]{0:T(128)} %stack.84.place, bf16[1024,1600]{1,0:T(8,128)(2,1)} %bitcast.59, f32[1,1600]{1,0:T(1,128)} %reshape.132.gain, f32[1,1600]{1,0:T(1,128)} %reshape.133.shift, f32[1,4992]{1,0:T(1,128)} %fusion.24.bias, ...), custom_call_target="tpu_custom_call" | custom-call | flops 10905190400 | bytes 4194304 | tf_op jit(solution)/shard_map/keys/pallas_call | solution.py:117
  165.1 13.2 %queries.1.q_ref = bf16[1024,1664]{1,0:T(8,128)(2,1)} custom-call(s32[13]{0:T(128)} %stack.84.place, bf16[1024,1600]{1,0:T(8,128)(2,1)} %get-tuple-element.103.first_ref, bf16[1024,16]{1,0:T(8,128)(2,1)} %get-tuple-element.104.low_ref, f32[1,4992]{1,0:T(1,128)} %fusion.24.bias, bf16[16,4992]{1,0:T(8,128)(2,1)} %fusion.22.a_out, ...), custom_call_target="tpu_custom_call" | custom-call | flops 5452595200 | bytes 4194304 | tf_op jit(solution)/shard_map/queries/pallas_call | solution.py:117
  178.6 13.2 %collective-permute-done.31 = bf16[4,52,1600]{2,0,1:T(4,128)(2,1)} collective-permute-done((bf16[4,52,1600]{2,0,1:T(4,128)(2,1)S(1)}, bf16[4,52,1600]{2,0,1:T(4,128)(2,1)}, u32[]{:S(2)}, u32[]{:S(2)}) %collective-permute-start.31) | collective-permute-done | bytes 665632 | tf_op jit(solution)/shard_map/ppermute | solution.py:1040
  198.8 23.9 %attend_forward.2 = (bf16[1024,1664]{1,0:T(8,128)(2,1)}, f32[13,2048,128]{2,1,0:T(8,128)}) custom-call(s32[4]{0:T(128)} %pad_add_fusion.meta, bf16[1024,1664]{1,0:T(8,128)(2,1)} %queries.1.q_ref, bf16[1024,3328]{1,0:T(8,128)(2,1)} %collective-permute-done.37.k_far.v_far, bf16[1024,3328]{1,0:T(8,128)(2,1)} %collective-permute-done.37.k_far.v_far, ...), custom_call_target="tpu_custom_call" | custom-call | flops 13421772800 | bytes 16777216 | tf_op jit(solution)/shard_map/attend_forward/pallas_call | solution.py:719
  233.5 35.1 %attend_forward.3 = (bf16[1024,1664]{1,0:T(8,128)(2,1)}, f32[13,2048,128]{2,1,0:T(8,128)}) custom-call(s32[4]{0:T(128)} %pad_add_fusion.meta, bf16[1024,1664]{1,0:T(8,128)(2,1)} %queries.1.q_ref, bf16[1024,3328]{1,0:T(8,128)(2,1)} %collective-permute-done.37.k_far.v_far, ...), custom_call_target="tpu_custom_call", output_to_operand_aliasing={{0}: (6, {}), {1}: (7, {})} | custom-call | flops 21474836480 | bytes 16777216 | tf_op jit(solution)/shard_map/attend_forward/pallas_call | solution.py:719
  268.6 7.5 %collective-permute-done.38.more_5_ = bf16[3,208,1600]{2,1,0:T(8,128)(2,1)} collective-permute-done((bf16[3,208,1600]{2,1,0:T(8,128)(2,1)}, bf16[3,208,1600]{2,1,0:T(8,128)(2,1)}, u32[]{:S(2)}, u32[]{:S(2)}) %collective-permute-start.38) | collective-permute-done | bytes 1996832 | tf_op jit(solution)/shard_map/ppermute | solution.py:901
  280.2 18.3 %out.1 = (f32[1024,1600]{1,0:T(8,128)}, bf16[1024,1600]{1,0:T(8,128)(2,1)}, bf16[1024,16]{1,0:T(8,128)(2,1)}, bf16[1024,16]{1,0:T(8,128)(2,1)}) custom-call(s32[13]{0:T(128)} %stack.84.place, bf16[1024,1600]{1,0:T(8,128)(2,1)} %bitcast.60, bf16[1024,1664]{1,0:T(8,128)(2,1)} %get-tuple-element.119.mixed_ref.o_ref, f32[1,1600]{1,0:T(1,128)} %reshape.137.gain, ...), custom_call_target="tpu_custom_call" | custom-call | flops 5242880000 | bytes 4194304 | tf_op jit(solution)/shard_map/out/pallas_call | solution.py:117
  309.0 18.0 %active_grad.2 = (bf16[1024,6400]{1,0:T(8,128)(2,1)}, bf16[1024,16]{1,0:T(8,128)(2,1)}) custom-call(s32[13]{0:T(128)} %stack.84.place, bf16[1024,1600]{1,0:T(8,128)(2,1)} %bitcast.53, bf16[8,16,6400]{2,1,0:T(8,128)(2,1)} %d_in.1, bf16[8,16,1600]{2,1,0:T(8,128)(2,1)} %a_out.9, bf16[1600,1600]{1,0:T(8,128)(2,1)} %more_0_.11, ...), custom_call_target="tpu_custom_call" | custom-call | flops 32 | bytes 4194304 | tf_op jit(solution)/shard_map/active_grad/pallas_call | solution.py:117
  327.0 19.3 %collective-permute-done.40.more_3_ = bf16[3,48,6400]{2,1,0:T(8,128)(2,1)} collective-permute-done((bf16[3,48,6400]{2,1,0:T(8,128)(2,1)}, bf16[3,48,6400]{2,1,0:T(8,128)(2,1)}, u32[]{:S(2)}, u32[]{:S(2)}) %collective-permute-start.40) | collective-permute-done | bytes 1843232 | tf_op jit(solution)/shard_map/ppermute | solution.py:901
  348.9 25.2 %active_grad.3 = (bf16[1024,6400]{1,0:T(8,128)(2,1)}, bf16[1024,16]{1,0:T(8,128)(2,1)}) custom-call(s32[13]{0:T(128)} %stack.84.place, bf16[1024,1600]{1,0:T(8,128)(2,1)} %bitcast.54, bf16[8,16,6400]{2,1,0:T(8,128)(2,1)} %d_in.1, bf16[8,16,1600]{2,1,0:T(8,128)(2,1)} %a_out.9, ...), custom_call_target="tpu_custom_call", output_to_operand_aliasing={{0}: (16, {}), {1}: (17, {})} | custom-call | flops 12582912000 | bytes 4194304 | tf_op jit(solution)/shard_map/active_grad/pallas_call | solution.py:117
  378.3 75.9 %up.1 = (bf16[1024,6400]{1,0:T(8,128)(2,1)}, f32[1024,1664]{1,0:T(8,128)}, bf16[1024,16]{1,0:T(8,128)(2,1)}, f32[16,6400]{1,0:T(8,128)}, f32[16,6400]{1,0:T(8,128)}) custom-call(s32[13]{0:T(128)} %stack.84.place, bf16[1024,1600]{1,0:T(8,128)(2,1)} %get-tuple-element.124.second_ref, bf16[1024,16]{1,0:T(8,128)(2,1)} %get-tuple-element.125.up_low_ref, ...), custom_call_target="tpu_custom_call" | custom-call | flops 41943040000 | bytes 4194304 | tf_op jit(solution)/shard_map/up/pallas_call | solution.py:117
  456.2 24.5 %out_grad.1 = (f32[1024,1600]{1,0:T(8,128)}, bf16[1024,1664]{1,0:T(8,128)(2,1)}, f32[16,1600]{1,0:T(8,128)}, f32[16,1600]{1,0:T(8,128)}, f32[16,1600]{1,0:T(8,128)}, /*index=5*/f32[16,1600]{1,0:T(8,128)}) custom-call(s32[13]{0:T(128)} %stack.84.place, f32[1024,1664]{1,0:T(8,128)} %get-tuple-element.139.acc_ref, f32[1024,1600]{1,0:T(8,128)} %get-tuple-element.126.hidden_ref, ...), custom_call_target="tpu_custom_call" | custom-call | flops 5242880000 | bytes 4194304 | tf_op jit(solution)/shard_map/out_grad/pallas_call | solution.py:117
  487.4 106.7 %attend_backward.1 = (bf16[3,1024,1664]{2,1,0:T(8,128)(2,1)}, bf16[2,1024,1664]{2,1,0:T(8,128)(2,1)}) custom-call(s32[4]{0:T(128)} %pad_add_fusion.meta, bf16[1024,1664]{1,0:T(8,128)(2,1)} %queries.1.q_ref, bf16[1024,3328]{1,0:T(8,128)(2,1)} %collective-permute-done.37.k_far.v_far, bf16[1024,3328]{1,0:T(8,128)(2,1)} %collective-permute-done.37.k_far.v_far, ...), custom_call_target="tpu_custom_call" | custom-call | flops 87241523200 | bytes 16777216 | tf_op jit(solution)/shard_map/attend_backward/pallas_call | solution.py:792
  599.2 7.9 %collective-permute-done.53.far_ref = bf16[2,1024,1664]{2,1,0:T(8,128)(2,1)} collective-permute-done((bf16[2,1024,1664]{2,1,0:T(8,128)(2,1)}, bf16[2,1024,1664]{2,1,0:T(8,128)(2,1)}, u32[]{:S(2)}, u32[]{:S(2)}) %collective-permute-start.53) | collective-permute-done | bytes 6815776 | tf_op jit(solution)/shard_map/ppermute | solution.py:845
  607.2 39.1 %tokens_grad.1 = (f32[1600,1024]{1,0:T(8,128)}, f32[16,4992]{1,0:T(8,128)}, f32[16,1600]{1,0:T(8,128)}) custom-call(s32[13]{0:T(128)} %stack.84.place, bf16[1024,1600]{1,0:T(8,128)(2,1)} %bitcast.61, bf16[1024,1600]{1,0:T(8,128)(2,1)} %get-tuple-element.103.first_ref, bf16[1024,16]{1,0:T(8,128)(2,1)} %get-tuple-element.104.low_ref, ...), custom_call_target="tpu_custom_call" | custom-call | flops 16357785600 | bytes 4194304 | tf_op jit(solution)/shard_map/tokens_grad/pallas_call | solution.py:117
  652.2 11.0 %combine.2 = (f32[8,16,6400]{2,1,0:T(8,128)}, f32[8,16,6400]{2,1,0:T(8,128)}, f32[8,16,1600]{2,1,0:T(8,128)}, f32[8,16,1600]{2,1,0:T(8,128)}, f32[8,16,1600]{2,1,0:T(8,128)}, /*index=5*/f32[8,16,1600]{2,1,0:T(8,128)}) custom-call(s32[17]{0:T(128)} %pad_add_fusion.1.numbers, bf16[16,16,9856]{2,1,0:T(8,128)(2,1)} %bitcast.58, ...), custom_call_target="tpu_custom_call" | custom-call | flops 1073741824 | bytes 4194304 | tf_op jit(solution)/shard_map/combine/pallas_call | solution.py:612
  663.2 32.8 %down.1 = bf16[1600,1024]{1,0:T(8,128)(2,1)} custom-call(s32[13]{0:T(128)} %stack.84.place, bf16[1024,6400]{1,0:T(8,128)(2,1)} %get-tuple-element.165.active_ref, f32[1024,1600]{1,0:T(8,128)} %get-tuple-element.126.hidden_ref, bf16[1024,16]{1,0:T(8,128)(2,1)} %get-tuple-element.141.down_low_ref, f32[1,1600]{1,0:T(1,128)} %reshape.143.bias, ...), custom_call_target="tpu_custom_call" | custom-call | flops 20971520000 | bytes 4194304 | tf_op jit(solution)/shard_map/down/pallas_call | solution.py:117
  696.1 30.8 %all-gather.11.cloned.1.call-done = bf16[256,3456]{1,0:T(8,128)(2,1)} async-done(((bf16[16,3456]{1,0:T(8,128)(2,1)}), bf16[256,3456]{1,0:T(8,128)(2,1)}) %all-gather.11.cloned.1.call-update) | async-done | bytes 1769488 | tf_op jit(solution)/shard_map/all_gather | solution.py:940
  (291 shorter events, 146.2 us)
Async XLA Ops:
  7.3 261.3 %all-gather.7.cloned.1.call-start = ((), (), s32[]{:S(2)}) async-start(), calls=%async_computation | async-start | bytes 4096000 | tf_op jit(solution)/shard_map/all_gather | solution.py:1038
  39.8 49.7 %collective-permute-start.9 = (bf16[48,4992]{1,0:T(8,128)(2,1)}, bf16[48,4992]{1,0:T(8,128)(2,1)}, u32[]{:S(2)}, u32[]{:S(2)}) collective-permute-start(bf16[48,4992]{1,0:T(8,128)(2,1)} %slice.165.more_4_), channel_id=1, source_target_pairs={{0,4},{4,0},{1,5},{5,1},{2,6},{6,2},{3,7},{7,3},{8,12},{12,8},{9,1... | collective-permute-start | bytes 1437704 | tf_op jit(solution)/shard_map/ppermute | solution.py:911
  47.1 35.9 %collective-permute-start.8 = (bf16[48,4992]{1,0:T(8,128)(2,1)}, bf16[48,4992]{1,0:T(8,128)(2,1)}, u32[]{:S(2)}, u32[]{:S(2)}) collective-permute-start(bf16[48,4992]{1,0:T(8,128)(2,1)} %collective-permute-done.6.more_5_), channel_id=1, source_target_pairs={{0,16},{4,12},{8,24},{12,4},{16,0},{20,28},{24,8},{28,20},{1,17},{... | collective-permute-start | bytes 1437704 | tf_op jit(solution)/shard_map/ppermute | solution.py:906
  47.4 43.4 %collective-permute-start.10 = (bf16[48,4992]{1,0:T(8,128)(2,1)}, bf16[48,4992]{1,0:T(8,128)(2,1)}, u32[]{:S(2)}, u32[]{:S(2)}) collective-permute-start(bf16[48,4992]{1,0:T(8,128)(2,1)} %collective-permute-done.6.more_5_), channel_id=1, source_target_pairs={{0,4},{4,0},{1,5},{5,1},{2,6},{6,2},{3,7},{7,3},{8,12},{12,8},{9,1... | collective-permute-start | bytes 1437704 | tf_op jit(solution)/shard_map/ppermute | solution.py:911
  123.3 30.6 %collective-permute-start.27 = (bf16[3,48,1600]{2,1,0:T(8,128)(2,1)S(1)}, bf16[3,48,1600]{2,1,0:T(8,128)(2,1)}, u32[]{:S(2)}, u32[]{:S(2)}) collective-permute-start(bf16[3,48,1600]{2,1,0:T(8,128)(2,1)S(1)} %pad_maximum_fusion.3.more_4_), channel_id=1, source_target_pairs={{0,8},{4,20},{8,0},{12,28},{16,24},{20,4},{24,16},{28,12},{1,9},{5... | collective-permute-start | bytes 1382408 | tf_op jit(solution)/shard_map/ppermute | solution.py:901
  124.6 29.4 %collective-permute-start.28 = (bf16[3,48,1600]{2,1,0:T(8,128)(2,1)S(1)}, bf16[3,48,1600]{2,1,0:T(8,128)(2,1)}, u32[]{:S(2)}, u32[]{:S(2)}) collective-permute-start(bf16[3,48,1600]{2,1,0:T(8,128)(2,1)S(1)} %pad_maximum_fusion.3.more_4_), channel_id=1, source_target_pairs={{0,16},{4,12},{8,24},{12,4},{16,0},{20,28},{24,8},{28,20},{1,17},{... | collective-permute-start | bytes 1382408 | tf_op jit(solution)/shard_map/ppermute | solution.py:901
  125.6 28.4 %collective-permute-start.29 = (bf16[4,52,1600]{2,0,1:T(4,128)(2,1)S(1)}, bf16[4,52,1600]{2,0,1:T(4,128)(2,1)S(1)}, u32[]{:S(2)}, u32[]{:S(2)}) collective-permute-start(bf16[4,52,1600]{2,0,1:T(4,128)(2,1)S(1)} %copy.44), channel_id=1, source_target_pairs={{0,1},{1,2},{2,3},{3,0},{4,5},{5,6},{6,7},{7,4},{8,9},{9,10},{10,1... | collective-permute-start | bytes 1996808 | tf_op jit(solution)/shard_map/ppermute | solution.py:1034
  154.0 44.8 %collective-permute-start.37 = (bf16[1024,3328]{1,0:T(8,128)(2,1)}, bf16[1024,3328]{1,0:T(8,128)(2,1)}, u32[]{:S(2)}, u32[]{:S(2)}) collective-permute-start(bf16[1024,3328]{1,0:T(8,128)(2,1)} %get-tuple-element.109.k_near.v_near), channel_id=1, source_target_pairs={{0,4},{1,5},{2,6},{3,7},{8,12},{9,13},{10,14},{11,15},{16,20},{17,... | collective-permute-start | bytes 20447240 | tf_op jit(solution)/shard_map/ppermute | solution.py:845
  160.5 434.9 %all-gather.9.cloned.1.call-start = ((), (), s32[]{:S(2)}) async-start(), calls=%async_computation.1 | async-start | bytes 5361664 | tf_op jit(solution)/shard_map/all_gather | solution.py:940
  161.3 61.4 %collective-permute-start.33 = (bf16[3,48,1600]{2,1,0:T(8,128)(2,1)S(1)}, bf16[3,48,1600]{2,1,0:T(8,128)(2,1)S(1)}, u32[]{:S(2)}, u32[]{:S(2)}) collective-permute-start(bf16[3,48,1600]{2,1,0:T(8,128)(2,1)S(1)} %pad_maximum_fusion.3.more_4_), channel_id=1, source_target_pairs={{0,4},{4,0},{1,5},{5,1},{2,6},{6,2},{3,7},{7,3},{8,12},{12,8},{9,1... | collective-permute-start | bytes 1382408 | tf_op jit(solution)/shard_map/ppermute | solution.py:911
  161.3 30.4 %collective-permute-start.31 = (bf16[4,52,1600]{2,0,1:T(4,128)(2,1)S(1)}, bf16[4,52,1600]{2,0,1:T(4,128)(2,1)}, u32[]{:S(2)}, u32[]{:S(2)}) collective-permute-start(bf16[4,52,1600]{2,0,1:T(4,128)(2,1)S(1)} %collective-permute-done.29), channel_id=1, source_target_pairs={{0,1},{1,2},{2,3},{3,0},{4,5},{5,6},{6,7},{7,4},{8,9},{9,10},{10,1... | collective-permute-start | bytes 1996808 | tf_op jit(solution)/shard_map/ppermute | solution.py:1040
  163.5 59.2 %collective-permute-start.34 = (bf16[3,48,1600]{2,1,0:T(8,128)(2,1)}, bf16[3,48,1600]{2,1,0:T(8,128)(2,1)}, u32[]{:S(2)}, u32[]{:S(2)}) collective-permute-start(bf16[3,48,1600]{2,1,0:T(8,128)(2,1)} %collective-permute-done.27.more_5_), channel_id=1, source_target_pairs={{0,4},{4,0},{1,5},{5,1},{2,6},{6,2},{3,7},{7,3},{8,12},{12,8},{9,1... | collective-permute-start | bytes 1382408 | tf_op jit(solution)/shard_map/ppermute | solution.py:911
  178.4 44.4 %collective-permute-start.35 = (bf16[3,48,1600]{2,1,0:T(8,128)(2,1)}, bf16[3,48,1600]{2,1,0:T(8,128)(2,1)}, u32[]{:S(2)}, u32[]{:S(2)}) collective-permute-start(bf16[3,48,1600]{2,1,0:T(8,128)(2,1)} %collective-permute-done.28.more_6_), channel_id=1, source_target_pairs={{0,4},{4,0},{1,5},{5,1},{2,6},{6,2},{3,7},{7,3},{8,12},{12,8},{9,1... | collective-permute-start | bytes 1382408 | tf_op jit(solution)/shard_map/ppermute | solution.py:911
  192.9 35.1 %collective-permute-start.32 = (bf16[4,52,1600]{2,0,1:T(4,128)(2,1)}, bf16[4,52,1600]{2,0,1:T(4,128)(2,1)}, u32[]{:S(2)}, u32[]{:S(2)}) collective-permute-start(bf16[4,52,1600]{2,0,1:T(4,128)(2,1)} %collective-permute-done.31), channel_id=1, source_target_pairs={{0,1},{1,2},{2,3},{3,0},{4,5},{5,6},{6,7},{7,4},{8,9},{9,10},{10,1... | collective-permute-start | bytes 1996808 | tf_op jit(solution)/shard_map/ppermute | solution.py:1047
  230.4 45.8 %collective-permute-start.38 = (bf16[3,208,1600]{2,1,0:T(8,128)(2,1)}, bf16[3,208,1600]{2,1,0:T(8,128)(2,1)}, u32[]{:S(2)}, u32[]{:S(2)}) collective-permute-start(bf16[3,208,1600]{2,1,0:T(8,128)(2,1)} %constant_dynamic-update-slice_fusion.more_4_), channel_id=1, source_target_pairs={{0,8},{4,20},{8,0},{12,28},{16,24},{20,4},{24,16},{28,12},{1,9},{5... | collective-permute-start | bytes 5990408 | tf_op jit(solution)/shard_map/ppermute | solution.py:901
  231.9 44.2 %collective-permute-start.39 = (bf16[3,208,1600]{2,1,0:T(8,128)(2,1)}, bf16[3,208,1600]{2,1,0:T(8,128)(2,1)}, u32[]{:S(2)}, u32[]{:S(2)}) collective-permute-start(bf16[3,208,1600]{2,1,0:T(8,128)(2,1)} %constant_dynamic-update-slice_fusion.more_4_), channel_id=1, source_target_pairs={{0,16},{4,12},{8,24},{12,4},{16,0},{20,28},{24,8},{28,20},{1,17},{... | collective-permute-start | bytes 5990408 | tf_op jit(solution)/shard_map/ppermute | solution.py:901
  279.7 29.3 %collective-permute-start.44 = (bf16[3,208,1600]{2,1,0:T(8,128)(2,1)}, bf16[3,208,1600]{2,1,0:T(8,128)(2,1)}, u32[]{:S(2)}, u32[]{:S(2)}) collective-permute-start(bf16[3,208,1600]{2,1,0:T(8,128)(2,1)} %collective-permute-done.38.more_5_), channel_id=1, source_target_pairs={{0,4},{4,0},{1,5},{5,1},{2,6},{6,2},{3,7},{7,3},{8,12},{12,8},{9,1... | collective-permute-start | bytes 5990408 | tf_op jit(solution)/shard_map/ppermute | solution.py:911
  280.2 28.8 %collective-permute-start.45 = (bf16[3,208,1600]{2,1,0:T(8,128)(2,1)}, bf16[3,208,1600]{2,1,0:T(8,128)(2,1)}, u32[]{:S(2)}, u32[]{:S(2)}) collective-permute-start(bf16[3,208,1600]{2,1,0:T(8,128)(2,1)} %collective-permute-done.39.more_6_), channel_id=1, source_target_pairs={{0,4},{4,0},{1,5},{5,1},{2,6},{6,2},{3,7},{7,3},{8,12},{12,8},{9,1... | collective-permute-start | bytes 5990408 | tf_op jit(solution)/shard_map/ppermute | solution.py:911
  303.7 42.6 %collective-permute-start.40 = (bf16[3,48,6400]{2,1,0:T(8,128)(2,1)}, bf16[3,48,6400]{2,1,0:T(8,128)(2,1)}, u32[]{:S(2)}, u32[]{:S(2)}) collective-permute-start(bf16[3,48,6400]{2,1,0:T(8,128)(2,1)} %pad_maximum_fusion.more_2_), channel_id=1, source_target_pairs={{0,8},{4,20},{8,0},{12,28},{16,24},{20,4},{24,16},{28,12},{1,9},{5... | collective-permute-start | bytes 5529608 | tf_op jit(solution)/shard_map/ppermute | solution.py:901
  305.2 41.4 %collective-permute-start.41 = (bf16[3,48,6400]{2,1,0:T(8,128)(2,1)}, bf16[3,48,6400]{2,1,0:T(8,128)(2,1)}, u32[]{:S(2)}, u32[]{:S(2)}) collective-permute-start(bf16[3,48,6400]{2,1,0:T(8,128)(2,1)} %pad_maximum_fusion.more_2_), channel_id=1, source_target_pairs={{0,16},{4,12},{8,24},{12,4},{16,0},{20,28},{24,8},{28,20},{1,17},{... | collective-permute-start | bytes 5529608 | tf_op jit(solution)/shard_map/ppermute | solution.py:901
  346.6 27.5 %collective-permute-start.47 = (bf16[3,48,6400]{2,1,0:T(8,128)(2,1)}, bf16[3,48,6400]{2,1,0:T(8,128)(2,1)S(1)}, u32[]{:S(2)}, u32[]{:S(2)}) collective-permute-start(bf16[3,48,6400]{2,1,0:T(8,128)(2,1)} %collective-permute-done.40.more_3_), channel_id=1, source_target_pairs={{0,16},{4,12},{8,24},{12,4},{16,0},{20,28},{24,8},{28,20},{1,17},{... | collective-permute-start | bytes 5529608 | tf_op jit(solution)/shard_map/ppermute | solution.py:906
  348.4 27.0 %collective-permute-start.48 = (bf16[3,48,6400]{2,1,0:T(8,128)(2,1)}, bf16[3,48,6400]{2,1,0:T(8,128)(2,1)}, u32[]{:S(2)}, u32[]{:S(2)}) collective-permute-start(bf16[3,48,6400]{2,1,0:T(8,128)(2,1)} %pad_maximum_fusion.more_2_), channel_id=1, source_target_pairs={{0,4},{4,0},{1,5},{5,1},{2,6},{6,2},{3,7},{7,3},{8,12},{12,8},{9,1... | collective-permute-start | bytes 5529608 | tf_op jit(solution)/shard_map/ppermute | solution.py:911
  487.3 239.6 %all-gather.11.cloned.1.call-start = ((), (), s32[]{:S(2)}) async-start(), calls=%async_computation.2 | async-start | bytes 1880064 | tf_op jit(solution)/shard_map/all_gather | solution.py:940
  595.3 56.8 %collective-permute-start.55 = (bf16[16,16,9856]{2,1,0:T(8,128)(2,1)}, bf16[16,16,9856]{2,1,0:T(8,128)(2,1)}, u32[]{:S(2)}, u32[]{:S(2)}) collective-permute-start(bf16[16,16,9856]{2,1,0:T(8,128)(2,1)} %bitcast.56), channel_id=1, source_target_pairs={{0,4},{4,0},{1,5},{5,1},{2,6},{6,2},{3,7},{7,3},{8,12},{12,8},{9,1... | collective-permute-start | bytes 15138824 | tf_op jit(solution)/shard_map/ppermute | solution.py:952
  (80 other events, 1207.4 us)
Sparse Core Ops, SparseCore 0:
  160.6 88.7 all-gather.6
  487.4 101.5 all-gather.8
  649.8 77.0 all-gather.10

commit v6 on v4

--- a/solution.py
+++ b/solution.py
@@ -510,8 +510,28 @@
     )
 
 
-def tokens_grad_kernel(place, x_ref, first_ref, low_ref, g_hidden_ref, gain, a_in, a_out, near_ref, far_ref, *more):
-    pieces, (out_ref, g_qkv_out, g_qkv_in, w, acc, x, first, g_hidden, sems, late) = more[:-10], more[-10:]
+def qkv_out_kernel(place, low_ref, near_ref, far_ref, out_ref):
+    scale = jnp.where(pl.program_id(0) > 0, 1.0, 0.0)
+    g = (near_ref[...].astype(jnp.float32) + scale * far_ref[...].astype(jnp.float32)).astype(jnp.bfloat16)
+    out_ref[...] = product_outer(low_ref[...], g)
+
+
+def qkv_out_call(place, low, near, far):
+    rows = low.shape[0]
+    near_block = pl.BlockSpec((None, rows, PADDED), lambda c, *_: (c, 0, 0))
+    far_block = pl.BlockSpec((None, rows, PADDED), lambda c, *_: (jnp.maximum(c - 1, 0), 0, 0))
+    return call(
+        qkv_out_kernel, "qkv_out", (3,), place, [low, near, far], [],
+        [whole_of(low), near_block, far_block],
+        out_of((RANK, 3 * PADDED), jnp.float32),
+        column_block(RANK, PADDED),
+        [],
+        3 * rows * PADDED * RANK,
+    )
+
+
+def tokens_grad_kernel(place, x_ref, first_ref, g_hidden_ref, gain, a_in, a_out, near_ref, far_ref, *more):
+    pieces, (out_ref, g_qkv_in, w, acc, x, first, g_hidden, sems, late) = more[:-9], more[-9:]
     rows, features = x_ref.shape
     step, steps = pl.program_id(0), pl.num_programs(0)
     pairs = ((x_ref, x), (first_ref, first), (g_hidden_ref, g_hidden))
@@ -532,12 +552,9 @@
     slot = next_columns(pieces, place, w, sems, features)
     w[slot, pl.ds(features, RANK), :] = a_out[...]
     scale = jnp.where(step > 0, 1.0, 0.0)
-    qkv_out_sum = jnp.zeros(g_qkv_out.shape, jnp.float32)
     for block in blocks_of(rows):
         g = (near_ref[block, :].astype(jnp.float32) + scale * far_ref[block, :].astype(jnp.float32)).astype(jnp.bfloat16)
         acc[block, :] += product_transposed(g, w[slot])
-        qkv_out_sum += product_outer(low_ref[block, :], g)
-    g_qkv_out[...] = qkv_out_sum
 
     @pl.when(step == steps - 1)
     def _():
@@ -553,17 +570,17 @@
         g_qkv_in[...] = qkv_in_sum
 
 
-def tokens_grad_call(place, x, first, low, g_hidden, gain, a_in, a_out, near, far, pieces):
+def tokens_grad_call(place, x, first, g_hidden, gain, a_in, a_out, near, far, pieces):
     rows, features = x.shape
     steps = 3
     near_block = pl.BlockSpec((None, rows, PADDED), lambda c, *_: (c, 0, 0))
     far_block = pl.BlockSpec((None, rows, PADDED), lambda c, *_: (jnp.maximum(c - 1, 0), 0, 0))
     return call(
-        tokens_grad_kernel, "tokens_grad", (steps,), place, [x, first, low, g_hidden, gain, a_in, a_out, near, far], pieces,
-        [HBM, HBM, whole_of(low), HBM, whole_of(gain), picked(features),
+        tokens_grad_kernel, "tokens_grad", (steps,), place, [x, first, g_hidden, gain, a_in, a_out, near, far], pieces,
+        [HBM, HBM, HBM, whole_of(gain), picked(features),
          column_block(RANK, PADDED), near_block, far_block],
-        [out_of((features, rows), jnp.float32), out_of((RANK, steps * PADDED), jnp.float32), out_of((RANK, features), jnp.float32)],
-        [pl.BlockSpec((features, rows), lambda *_: (0, 0)), column_block(RANK, PADDED),
+        [out_of((features, rows), jnp.float32), out_of((RANK, features), jnp.float32)],
+        [pl.BlockSpec((features, rows), lambda *_: (0, 0)),
          pl.BlockSpec((RANK, features), lambda *_: (0, 0))],
         [pltpu.VMEM((2, PADDED, PADDED), jnp.bfloat16), pltpu.VMEM((rows, PADDED), jnp.float32),
          pltpu.VMEM((rows, features), jnp.bfloat16), pltpu.VMEM((rows, features), jnp.bfloat16), pltpu.VMEM((rows, features), jnp.float32),
@@ -923,6 +940,7 @@
     flat = jnp.concatenate(
         [jnp.pad(term, ((0, 0), (0, -term.shape[1] % 128))) for term in terms], axis=1
     )
+    flat = jnp.pad(flat, ((0, 0), (0, -flat.shape[1] % 256)))
     paired = sizes["ctx"] == 2
     if paired:
         half = flat.shape[1] // 2
@@ -1094,20 +1112,25 @@
         moved += shifted(far_grads[:, first_row : first_row + row_count], ctx, -offset)
     halves = both_halves(sizes, everyone)
     numbers = sequence_numbers(sizes, everyone)
-    grad_input, grad_qkv_out, grad_qkv_in = tokens_grad_call(
-        place, values, first_in, qkv_low, grad_hidden, gain_one, qkv_adapt_in, adapter_qkv_out,
-        after(near_grads, everyone), moved, pieces_qkv,
-    )
-    last_sent = send_adapters(sizes, [grad_qkv_out, grad_qkv_in], chosen)
-    last_everyone = share_adapters(last_sent)
-    numbers, active = after_all([numbers, active], last_sent)
+    grad_qkv_out = qkv_out_call(place, qkv_low, near_grads, moved)
+    out_sent = send_adapters(sizes, [grad_qkv_out], chosen)
+    out_everyone = share_adapters(out_sent)
+    grad_input, grad_qkv_in = tokens_grad_call(
+        place, values, first_in, grad_hidden, gain_one, qkv_adapt_in, adapter_qkv_out,
+        after(near_grads, everyone, out_sent), moved, pieces_qkv,
+    )
+    in_sent = send_adapters(sizes, [grad_qkv_in], chosen)
+    in_everyone = share_adapters(in_sent)
+    numbers, active = after_all([numbers, active], in_sent)
     totals = combine_call(numbers, halves, widths)
     total_up_out, total_down_in, total_up_in, total_out_out, total_out_in, total_down_out = totals
     output = down_call(
         place, after(active, *totals), hidden, down_low, bias_down, down_adapt_out, pieces_down
     )
-    last_halves = both_halves(sizes, after(last_everyone, output))
-    total_qkv_out, total_qkv_in = combine_call(numbers, last_halves, [(feature_count,) * 3, (feature_count,)])
+    out_halves = both_halves(sizes, after(out_everyone, output))
+    in_halves = both_halves(sizes, after(in_everyone, output))
+    total_qkv_out, = combine_call(numbers, out_halves, [(feature_count,) * 3])
+    total_qkv_in, = combine_call(numbers, in_halves, [(feature_count,)])
     return (
         output.T[None],
         grad_input.T[None],

time: 736 us -> 779 us (1.058)
  blocking collectives: 0 us -> 54.6 us
  waiting for transfers between devices: 159 us -> 134 us
  Pallas kernels: 452 us -> 463 us
    all_gather x0 -> x1, blocking collectives: none -> 54.6 us  [share_adapters(): return lax.all_gather(sent, ('dp', 'wt'), axis=0)]
    all_gather x2, waiting for transfers between devices: 23.2 us -> 0.04 us  [share_adapters(): return lax.all_gather(sent, ('dp', 'wt'), axis=0)]
    pallas_call x9 -> x10, Pallas kernels: 270 us -> 279 us  [call(): pl.pallas_call(kernel, grid_spec=pltpu.PrefetchScalarGridSpec(num_scalar_...]
    pallas_call x2 -> x3, Pallas kernels: 16.5 us -> 18.9 us  [combine_call(): pl.pallas_call(partial(combine_kernel, widths), grid_spec=pltpu.PrefetchS...]
    unnamed x88 -> x92, local copies, waits for them, and re-layouts: 21.3 us -> 21.9 us
  transfers between devices with their start and end apart: 60 -> 62, of which waited for: 21 -> 20; matrix products, arithmetic and copies ran while one was open for 6% -> 6% of each run, Pallas kernels for 47% -> 46%
where the time goes in v6:
time: 779 us; the launch traced here: 773 us
  Pallas kernels  463 us (59%)
  waiting for transfers between devices  134 us (17%)
  blocking collectives  54.6 us (7%)
  local copies, waits for them, and re-layouts  52.5 us (7%)
  starting transfers between devices  39.3 us (5%)
  between operations  15.7 us (2%)
  other arithmetic  13.9 us (2%)
    pallas_call x10, Pallas kernels, call(): pl.pallas_call(kernel, grid_spec=pltpu.PrefetchScalarGridSpec(num_scalar_...  279 us
    pallas_call x1, Pallas kernels, attend_backward(): pl.pallas_call(partial(attend_backward_kernel, tiles), grid_spec=pltpu.Pr...  107 us
    pallas_call x2, Pallas kernels, attend_forward(): pl.pallas_call(partial(attend_forward_kernel, tiles), grid_spec=pltpu.Pre...  59 us
    ppermute x6, waiting for transfers between devices, plane_start(): lax.ppermute(mine, ('dp', 'ctx'), first)  54.6 us
    all_gather x1, blocking collectives, share_adapters(): return lax.all_gather(sent, ('dp', 'wt'), axis=0)  54.6 us
    ppermute x3, waiting for transfers between devices, ring(): moved = lax.ppermute(moved, 'wt', ring_pairs(sizes['wt']))  29.2 us
    unnamed x92, local copies, waits for them, and re-layouts  21.9 us
    pallas_call x3, Pallas kernels, combine_call(): pl.pallas_call(partial(combine_kernel, widths), grid_spec=pltpu.PrefetchS...  18.9 us
  transfers between devices with their start and end apart: 62, of which 20 were waited for; matrix products, arithmetic and copies ran while one was open for 6% of the time, Pallas kernels for 46%

profile of v6, /device:TPU:0, one launch (start us, length us, event | category | flops | bytes accessed | tf_op | source)
XLA Modules:
  0.0 772.8 jit_solution(108615780718633233)
XLA Ops:
  42.2 8.9 %collective-permute-done.6.more_5_ = bf16[48,4992]{1,0:T(8,128)(2,1)} collective-permute-done((bf16[48,4992]{1,0:T(8,128)(2,1)}, bf16[48,4992]{1,0:T(8,128)(2,1)}, u32[]{:S(2)}, u32[]{:S(2)}) %collective-permute-start.6) | collective-permute-done | bytes 479264 | tf_op jit(solution)/shard_map/ppermute | solution.py:918
  51.9 8.4 %collective-permute-done.1.more_2_ = bf16[66,4992]{1,0:T(8,128)(2,1)S(1)} collective-permute-done((bf16[66,4992]{1,0:T(8,128)(2,1)S(1)}, bf16[66,4992]{1,0:T(8,128)(2,1)S(1)}, u32[]{:S(2)}, u32[]{:S(2)}) %collective-permute-start.1) | collective-permute-done | bytes 658976 | tf_op jit(solution)/shard_map/ppermute | solution.py:903
  61.3 18.7 %collective-permute-done.2.more_3_ = bf16[66,4992]{1,0:T(8,128)(2,1)S(1)} collective-permute-done((bf16[66,4992]{1,0:T(8,128)(2,1)S(1)}, bf16[66,4992]{1,0:T(8,128)(2,1)S(1)}, u32[]{:S(2)}, u32[]{:S(2)}) %collective-permute-start.2) | collective-permute-done | bytes 658976 | tf_op jit(solution)/shard_map/ppermute | solution.py:903
  85.1 8.3 %collective-permute-done.13.more_13_ = bf16[48,4992]{1,0:T(8,128)(2,1)S(1)} collective-permute-done((bf16[48,4992]{1,0:T(8,128)(2,1)S(1)}, bf16[48,4992]{1,0:T(8,128)(2,1)S(1)}, u32[]{:S(2)}, u32[]{:S(2)}) %collective-permute-start.13) | collective-permute-done | bytes 479264 | tf_op jit(solution)/shard_map/ppermute | solution.py:918
  102.7 6.2 collective-permute-done.4.more_2_
  129.3 23.2 %keys.1 = (bf16[1024,1600]{1,0:T(8,128)(2,1)}, bf16[1024,16]{1,0:T(8,128)(2,1)}, bf16[1024,3328]{1,0:T(8,128)(2,1)}) custom-call(s32[13]{0:T(128)} %stack.84.place, bf16[1024,1600]{1,0:T(8,128)(2,1)} %bitcast.60, f32[1,1600]{1,0:T(1,128)} %reshape.132.gain, f32[1,1600]{1,0:T(1,128)} %reshape.133.shift, f32[1,4992]{1,0:T(1,128)} %fusion.28.bias, ...), custom_call_target="tpu_custom_call" | custom-call | flops 10905190400 | bytes 4194304 | tf_op jit(solution)/shard_map/keys/pallas_call | solution.py:117
  163.7 13.0 %queries.1.q_ref = bf16[1024,1664]{1,0:T(8,128)(2,1)} custom-call(s32[13]{0:T(128)} %stack.84.place, bf16[1024,1600]{1,0:T(8,128)(2,1)} %get-tuple-element.97.first_ref, bf16[1024,16]{1,0:T(8,128)(2,1)} %get-tuple-element.98.low_ref, f32[1,4992]{1,0:T(1,128)} %fusion.28.bias, bf16[16,4992]{1,0:T(8,128)(2,1)} %fusion.24.a_out, ...), custom_call_target="tpu_custom_call" | custom-call | flops 5452595200 | bytes 4194304 | tf_op jit(solution)/shard_map/queries/pallas_call | solution.py:117
  176.8 7.5 collective-permute-done.31
  186.0 31.3 %attend_forward.2 = (bf16[1024,1664]{1,0:T(8,128)(2,1)}, f32[13,2048,128]{2,1,0:T(8,128)}) custom-call(s32[4]{0:T(128)} %pad_add_fusion.meta, bf16[1024,1664]{1,0:T(8,128)(2,1)} %queries.1.q_ref, bf16[1024,3328]{1,0:T(8,128)(2,1)} %collective-permute-done.37.k_far.v_far, bf16[1024,3328]{1,0:T(8,128)(2,1)} %collective-permute-done.37.k_far.v_far, ...), custom_call_target="tpu_custom_call" | custom-call | flops 18790481920 | bytes 16777216 | tf_op jit(solution)/shard_map/attend_forward/pallas_call | solution.py:736
  224.3 27.6 %attend_forward.3 = (bf16[1024,1664]{1,0:T(8,128)(2,1)}, f32[13,2048,128]{2,1,0:T(8,128)}) custom-call(s32[4]{0:T(128)} %pad_add_fusion.meta, bf16[1024,1664]{1,0:T(8,128)(2,1)} %queries.1.q_ref, bf16[1024,3328]{1,0:T(8,128)(2,1)} %collective-permute-done.37.k_far.v_far, ...), custom_call_target="tpu_custom_call", output_to_operand_aliasing={{0}: (6, {}), {1}: (7, {})} | custom-call | flops 16106127360 | bytes 16777216 | tf_op jit(solution)/shard_map/attend_forward/pallas_call | solution.py:736
  251.9 16.6 %collective-permute-done.38.more_5_ = bf16[3,208,1600]{2,1,0:T(8,128)(2,1)} collective-permute-done((bf16[3,208,1600]{2,1,0:T(8,128)(2,1)}, bf16[3,208,1600]{2,1,0:T(8,128)(2,1)}, u32[]{:S(2)}, u32[]{:S(2)}) %collective-permute-start.38) | collective-permute-done | bytes 1996832 | tf_op jit(solution)/shard_map/ppermute | solution.py:918
  271.3 18.3 %out.1 = (f32[1024,1600]{1,0:T(8,128)}, bf16[1024,1600]{1,0:T(8,128)(2,1)}, bf16[1024,16]{1,0:T(8,128)(2,1)}, bf16[1024,16]{1,0:T(8,128)(2,1)}) custom-call(s32[13]{0:T(128)} %stack.84.place, bf16[1024,1600]{1,0:T(8,128)(2,1)} %bitcast.61, bf16[1024,1664]{1,0:T(8,128)(2,1)} %get-tuple-element.113.mixed_ref.o_ref, f32[1,1600]{1,0:T(1,128)} %reshape.137.gain, ...), custom_call_target="tpu_custom_call" | custom-call | flops 5242880000 | bytes 4194304 | tf_op jit(solution)/shard_map/out/pallas_call | solution.py:117
  301.7 18.0 %active_grad.2 = (bf16[1024,6400]{1,0:T(8,128)(2,1)}, bf16[1024,16]{1,0:T(8,128)(2,1)}) custom-call(s32[13]{0:T(128)} %stack.84.place, bf16[1024,1600]{1,0:T(8,128)(2,1)} %bitcast.54, bf16[8,16,6400]{2,1,0:T(8,128)(2,1)} %d_in.1, bf16[8,16,1600]{2,1,0:T(8,128)(2,1)} %a_out.9, bf16[1600,1600]{1,0:T(8,128)(2,1)} %more_0_.11, ...), custom_call_target="tpu_custom_call" | custom-call | flops 8388608000 | bytes 4194304 | tf_op jit(solution)/shard_map/active_grad/pallas_call | solution.py:117
  319.6 20.9 %collective-permute-done.40.more_3_ = bf16[3,48,6400]{2,1,0:T(8,128)(2,1)} collective-permute-done((bf16[3,48,6400]{2,1,0:T(8,128)(2,1)}, bf16[3,48,6400]{2,1,0:T(8,128)(2,1)}, u32[]{:S(2)}, u32[]{:S(2)}) %collective-permute-start.40) | collective-permute-done | bytes 1843232 | tf_op jit(solution)/shard_map/ppermute | solution.py:918
  342.0 25.1 %active_grad.3 = (bf16[1024,6400]{1,0:T(8,128)(2,1)}, bf16[1024,16]{1,0:T(8,128)(2,1)}) custom-call(s32[13]{0:T(128)} %stack.84.place, bf16[1024,1600]{1,0:T(8,128)(2,1)} %bitcast.55, bf16[8,16,6400]{2,1,0:T(8,128)(2,1)} %d_in.1, bf16[8,16,1600]{2,1,0:T(8,128)(2,1)} %a_out.9, ...), custom_call_target="tpu_custom_call", output_to_operand_aliasing={{0}: (16, {}), {1}: (17, {})} | custom-call | flops 12582912000 | bytes 4194304 | tf_op jit(solution)/shard_map/active_grad/pallas_call | solution.py:117
  371.1 75.9 %up.1 = (bf16[1024,6400]{1,0:T(8,128)(2,1)}, f32[1024,1664]{1,0:T(8,128)}, bf16[1024,16]{1,0:T(8,128)(2,1)}, f32[16,6400]{1,0:T(8,128)}, f32[16,6400]{1,0:T(8,128)}) custom-call(s32[13]{0:T(128)} %stack.84.place, bf16[1024,1600]{1,0:T(8,128)(2,1)} %get-tuple-element.118.second_ref, bf16[1024,16]{1,0:T(8,128)(2,1)} %get-tuple-element.119.up_low_ref, ...), custom_call_target="tpu_custom_call" | custom-call | flops 41943040000 | bytes 4194304 | tf_op jit(solution)/shard_map/up/pallas_call | solution.py:117
  449.1 24.5 %out_grad.1 = (f32[1024,1600]{1,0:T(8,128)}, bf16[1024,1664]{1,0:T(8,128)(2,1)}, f32[16,1600]{1,0:T(8,128)}, f32[16,1600]{1,0:T(8,128)}, f32[16,1600]{1,0:T(8,128)}, /*index=5*/f32[16,1600]{1,0:T(8,128)}) custom-call(s32[13]{0:T(128)} %stack.84.place, f32[1024,1664]{1,0:T(8,128)} %get-tuple-element.133.acc_ref, f32[1024,1600]{1,0:T(8,128)} %get-tuple-element.120.hidden_ref, ...), custom_call_target="tpu_custom_call" | custom-call | flops 5242880000 | bytes 4194304 | tf_op jit(solution)/shard_map/out_grad/pallas_call | solution.py:117
  480.3 106.7 %attend_backward.1 = (bf16[3,1024,1664]{2,1,0:T(8,128)(2,1)}, bf16[2,1024,1664]{2,1,0:T(8,128)(2,1)}) custom-call(s32[4]{0:T(128)} %pad_add_fusion.meta, bf16[1024,1664]{1,0:T(8,128)(2,1)} %queries.1.q_ref, bf16[1024,3328]{1,0:T(8,128)(2,1)} %collective-permute-done.37.k_far.v_far, bf16[1024,3328]{1,0:T(8,128)(2,1)} %collective-permute-done.37.k_far.v_far, ...), custom_call_target="tpu_custom_call" | custom-call | flops 87241523200 | bytes 16777216 | tf_op jit(solution)/shard_map/attend_backward/pallas_call | solution.py:809
  592.2 7.9 %collective-permute-done.53.far_ref = bf16[2,1024,1664]{2,1,0:T(8,128)(2,1)} collective-permute-done((bf16[2,1024,1664]{2,1,0:T(8,128)(2,1)}, bf16[2,1024,1664]{2,1,0:T(8,128)(2,1)}, u32[]{:S(2)}, u32[]{:S(2)}) %collective-permute-start.53) | collective-permute-done | bytes 6815776 | tf_op jit(solution)/shard_map/ppermute | solution.py:862
  600.1 9.6 %qkv_out.1 = f32[16,4992]{1,0:T(8,128)} custom-call(s32[13]{0:T(128)} %stack.84.place, bf16[1024,16]{1,0:T(8,128)(2,1)} %get-tuple-element.98.low_ref, bf16[3,1024,1664]{2,1,0:T(8,128)(2,1)} %get-tuple-element.148.near_ref, bf16[2,1024,1664]{2,1,0:T(8,128)(2,1)} %collective-permute-done.53.far_ref), custom_call_target="tpu_custom_call" | custom-call | flops 163577856 | bytes 4194304 | tf_op jit(solution)/shard_map/qkv_out/pallas_call | solution.py:117
  613.7 38.1 %tokens_grad.1 = (f32[1600,1024]{1,0:T(8,128)}, f32[16,1600]{1,0:T(8,128)}) custom-call(s32[13]{0:T(128)} %stack.84.place, bf16[1024,1600]{1,0:T(8,128)(2,1)} %bitcast.62, bf16[1024,1600]{1,0:T(8,128)(2,1)} %get-tuple-element.97.first_ref, f32[1024,1600]{1,0:T(8,128)} %get-tuple-element.146.g_hidden_ref, f32[1,1600]{1,0:T(1,128)} %reshape.132.gain, ...), custom_call_target="tpu_custom_call" | custom-call | flops 16357785600 | bytes 4194304 | tf_op jit(solution)/shard_map/tokens_grad/pallas_call | solution.py:117
  655.5 11.0 %combine.3 = (f32[8,16,6400]{2,1,0:T(8,128)}, f32[8,16,6400]{2,1,0:T(8,128)}, f32[8,16,1600]{2,1,0:T(8,128)}, f32[8,16,1600]{2,1,0:T(8,128)}, f32[8,16,1600]{2,1,0:T(8,128)}, /*index=5*/f32[8,16,1600]{2,1,0:T(8,128)}) custom-call(s32[17]{0:T(128)} %pad_add_fusion.1.numbers, bf16[16,16,9856]{2,1,0:T(8,128)(2,1)} %bitcast.59, ...), custom_call_target="tpu_custom_call" | custom-call | flops 1073741824 | bytes 4194304 | tf_op jit(solution)/shard_map/combine/pallas_call | solution.py:629
  666.6 32.7 %down.1 = bf16[1600,1024]{1,0:T(8,128)(2,1)} custom-call(s32[13]{0:T(128)} %stack.84.place, bf16[1024,6400]{1,0:T(8,128)(2,1)} %get-tuple-element.158.active_ref, f32[1024,1600]{1,0:T(8,128)} %get-tuple-element.120.hidden_ref, bf16[1024,16]{1,0:T(8,128)(2,1)} %get-tuple-element.135.down_low_ref, f32[1,1600]{1,0:T(1,128)} %reshape.143.bias, ...), custom_call_target="tpu_custom_call" | custom-call | flops 20971520000 | bytes 4194304 | tf_op jit(solution)/shard_map/down/pallas_call | solution.py:117
  699.8 54.6 %all-gather.2 = bf16[256,1024]{1,0:T(8,128)(2,1)S(1)} all-gather(bf16[16,1024]{1,0:T(8,128)(2,1)S(1)} %concatenate.63), channel_id=4, replica_groups=mesh['dp'=4,'ctx'=2,'wt'=4] {'dp','wt'}, dimensions={0}, use_global_device_ids=true | all-gather | bytes 557056 | tf_op jit(solution)/shard_map/all_gather | solution.py:958
  (300 shorter events, 143.9 us)
Async XLA Ops:
  7.3 244.6 %all-gather.8.cloned.1.call-start = ((), (), s32[]{:S(2)}) async-start(), calls=%async_computation | async-start | bytes 4096000 | tf_op jit(solution)/shard_map/all_gather | solution.py:1054
  40.0 41.9 %collective-permute-start.9 = (bf16[48,4992]{1,0:T(8,128)(2,1)}, bf16[48,4992]{1,0:T(8,128)(2,1)}, u32[]{:S(2)}, u32[]{:S(2)}) collective-permute-start(bf16[48,4992]{1,0:T(8,128)(2,1)} %slice.165.more_4_), channel_id=1, source_target_pairs={{0,4},{4,0},{1,5},{5,1},{2,6},{6,2},{3,7},{7,3},{8,12},{12,8},{9,1... | collective-permute-start | bytes 1437704 | tf_op jit(solution)/shard_map/ppermute | solution.py:928
  51.1 31.4 %collective-permute-start.8 = (bf16[48,4992]{1,0:T(8,128)(2,1)}, bf16[48,4992]{1,0:T(8,128)(2,1)}, u32[]{:S(2)}, u32[]{:S(2)}) collective-permute-start(bf16[48,4992]{1,0:T(8,128)(2,1)} %collective-permute-done.6.more_5_), channel_id=1, source_target_pairs={{0,16},{4,12},{8,24},{12,4},{16,0},{20,28},{24,8},{28,20},{1,17},{... | collective-permute-start | bytes 1437704 | tf_op jit(solution)/shard_map/ppermute | solution.py:923
  51.4 31.1 %collective-permute-start.10 = (bf16[48,4992]{1,0:T(8,128)(2,1)}, bf16[48,4992]{1,0:T(8,128)(2,1)}, u32[]{:S(2)}, u32[]{:S(2)}) collective-permute-start(bf16[48,4992]{1,0:T(8,128)(2,1)} %collective-permute-done.6.more_5_), channel_id=1, source_target_pairs={{0,4},{4,0},{1,5},{5,1},{2,6},{6,2},{3,7},{7,3},{8,12},{12,8},{9,1... | collective-permute-start | bytes 1437704 | tf_op jit(solution)/shard_map/ppermute | solution.py:928
  51.4 31.7 %collective-permute-start.11 = (bf16[48,4992]{1,0:T(8,128)(2,1)}, bf16[48,4992]{1,0:T(8,128)(2,1)}, u32[]{:S(2)}, u32[]{:S(2)}) collective-permute-start(bf16[48,4992]{1,0:T(8,128)(2,1)} %collective-permute-done.7.more_6_), channel_id=1, source_target_pairs={{0,4},{4,0},{1,5},{5,1},{2,6},{6,2},{3,7},{7,3},{8,12},{12,8},{9,1... | collective-permute-start | bytes 1437704 | tf_op jit(solution)/shard_map/ppermute | solution.py:928
  123.0 29.5 %collective-permute-start.27 = (bf16[3,48,1600]{2,1,0:T(8,128)(2,1)S(1)}, bf16[3,48,1600]{2,1,0:T(8,128)(2,1)}, u32[]{:S(2)}, u32[]{:S(2)}) collective-permute-start(bf16[3,48,1600]{2,1,0:T(8,128)(2,1)S(1)} %pad_maximum_fusion.3.more_4_), channel_id=1, source_target_pairs={{0,8},{4,20},{8,0},{12,28},{16,24},{20,4},{24,16},{28,12},{1,9},{5... | collective-permute-start | bytes 1382408 | tf_op jit(solution)/shard_map/ppermute | solution.py:918
  123.8 28.8 %collective-permute-start.28 = (bf16[3,48,1600]{2,1,0:T(8,128)(2,1)S(1)}, bf16[3,48,1600]{2,1,0:T(8,128)(2,1)}, u32[]{:S(2)}, u32[]{:S(2)}) collective-permute-start(bf16[3,48,1600]{2,1,0:T(8,128)(2,1)S(1)} %pad_maximum_fusion.3.more_4_), channel_id=1, source_target_pairs={{0,16},{4,12},{8,24},{12,4},{16,0},{20,28},{24,8},{28,20},{1,17},{... | collective-permute-start | bytes 1382408 | tf_op jit(solution)/shard_map/ppermute | solution.py:918
  152.6 33.4 %collective-permute-start.37 = (bf16[1024,3328]{1,0:T(8,128)(2,1)}, bf16[1024,3328]{1,0:T(8,128)(2,1)}, u32[]{:S(2)}, u32[]{:S(2)}) collective-permute-start(bf16[1024,3328]{1,0:T(8,128)(2,1)} %get-tuple-element.103.k_near.v_near), channel_id=1, source_target_pairs={{0,4},{1,5},{2,6},{3,7},{8,12},{9,13},{10,14},{11,15},{16,20},{17,... | collective-permute-start | bytes 20447240 | tf_op jit(solution)/shard_map/ppermute | solution.py:862
  159.8 57.6 %collective-permute-start.33 = (bf16[3,48,1600]{2,1,0:T(8,128)(2,1)S(1)}, bf16[3,48,1600]{2,1,0:T(8,128)(2,1)}, u32[]{:S(2)}, u32[]{:S(2)}) collective-permute-start(bf16[3,48,1600]{2,1,0:T(8,128)(2,1)S(1)} %pad_maximum_fusion.3.more_4_), channel_id=1, source_target_pairs={{0,4},{4,0},{1,5},{5,1},{2,6},{6,2},{3,7},{7,3},{8,12},{12,8},{9,1... | collective-permute-start | bytes 1382408 | tf_op jit(solution)/shard_map/ppermute | solution.py:928
  161.2 56.2 %collective-permute-start.34 = (bf16[3,48,1600]{2,1,0:T(8,128)(2,1)}, bf16[3,48,1600]{2,1,0:T(8,128)(2,1)}, u32[]{:S(2)}, u32[]{:S(2)}) collective-permute-start(bf16[3,48,1600]{2,1,0:T(8,128)(2,1)} %collective-permute-done.27.more_5_), channel_id=1, source_target_pairs={{0,4},{4,0},{1,5},{5,1},{2,6},{6,2},{3,7},{7,3},{8,12},{12,8},{9,1... | collective-permute-start | bytes 1382408 | tf_op jit(solution)/shard_map/ppermute | solution.py:928
  162.5 425.8 %all-gather.10.cloned.1.call-start = ((), (), s32[]{:S(2)}) async-start(), calls=%async_computation.1 | async-start | bytes 5361664 | tf_op jit(solution)/shard_map/all_gather | solution.py:958
  176.7 40.6 %collective-permute-start.35 = (bf16[3,48,1600]{2,1,0:T(8,128)(2,1)}, bf16[3,48,1600]{2,1,0:T(8,128)(2,1)}, u32[]{:S(2)}, u32[]{:S(2)}) collective-permute-start(bf16[3,48,1600]{2,1,0:T(8,128)(2,1)} %collective-permute-done.28.more_6_), channel_id=1, source_target_pairs={{0,4},{4,0},{1,5},{5,1},{2,6},{6,2},{3,7},{7,3},{8,12},{12,8},{9,1... | collective-permute-start | bytes 1382408 | tf_op jit(solution)/shard_map/ppermute | solution.py:928
  184.3 34.9 %collective-permute-start.32 = (bf16[4,52,1600]{2,0,1:T(4,128)(2,1)S(1)}, bf16[4,52,1600]{2,0,1:T(4,128)(2,1)}, u32[]{:S(2)}, u32[]{:S(2)}) collective-permute-start(bf16[4,52,1600]{2,0,1:T(4,128)(2,1)S(1)} %collective-permute-done.31), channel_id=1, source_target_pairs={{0,1},{1,2},{2,3},{3,0},{4,5},{5,6},{6,7},{7,4},{8,9},{9,10},{10,1... | collective-permute-start | bytes 1996808 | tf_op jit(solution)/shard_map/ppermute | solution.py:1063
  186.0 31.4 %collective-permute-start.36 = (bf16[3,48,1600]{2,1,0:T(8,128)(2,1)}, bf16[3,48,1600]{2,1,0:T(8,128)(2,1)S(1)}, u32[]{:S(2)}, u32[]{:S(2)}) collective-permute-start(bf16[3,48,1600]{2,1,0:T(8,128)(2,1)} %collective-permute-done.30.more_7_), channel_id=1, source_target_pairs={{0,4},{4,0},{1,5},{5,1},{2,6},{6,2},{3,7},{7,3},{8,12},{12,8},{9,1... | collective-permute-start | bytes 1382408 | tf_op jit(solution)/shard_map/ppermute | solution.py:928
  221.7 46.8 %collective-permute-start.38 = (bf16[3,208,1600]{2,1,0:T(8,128)(2,1)}, bf16[3,208,1600]{2,1,0:T(8,128)(2,1)}, u32[]{:S(2)}, u32[]{:S(2)}) collective-permute-start(bf16[3,208,1600]{2,1,0:T(8,128)(2,1)} %constant_dynamic-update-slice_fusion.more_4_), channel_id=1, source_target_pairs={{0,8},{4,20},{8,0},{12,28},{16,24},{20,4},{24,16},{28,12},{1,9},{5... | collective-permute-start | bytes 5990408 | tf_op jit(solution)/shard_map/ppermute | solution.py:918
  223.2 45.3 %collective-permute-start.39 = (bf16[3,208,1600]{2,1,0:T(8,128)(2,1)}, bf16[3,208,1600]{2,1,0:T(8,128)(2,1)}, u32[]{:S(2)}, u32[]{:S(2)}) collective-permute-start(bf16[3,208,1600]{2,1,0:T(8,128)(2,1)} %constant_dynamic-update-slice_fusion.more_4_), channel_id=1, source_target_pairs={{0,16},{4,12},{8,24},{12,4},{16,0},{20,28},{24,8},{28,20},{1,17},{... | collective-permute-start | bytes 5990408 | tf_op jit(solution)/shard_map/ppermute | solution.py:918
  270.8 28.3 %collective-permute-start.43 = (bf16[3,208,1600]{2,1,0:T(8,128)(2,1)}, bf16[3,208,1600]{2,1,0:T(8,128)(2,1)}, u32[]{:S(2)}, u32[]{:S(2)}) collective-permute-start(bf16[3,208,1600]{2,1,0:T(8,128)(2,1)} %constant_dynamic-update-slice_fusion.more_4_), channel_id=1, source_target_pairs={{0,4},{4,0},{1,5},{5,1},{2,6},{6,2},{3,7},{7,3},{8,12},{12,8},{9,1... | collective-permute-start | bytes 5990408 | tf_op jit(solution)/shard_map/ppermute | solution.py:928
  270.8 30.9 %collective-permute-start.44 = (bf16[3,208,1600]{2,1,0:T(8,128)(2,1)}, bf16[3,208,1600]{2,1,0:T(8,128)(2,1)}, u32[]{:S(2)}, u32[]{:S(2)}) collective-permute-start(bf16[3,208,1600]{2,1,0:T(8,128)(2,1)} %collective-permute-done.38.more_5_), channel_id=1, source_target_pairs={{0,4},{4,0},{1,5},{5,1},{2,6},{6,2},{3,7},{7,3},{8,12},{12,8},{9,1... | collective-permute-start | bytes 5990408 | tf_op jit(solution)/shard_map/ppermute | solution.py:928
  271.3 30.4 %collective-permute-start.45 = (bf16[3,208,1600]{2,1,0:T(8,128)(2,1)}, bf16[3,208,1600]{2,1,0:T(8,128)(2,1)}, u32[]{:S(2)}, u32[]{:S(2)}) collective-permute-start(bf16[3,208,1600]{2,1,0:T(8,128)(2,1)} %collective-permute-done.39.more_6_), channel_id=1, source_target_pairs={{0,4},{4,0},{1,5},{5,1},{2,6},{6,2},{3,7},{7,3},{8,12},{12,8},{9,1... | collective-permute-start | bytes 5990408 | tf_op jit(solution)/shard_map/ppermute | solution.py:928
  297.6 42.9 %collective-permute-start.40 = (bf16[3,48,6400]{2,1,0:T(8,128)(2,1)}, bf16[3,48,6400]{2,1,0:T(8,128)(2,1)}, u32[]{:S(2)}, u32[]{:S(2)}) collective-permute-start(bf16[3,48,6400]{2,1,0:T(8,128)(2,1)} %pad_maximum_fusion.more_2_), channel_id=1, source_target_pairs={{0,8},{4,20},{8,0},{12,28},{16,24},{20,4},{24,16},{28,12},{1,9},{5... | collective-permute-start | bytes 5529608 | tf_op jit(solution)/shard_map/ppermute | solution.py:918
  299.1 41.4 %collective-permute-start.41 = (bf16[3,48,6400]{2,1,0:T(8,128)(2,1)}, bf16[3,48,6400]{2,1,0:T(8,128)(2,1)}, u32[]{:S(2)}, u32[]{:S(2)}) collective-permute-start(bf16[3,48,6400]{2,1,0:T(8,128)(2,1)} %pad_maximum_fusion.more_2_), channel_id=1, source_target_pairs={{0,16},{4,12},{8,24},{12,4},{16,0},{20,28},{24,8},{28,20},{1,17},{... | collective-permute-start | bytes 5529608 | tf_op jit(solution)/shard_map/ppermute | solution.py:918
  480.3 219.1 %all-gather.12.cloned.1.call-start = ((), (), s32[]{:S(2)}) async-start(), calls=%async_computation.2 | async-start | bytes 1462272 | tf_op jit(solution)/shard_map/all_gather | solution.py:958
  588.3 67.2 %collective-permute-start.56 = (bf16[16,16,9856]{2,1,0:T(8,128)(2,1)}, bf16[16,16,9856]{2,1,0:T(8,128)(2,1)}, u32[]{:S(2)}, u32[]{:S(2)}) collective-permute-start(bf16[16,16,9856]{2,1,0:T(8,128)(2,1)} %bitcast.57), channel_id=1, source_target_pairs={{0,4},{4,0},{1,5},{5,1},{2,6},{6,2},{3,7},{7,3},{8,12},{12,8},{9,1... | collective-permute-start | bytes 15138824 | tf_op jit(solution)/shard_map/ppermute | solution.py:970
  699.3 61.0 %collective-permute-start.58 = (bf16[16,16,2688]{2,1,0:T(8,128)(2,1)}, bf16[16,16,2688]{2,1,0:T(8,128)(2,1)S(1)}, u32[]{:S(2)}, u32[]{:S(2)}) collective-permute-start(bf16[16,16,2688]{2,1,0:T(8,128)(2,1)} %bitcast.63), channel_id=1, source_target_pairs={{0,4},{4,0},{1,5},{5,1},{2,6},{6,2},{3,7},{7,3},{8,12},{12,8},{9,1... | collective-permute-start | bytes 4128776 | tf_op jit(solution)/shard_map/ppermute | solution.py:970
  (82 other events, 1164.2 us)
Sparse Core Ops, SparseCore 0:
  162.6 85.0 all-gather.7
  480.4 93.9 all-gather.9
  613.9 67.7 all-gather.11
